TPU v7x, 512 devices: a whole 4x4x16 slice. The times are simulated.
512 devices in a mesh: dp: 8 (over y, core), expert: 64 (over x, z).
Axes of the slice: x: 4, y: 4, z: 16, core: 2. Of those that a mesh axis runs over, the one named last changes fastest.
Arguments:
- input_rows: bfloat16 [32768, 7168], P(('dp', 'expert')), may hold values from -6 to 6
- row_scales: float32 [32768, 56], P(('dp', 'expert')), may hold values from 0.25 to 4
- output_grad: bfloat16 [32768, 7168], P(('dp', 'expert')), may hold values from -6 to 6
- expert_ids: int32 [32768, 8], P(('dp', 'expert')), may hold values from 0 to 255, all different within a row; in each aligned block of 64 rows (0 to 63, 64 to 127, ...) at most 4 rows name the same one
- combine_weights: float32 [32768, 8], P(('dp', 'expert')), may hold values from 0.1 to 1
- gate_proj: bfloat16 [64, 7168, 256], P('expert', 'dp'), may hold values from -0.0625 to 0.0625
- up_proj: bfloat16 [64, 7168, 256], P('expert', 'dp'), may hold values from -0.0625 to 0.0625
- down_proj: bfloat16 [64, 256, 7168], P('expert', None, 'dp'), may hold values from -0.1875 to 0.1875
Outputs:
- input_grad: bfloat16 [32768, 7168], P(('dp', 'expert'))
Inputs may be any that keep to these rules, and one draw needn't show every extreme that they name: `expert_ids`: each row names 8 different experts. Among the rows of one device no number appears more than 4 times, and some number appears exactly 4 times in the rows of some device.
All inputs are finite; a program needn't handle non-finite values.
Results may differ from a plain program's by a relative error of at most 0.034.
Values may be sent and summed in bfloat16 or wider, within the bound.
No kernel may reach another device: no remote copies, remote signals or barrier semaphores. Data moves between devices by JAX's collectives and lax.ppermute only.
A program may use at most 128 MiB of HBM per device.

v0:
```python
import jax
import jax.numpy as jnp
from jax import lax
from jax.sharding import PartitionSpec as P

BLOCK = 128
CAP = 4


def swiglu_grads(gate_val, up_val, hidden_grad):
    sigmoid_gate = jax.nn.sigmoid(gate_val)
    gate_grad = (
        hidden_grad * up_val * sigmoid_gate * (1.0 + gate_val * (1.0 - sigmoid_gate))
    ).astype(jnp.bfloat16)
    up_grad = (hidden_grad * gate_val * sigmoid_gate).astype(jnp.bfloat16)
    return (gate_grad, up_grad)


def times_transpose(left, right):
    return lax.dot_general(
        left, right, (((1,), (1,)), ((), ())), preferred_element_type=jnp.float32
    )


def per_device(
    input_rows, row_scales, output_grad, expert_ids, combine_weights, gate_proj, up_proj, down_proj
):
    tokens_here = input_rows.shape[0]
    width = input_rows.shape[1]
    n_data = lax.axis_size("dp")
    n_owner = lax.axis_size("expert")
    window = n_owner // 4
    columns = width // n_data
    expert_range = jnp.arange(window, dtype=jnp.int32)
    hits = (expert_ids[:, :, None] == expert_range).astype(jnp.float32)
    member = jnp.sum(hits, axis=1)
    pick_weight = jnp.sum(combine_weights[:, :, None] * hits, axis=1)
    before = jnp.cumsum(member, axis=0) - member
    slot_range = jnp.arange(CAP, dtype=jnp.float32)
    select = member[:, :, None] * (before[:, :, None] == slot_range).astype(jnp.float32)
    select_rows = select.reshape(tokens_here, window * CAP)
    select_bf = select_rows.T.astype(jnp.bfloat16)
    rows_buf = jnp.dot(select_bf, input_rows, preferred_element_type=jnp.float32).astype(
        jnp.bfloat16
    )
    grad_buf = jnp.dot(select_bf, output_grad, preferred_element_type=jnp.float32).astype(
        jnp.bfloat16
    )
    scale_buf = jnp.dot(select_rows.T, row_scales, precision=lax.Precision.HIGHEST)
    rows_buf = rows_buf.reshape(window, CAP, width)
    grad_buf = grad_buf.reshape(window, CAP, width)
    scale_buf = scale_buf.reshape(window, CAP, width // BLOCK)
    rows_got, scales_got, grads_got = (
        lax.all_to_all(
            lax.all_to_all(
                jnp.repeat(rows_buf, 4, axis=0), "dp", split_axis=2, concat_axis=1, tiled=True
            ),
            "expert",
            split_axis=0,
            concat_axis=0,
            tiled=True,
        ),
        lax.all_to_all(
            lax.all_to_all(
                jnp.repeat(scale_buf, 4, axis=0).astype(jnp.bfloat16),
                "dp",
                split_axis=2,
                concat_axis=1,
                tiled=True,
            ),
            "expert",
            split_axis=0,
            concat_axis=0,
            tiled=True,
        ).astype(jnp.float32),
        lax.all_to_all(
            lax.all_to_all(
                jnp.repeat(grad_buf, 4, axis=0), "dp", split_axis=2, concat_axis=1, tiled=True
            ),
            "expert",
            split_axis=0,
            concat_axis=0,
            tiled=True,
        ),
    )
    rows_all = n_owner * n_data * CAP
    rows_mat = rows_got.reshape(rows_all, columns)
    scales = scales_got.reshape(rows_all, columns // BLOCK)
    scale_wide = jnp.repeat(scales, BLOCK, axis=1)
    x_rows = (rows_mat.astype(jnp.float32) * scale_wide).astype(jnp.bfloat16)
    grads = grads_got.reshape(rows_all, columns)
    gate_piece = gate_proj[0]
    up_piece = up_proj[0]
    down_piece = down_proj[0]
    gate_part = jnp.dot(x_rows, gate_piece, preferred_element_type=jnp.float32)
    up_part = jnp.dot(x_rows, up_piece, preferred_element_type=jnp.float32)
    hidden_part = times_transpose(grads, down_piece)
    gate_val, up_val, hidden_grad = (
        lax.psum(gate_part.astype(jnp.bfloat16), "dp").astype(jnp.float32),
        lax.psum(up_part.astype(jnp.bfloat16), "dp").astype(jnp.float32),
        lax.psum(hidden_part.astype(jnp.bfloat16), "dp").astype(jnp.float32),
    )
    gate_grad, up_grad = swiglu_grads(gate_val, up_val, hidden_grad)
    part = times_transpose(gate_grad, gate_piece) + times_transpose(up_grad, up_piece)
    part = part.astype(jnp.bfloat16).reshape(n_owner, n_data * CAP, columns)
    returned = lax.all_to_all(
        lax.all_to_all(part, "dp", split_axis=1, concat_axis=2, tiled=True),
        "expert",
        split_axis=0,
        concat_axis=0,
        tiled=True,
    )
    quarters = returned.reshape(window, 4, CAP, width).astype(jnp.float32)
    joined_sum = jnp.sum(quarters, axis=1).reshape(window * CAP, width)
    weighting = (select * pick_weight[:, :, None]).reshape(tokens_here, window * CAP)
    gradient = jnp.dot(weighting, joined_sum, precision=lax.Precision.HIGHEST)
    return gradient.astype(jnp.bfloat16)


def solution(mesh):
    return jax.shard_map(
        per_device,
        mesh=mesh,
        in_specs=(
            P(("dp", "expert"), None),
            P(("dp", "expert"), None),
            P(("dp", "expert"), None),
            P(("dp", "expert"), None),
            P(("dp", "expert"), None),
            P("expert", "dp", None),
            P("expert", "dp", None),
            P("expert", None, "dp"),
        ),
        out_specs=P(("dp", "expert"), None),
        check_vma=False,
    )
```

profile of v0, /device:TPU:32, one launch (start us, length us, event | category | flops | bytes accessed | tf_op | source)
XLA Modules:
  0.0 872.4 jit_solution(1402857202966348713)
XLA Ops:
  9.0 9.7 %all_to_all.92 = bf16[8,2,896]{2,1,0:T(2,128)(2,1)S(1)} all-to-all(bf16[8,2,896]{2,1,0:T(2,128)(2,1)S(1)} %reshape.94), channel_id=1, replica_groups=mesh['dp'=8,'expert'=64] {'dp'}, dimensions={0} | all-to-all | bytes 57344 | tf_op jit(solution)/shard_map/all_to_all | solution.py:64
  19.6 18.2 %all-to-all-start.5 = ((bf16[64,32,7]{1,2,0:T(8,128)(2,1)}), bf16[64,32,7]{1,2,0:T(8,128)(2,1)S(1)}, u32[]{:S(2)}, u32[]{:S(2)}) async-start(bf16[64,32,7]{1,2,0:T(8,128)(2,1)} %copy.182), calls=%async_computation.5 | async-start | bytes 262144 | tf_op jit(solution)/shard_map/all_to_all | solution.py:63
  41.6 12.2 %copy.175 = bf16[64,4,7168]{0,1,2:T(4,128)(2,1)} copy(bf16[64,4,7168]{2,1,0:T(4,128)(2,1)} %bitcast.97) | data formatting | bytes 7340032 | tf_op jit(solution)/shard_map/reshape | solution.py:56
  53.8 9.7 %reshape.92 = bf16[8,2,114688]{2,1,0:T(2,128)(2,1)} reshape(bf16[7168,4,64]{2,1,0:T(4,128)(2,1)} %bitcast.89) | data formatting | bytes 7340032
  63.5 4.6 all-to-all-start.2
  71.9 12.2 %copy.171 = bf16[64,4,7168]{0,1,2:T(4,128)(2,1)} copy(bf16[64,4,7168]{2,1,0:T(4,128)(2,1)} %bitcast.98) | data formatting | bytes 7340032 | tf_op jit(solution)/shard_map/reshape | solution.py:78
  84.1 9.6 %reshape.90 = bf16[8,2,114688]{2,1,0:T(2,128)(2,1)} reshape(bf16[7168,4,64]{2,1,0:T(4,128)(2,1)} %bitcast.90) | data formatting | bytes 7340032
  93.8 18.5 %all-to-all-done.2 = bf16[8,2,114688]{2,1,0:T(2,128)(2,1)} async-done(((bf16[8,2,114688]{2,1,0:T(2,128)(2,1)}), bf16[8,2,114688]{2,1,0:T(2,128)(2,1)}, u32[]{:S(2)}, u32[]{:S(2)}) %all-to-all-start.2) | async-done | bytes 3670048 | tf_op jit(solution)/shard_map/all_to_all | solution.py:55
  112.2 4.5 all-to-all-start
  116.7 9.5 %reshape.93 = bf16[7168,4,64]{2,1,0:T(4,128)(2,1)} reshape(bf16[8,2,114688]{2,1,0:T(2,128)(2,1)} %all-to-all-done.2) | data formatting | bytes 7340032
  126.2 11.0 %copy.195 = bf16[64,4,8,896]{3,0,1,2:T(8,128)(2,1)} copy(bf16[64,4,8,896]{0,1,3,2:T(4,128)(2,1)} %bitcast.91) | data formatting | bytes 7340032 | tf_op jit(solution)/shard_map/all_to_all | solution.py:55
  137.2 5.9 copy.178
  143.1 17.6 %all-to-all-done = bf16[8,2,114688]{2,1,0:T(2,128)(2,1)} async-done(((bf16[8,2,114688]{2,1,0:T(2,128)(2,1)}), bf16[8,2,114688]{2,1,0:T(2,128)(2,1)}, u32[]{:S(2)}, u32[]{:S(2)}) %all-to-all-start) | async-done | bytes 3670048 | tf_op jit(solution)/shard_map/all_to_all | solution.py:77
  160.8 26.3 %all-to-all-start.3 = ((bf16[64,32,896]{2,1,0:T(8,128)(2,1)}), bf16[64,32,896]{2,1,0:T(8,128)(2,1)}, u32[]{:S(2)}, u32[]{:S(2)}) async-start(bf16[64,32,896]{2,1,0:T(8,128)(2,1)} %copy.178), calls=%async_computation.3 | async-start | bytes 7340032 | tf_op jit(solution)/shard_map/all_to_all | solution.py:54
  187.1 9.5 %reshape.91 = bf16[7168,4,64]{2,1,0:T(4,128)(2,1)} reshape(bf16[8,2,114688]{2,1,0:T(2,128)(2,1)} %all-to-all-done) | data formatting | bytes 7340032
  196.6 11.0 %copy.193 = bf16[64,4,8,896]{3,0,1,2:T(8,128)(2,1)} copy(bf16[64,4,8,896]{0,1,3,2:T(4,128)(2,1)} %bitcast.92) | data formatting | bytes 7340032 | tf_op jit(solution)/shard_map/all_to_all | solution.py:77
  207.6 5.9 copy.174
  213.6 138.5 %all-to-all-done.3 = bf16[64,32,896]{2,1,0:T(8,128)(2,1)} async-done(((bf16[64,32,896]{2,1,0:T(8,128)(2,1)}), bf16[64,32,896]{2,1,0:T(8,128)(2,1)}, u32[]{:S(2)}, u32[]{:S(2)}) %all-to-all-start.3) | async-done | bytes 3670048 | tf_op jit(solution)/shard_map/all_to_all | solution.py:54
  352.1 7.7 all-to-all-start.1
  360.9 8.7 reshape.84
  369.6 8.2 multiply_convert_fusion
  377.8 6.6 copy.186
  384.4 4.5 convolution_convert_fusion.2
  391.2 133.6 %all-to-all-done.1 = bf16[64,32,896]{2,1,0:T(8,128)(2,1)} async-done(((bf16[64,32,896]{2,1,0:T(8,128)(2,1)}), bf16[64,32,896]{2,1,0:T(8,128)(2,1)}, u32[]{:S(2)}, u32[]{:S(2)}) %all-to-all-start.1) | async-done | bytes 3670048 | tf_op jit(solution)/shard_map/all_to_all | solution.py:76
  524.8 4.3 convolution_convert_fusion.4
  529.2 76.2 %all-reduce.3.cloned.1.call-done = (bf16[2048,256]{1,0:T(8,128)(2,1)}, bf16[2048,256]{1,0:T(8,128)(2,1)}, bf16[2048,256]{1,0:T(8,128)(2,1)}) async-done(((bf16[2048,256]{1,0:T(8,128)(2,1)}, bf16[2048,256]{1,0:T(8,128)(2,1)}, bf16[2048,256]{1,0:T(8,128)(2,1)}), (bf16[2048,256]{1,0:T(8,128)(2,1)}, bf16[2048,256]{1,0:T(8,128)(2,1)}, bf16[2048,256]{1,0:T(8,128)(2,1)})) %all-reduce.3.cloned.1.call-update) | async-done | bytes 3145744 | tf_op jit(solution)/shard_map/psum | solution.py:101
  612.0 47.3 %all_to_all.93 = bf16[64,32,896]{2,0,1:T(8,128)(2,1)S(1)} all-to-all(bf16[64,32,896]{2,0,1:T(8,128)(2,1)S(1)} %copy.187), channel_id=1, replica_groups=mesh['dp'=8,'expert'=64] {'dp'}, dimensions={1} | all-to-all | bytes 7340032 | tf_op jit(solution)/shard_map/all_to_all | solution.py:107
  663.2 6.6 all_to_all.82
  669.9 6.7 copy.189
  676.6 15.8 %all-to-all-start.7 = ((bf16[64,4,7168]{2,1,0:T(4,128)(2,1)}), bf16[64,4,7168]{2,1,0:T(4,128)(2,1)}, u32[]{:S(2)}, u32[]{:S(2)}) async-start(bf16[64,4,7168]{2,1,0:T(4,128)(2,1)} %copy.189), calls=%async_computation.7 | async-start | bytes 7340032 | tf_op jit(solution)/shard_map/all_to_all | solution.py:106
  692.4 165.0 %all-to-all-done.7 = bf16[64,4,7168]{2,1,0:T(4,128)(2,1)} async-done(((bf16[64,4,7168]{2,1,0:T(4,128)(2,1)}), bf16[64,4,7168]{2,1,0:T(4,128)(2,1)}, u32[]{:S(2)}, u32[]{:S(2)}) %all-to-all-start.7) | async-done | bytes 3670048 | tf_op jit(solution)/shard_map/all_to_all | solution.py:106
  857.4 4.3 convert_reduce_fusion
  (53 shorter events, 28.4 us)
Async XLA Ops:
  6.5 31.3 %copy-start = (bf16[64,7168]{1,0:T(8,128)(2,1)S(1)}, bf16[64,7168]{1,0:T(8,128)(2,1)}, u32[]{:S(2)}) copy-start(bf16[64,7168]{1,0:T(8,128)(2,1)} %param.8) | copy-start | bytes 2752516
  19.6 43.9 %all-to-all-start.5 = ((bf16[64,32,7]{1,2,0:T(8,128)(2,1)}), bf16[64,32,7]{1,2,0:T(8,128)(2,1)S(1)}, u32[]{:S(2)}, u32[]{:S(2)}) async-start(bf16[64,32,7]{1,2,0:T(8,128)(2,1)} %copy.182), calls=%async_computation.5 | async-start | bytes 262144 | tf_op jit(solution)/shard_map/all_to_all | solution.py:63
  63.5 4.7 copy-start.3
  63.5 48.7 %all-to-all-start.2 = ((bf16[8,2,114688]{2,1,0:T(2,128)(2,1)}), bf16[8,2,114688]{2,1,0:T(2,128)(2,1)}, u32[]{:S(2)}, u32[]{:S(2)}) async-start(bf16[8,2,114688]{2,1,0:T(2,128)(2,1)} %reshape.92), calls=%async_computation.2 | async-start | bytes 7340032 | tf_op jit(solution)/shard_map/all_to_all | solution.py:55
  112.2 48.6 %all-to-all-start = ((bf16[8,2,114688]{2,1,0:T(2,128)(2,1)}), bf16[8,2,114688]{2,1,0:T(2,128)(2,1)}, u32[]{:S(2)}, u32[]{:S(2)}) async-start(bf16[8,2,114688]{2,1,0:T(2,128)(2,1)} %reshape.90), calls=%async_computation | async-start | bytes 7340032 | tf_op jit(solution)/shard_map/all_to_all | solution.py:77
  160.8 191.3 %all-to-all-start.3 = ((bf16[64,32,896]{2,1,0:T(8,128)(2,1)}), bf16[64,32,896]{2,1,0:T(8,128)(2,1)}, u32[]{:S(2)}, u32[]{:S(2)}) async-start(bf16[64,32,896]{2,1,0:T(8,128)(2,1)} %copy.178), calls=%async_computation.3 | async-start | bytes 7340032 | tf_op jit(solution)/shard_map/all_to_all | solution.py:54
  352.1 172.7 %all-to-all-start.1 = ((bf16[64,32,896]{2,1,0:T(8,128)(2,1)}), bf16[64,32,896]{2,1,0:T(8,128)(2,1)}, u32[]{:S(2)}, u32[]{:S(2)}) async-start(bf16[64,32,896]{2,1,0:T(8,128)(2,1)} %copy.174), calls=%async_computation.1 | async-start | bytes 7340032 | tf_op jit(solution)/shard_map/all_to_all | solution.py:76
  359.8 245.5 %all-reduce.3.cloned.1.call-start = ((), (), s32[]{:S(2)}) async-start(), calls=%async_computation.8 | async-start | bytes 6291456 | tf_op jit(solution)/shard_map/psum | solution.py:101
  377.8 6.6 copy-start.7
  384.4 4.5 copy-start.2
  384.4 4.5 copy-start.8
  388.9 135.9 %copy-start.6 = (bf16[1,256,896]{2,1,0:T(8,128)(2,1)S(1)}, bf16[1,256,896]{2,1,0:T(8,128)(2,1)}, u32[]{:S(2)}) copy-start(bf16[1,256,896]{2,1,0:T(8,128)(2,1)} %param.15) | copy-start | bytes 1376260
  605.4 3.8 copy-start.4
  605.4 3.8 copy-start.5
  676.6 180.8 %all-to-all-start.7 = ((bf16[64,4,7168]{2,1,0:T(4,128)(2,1)}), bf16[64,4,7168]{2,1,0:T(4,128)(2,1)}, u32[]{:S(2)}, u32[]{:S(2)}) async-start(bf16[64,4,7168]{2,1,0:T(4,128)(2,1)} %copy.189), calls=%async_computation.7 | async-start | bytes 7340032 | tf_op jit(solution)/shard_map/all_to_all | solution.py:106
  692.4 172.8 %copy-start.1 = (bf16[64,7168]{1,0:T(8,128)(2,1)S(1)}, bf16[64,7168]{1,0:T(8,128)(2,1)}, u32[]{:S(2)}) copy-start(bf16[64,7168]{1,0:T(8,128)(2,1)} %param.8) | copy-start | bytes 2752516
Sparse Core Ops, SparseCore 0:
  529.3 75.9 all-reduce.2
where the time goes:
time: 884 us; the launch traced here: 872 us
  waiting for transfers between devices  549 us (62%)
  local copies, waits for them, and re-layouts  140 us (16%)
  starting transfers between devices  77.2 us (9%)
  blocking collectives  57 us (6%)
  matrix products  21.7 us (2%)
  between operations  14 us (2%)
  other arithmetic  13.5 us (2%)
    all_to_all x1, waiting for transfers between devices, per_device(): lax.all_to_all(lax.all_to_all(part, 'dp', split_axis=1, concat_axis=2, ti...  165 us
    all_to_all x1, waiting for transfers between devices, per_device(): lax.all_to_all(lax.all_to_all(jnp.repeat(rows_buf, 4, axis=0), 'dp', spli...  139 us
    all_to_all x1, waiting for transfers between devices, per_device(): lax.all_to_all(lax.all_to_all(jnp.repeat(grad_buf, 4, axis=0), 'dp', spli...  134 us
    psum x1, waiting for transfers between devices, per_device(): lax.psum(hidden_part.astype(jnp.bfloat16), 'dp').astype(jnp.float32)  76.2 us
    all_to_all x1, blocking collectives, per_device(): lax.all_to_all(part, 'dp', split_axis=1, concat_axis=2, tiled=True)  47.3 us
    unnamed x24, local copies, waits for them, and re-layouts  38.6 us
    all_to_all x1, starting transfers between devices, per_device(): lax.all_to_all(lax.all_to_all(jnp.repeat(rows_buf, 4, axis=0), 'dp', spli...  26.3 us
    all_to_all x1, waiting for transfers between devices, per_device(): lax.all_to_all(jnp.repeat(rows_buf, 4, axis=0), 'dp', split_axis=2, conca...  18.5 us
  transfers between devices with their start and end apart: 7, of which 6 were waited for; matrix products, arithmetic and copies ran while one was open for 16% of the time, Pallas kernels for 0%

commit v1 on v0

v1 whole, which is shorter than its diff:
```python
import jax
import jax.numpy as jnp
from jax import lax
from jax.sharding import Mesh, PartitionSpec as P

BLOCK = 128
CAP = 4
QUARTERS = 4
CHUNKS = 2

DP = ("y", "c")
EX = ("xh", "l")
bf16 = jnp.bfloat16
f32 = jnp.float32


def mm(left, right):
    return jnp.dot(left, right, preferred_element_type=f32)


def mm_t(left, right):
    return lax.dot_general(left, right, (((1,), (1,)), ((), ())), preferred_element_type=f32)


def one_hot_rows(source):
    count = source.shape[0]
    return (source[:, None] == jnp.arange(count, dtype=jnp.int32)[None, :]).astype(bf16)


def swiglu_grads(gate_val, up_val, hidden_grad):
    sigmoid_gate = jax.nn.sigmoid(gate_val)
    gate_grad = hidden_grad * up_val * sigmoid_gate * (1.0 + gate_val * (1.0 - sigmoid_gate))
    up_grad = hidden_grad * gate_val * sigmoid_gate
    return gate_grad.astype(bf16), up_grad.astype(bf16)


def per_device(
    input_rows, row_scales, output_grad, expert_ids, combine_weights, gate_proj, up_proj, down_proj
):
    tokens, width = input_rows.shape
    n_dp = lax.axis_size(DP)
    n_ex = lax.axis_size(EX)
    window = n_ex // QUARTERS
    cols = width // n_dp

    gate_all, up_all, down_all = (
        lax.all_gather(gate_proj[0], "l"),
        lax.all_gather(up_proj[0], "l"),
        lax.all_gather(down_proj[0], "l"),
    )

    hits = (expert_ids[:, :, None] == jnp.arange(window, dtype=jnp.int32)).astype(f32)
    member = jnp.sum(hits, axis=1)
    pick_weight = jnp.sum(combine_weights[:, :, None] * hits, axis=1)
    before = jnp.cumsum(member, axis=0) - member
    select = member[:, :, None] * (
        before[:, :, None] == jnp.arange(CAP, dtype=f32)
    ).astype(f32)
    weighting = (select * pick_weight[:, :, None]).reshape(tokens, window * CAP)
    select = select.reshape(tokens, window * CAP).T.astype(bf16)

    x = (input_rows.astype(f32) * jnp.repeat(row_scales, BLOCK, axis=1)).astype(bf16)

    def picked(array):
        return jnp.stack(
            [
                mm(select, array[:, d * cols : (d + 1) * cols]).astype(bf16)
                for d in range(n_dp)
            ]
        )

    sent = jnp.concatenate([picked(x), picked(output_grad)], axis=1)
    got = lax.all_to_all(sent, DP, split_axis=0, concat_axis=0, tiled=True)

    part_dp = n_dp // CHUNKS
    rows = n_ex * part_dp
    both = 2 * rows
    place = jnp.arange(both, dtype=jnp.int32)
    dest, kind, src = place // (2 * part_dp), place // part_dp % 2, place % part_dp
    to_send = one_hot_rows(src * (2 * n_ex) + kind * n_ex + dest)
    kind2, rest = place // rows, place % rows
    to_split = one_hot_rows(rest // part_dp * (2 * part_dp) + kind2 * part_dp + rest % part_dp)
    place3 = jnp.arange(rows, dtype=jnp.int32)
    to_slots = one_hot_rows(place3 % n_ex * part_dp + place3 // n_ex)

    def forward(chunk):
        mine = got[chunk * part_dp : (chunk + 1) * part_dp].reshape(both, cols)
        mine = mm(to_send, mine).astype(bf16).reshape(n_ex, 2 * part_dp, cols)
        there = lax.all_to_all(mine, EX, split_axis=0, concat_axis=0, tiled=True)
        return there.reshape(both, cols)

    def hidden_parts(there):
        split = mm(to_split, there).astype(bf16)
        x_rows, grads = split[:rows], split[rows:]
        parts = [mm(x_rows, gate_all[q]).astype(bf16) for q in range(QUARTERS)]
        parts += [mm(x_rows, up_all[q]).astype(bf16) for q in range(QUARTERS)]
        parts += [mm_t(grads, down_all[q]).astype(bf16) for q in range(QUARTERS)]
        return jnp.concatenate(parts, axis=1)

    def activations(parts):
        summed = lax.psum_scatter(parts, DP, scatter_dimension=0, tiled=True).astype(f32)
        hidden = summed.shape[1] // 3
        grads = swiglu_grads(
            summed[:, :hidden], summed[:, hidden : 2 * hidden], summed[:, 2 * hidden :]
        )
        return lax.all_gather(jnp.concatenate(grads, axis=1), DP, axis=0, tiled=True)

    def backward(acts):
        hq = gate_all.shape[2]
        part = jnp.zeros((rows, cols), f32)
        for q in range(QUARTERS):
            part = part + mm_t(acts[:, q * hq : (q + 1) * hq], gate_all[q])
            part = part + mm_t(acts[:, (QUARTERS + q) * hq : (QUARTERS + q + 1) * hq], up_all[q])
        part = part.astype(bf16).reshape(n_ex, part_dp, cols)
        back = lax.all_to_all(part, EX, split_axis=0, concat_axis=0, tiled=True)
        back = mm(to_slots, back.reshape(rows, cols)).astype(bf16)
        return back.reshape(part_dp, n_ex, cols)

    arrived = [forward(k) for k in range(CHUNKS)]
    acts = [activations(hidden_parts(a)) for a in arrived]
    back = jnp.concatenate([backward(a) for a in acts], axis=0)
    home = lax.all_to_all(back, DP, split_axis=0, concat_axis=0, tiled=True)
    high = weighting.astype(bf16)
    low = (weighting - high.astype(f32)).astype(bf16)
    return jnp.concatenate(
        [(mm(high, home[d]) + mm(low, home[d])).astype(bf16) for d in range(n_dp)], axis=1
    )


def solution(mesh):
    n_dp, n_ex = mesh.devices.shape
    fine = Mesh(
        mesh.devices.reshape(n_dp // 2, 2, n_ex // QUARTERS, QUARTERS), ("y", "c", "xh", "l")
    )
    tok = P(("y", "c", "xh", "l"), None)
    return jax.shard_map(
        per_device,
        mesh=fine,
        in_specs=(tok, tok, tok, tok, tok, P(EX, DP, None), P(EX, DP, None), P(EX, None, DP)),
        out_specs=tok,
        check_vma=False,
    )
```

time: 884 us -> 493 us (0.56)
  the two profiles are of different devices: /device:TPU:32 before, /device:TPU:1 now
where the time goes in v1:
time: 493 us; the launch traced here: 492 us
  waiting for transfers between devices  353 us (72%)
  starting transfers between devices  66.9 us (14%)
  matrix products  41.7 us (8%)
  between operations  14.2 us (3%)
  local copies, waits for them, and re-layouts  9.07 us (2%)
  other arithmetic  7.19 us (1%)
    reduce_scatter x2, waiting for transfers between devices, activations(): lax.psum_scatter(parts, DP, scatter_dimension=0, tiled=True).astype(f32)  69.8 us
    all_gather x1, waiting for transfers between devices, per_device(): lax.all_gather(up_proj[0], 'l')  65 us
    all_to_all x2, waiting for transfers between devices, forward(): there = lax.all_to_all(mine, EX, split_axis=0, concat_axis=0, tiled=True)  52.8 us
    all_gather x1, waiting for transfers between devices, per_device(): lax.all_gather(down_proj[0], 'l')  47 us
    all_gather x2, waiting for transfers between devices, activations(): lax.all_gather(jnp.concatenate(grads, axis=1), DP, axis=0, tiled=True)  44.9 us
    all_to_all x2, waiting for transfers between devices, backward(): back = lax.all_to_all(part, EX, split_axis=0, concat_axis=0, tiled=True)  34.6 us
    dot_general x54, matrix products, mm(): return jnp.dot(left, right, preferred_element_type=f32)  26.9 us
    all_to_all x2, starting transfers between devices, forward(): there = lax.all_to_all(mine, EX, split_axis=0, concat_axis=0, tiled=True)  25.6 us
  transfers between devices with their start and end apart: 13, of which 11 were waited for; matrix products, arithmetic and copies ran while one was open for 9% of the time, Pallas kernels for 0%

profile of v1, /device:TPU:1, one launch (start us, length us, event | category | flops | bytes accessed | tf_op | source)
XLA Modules:
  0.0 491.8 jit_solution(1164956303898697981)
XLA Ops:
  12.4 1.4 pad_maximum_fusion
  13.8 10.4 %all-to-all-start = ((bf16[8,128,896]{2,1,0:T(8,128)(2,1)}), bf16[8,128,896]{2,1,0:T(8,128)(2,1)S(1)}, u32[]{:S(2)}, u32[]{:S(2)}) async-start(bf16[8,128,896]{2,1,0:T(8,128)(2,1)} %pad_maximum_fusion), calls=%async_computation | async-start | bytes 3670016 | tf_op jit(solution)/shard_map/all_to_all | solution.py:73
  24.9 22.8 %all-to-all-done = bf16[8,128,896]{2,1,0:T(8,128)(2,1)S(1)} async-done(((bf16[8,128,896]{2,1,0:T(8,128)(2,1)}), bf16[8,128,896]{2,1,0:T(8,128)(2,1)S(1)}, u32[]{:S(2)}, u32[]{:S(2)}) %all-to-all-start) | async-done | bytes 1835040 | tf_op jit(solution)/shard_map/all_to_all | solution.py:73
  47.8 1.7 fusion.1
  49.5 13.9 %all-to-all-start.1 = ((bf16[64,8,896]{2,1,0:T(8,128)(2,1)}), bf16[64,8,896]{2,1,0:T(8,128)(2,1)S(1)}, u32[]{:S(2)}, u32[]{:S(2)}) async-start(bf16[64,8,896]{2,1,0:T(8,128)(2,1)} %fusion.1), calls=%async_computation.1 | async-start | bytes 1835008 | tf_op jit(solution)/shard_map/all_to_all | solution.py:89
  64.9 1.7 fusion.2
  66.6 52.8 %all-to-all-done.1 = bf16[64,8,896]{2,1,0:T(8,128)(2,1)S(1)} async-done(((bf16[64,8,896]{2,1,0:T(8,128)(2,1)}), bf16[64,8,896]{2,1,0:T(8,128)(2,1)S(1)}, u32[]{:S(2)}, u32[]{:S(2)}) %all-to-all-start.1) | async-done | bytes 917536 | tf_op jit(solution)/shard_map/all_to_all | solution.py:89
  119.3 11.7 %all-to-all-start.3 = ((bf16[64,8,896]{2,1,0:T(8,128)(2,1)}), bf16[64,8,896]{2,1,0:T(8,128)(2,1)}, u32[]{:S(2)}, u32[]{:S(2)}) async-start(bf16[64,8,896]{2,1,0:T(8,128)(2,1)} %fusion.2), calls=%async_computation.3 | async-start | bytes 1835008 | tf_op jit(solution)/shard_map/all_to_all | solution.py:89
  131.2 1.7 convolution_convert_fusion.2
  132.8 1.7 fusion.28
  134.5 1.6 fusion.27
  137.8 65.0 %all-gather.8.cloned.1.call-done = bf16[4,896,256]{2,1,0:T(8,128)(2,1)} async-done(((bf16[1,896,256]{2,1,0:T(8,128)(2,1)}), bf16[4,896,256]{2,1,0:T(8,128)(2,1)}) %all-gather.8.cloned.1.call-update) | async-done | bytes 1835024 | tf_op jit(solution)/shard_map/all_gather | solution.py:48
  202.8 1.7 fusion.24
  204.5 1.5 fusion.23
  207.7 47.0 %all-gather.10.cloned.1.call-done = bf16[4,256,896]{2,1,0:T(8,128)(2,1)} async-done(((bf16[1,256,896]{2,1,0:T(8,128)(2,1)}), bf16[4,256,896]{2,1,0:T(8,128)(2,1)}) %all-gather.10.cloned.1.call-update) | async-done | bytes 1835024 | tf_op jit(solution)/shard_map/all_gather | solution.py:49
  254.8 1.6 fusion.20
  256.4 1.5 fusion.19
  258.6 1.8 copy.40
  260.6 1.9 convolution_convert_fusion
  267.6 1.7 copy.42
  269.4 29.5 %reduce-scatter.7.cloned.1.call-done = bf16[32,3072]{1,0:T(8,128)(2,1)} async-done(((bf16[256,3072]{1,0:T(8,128)(2,1)}), bf16[32,3072]{1,0:T(8,128)(2,1)}) %reduce-scatter.7.cloned.1.call-update) | async-done | bytes 196624 | tf_op jit(solution)/shard_map/reduce_scatter | solution.py:101
  300.8 40.2 %reduce-scatter.9.cloned.1.call-done = bf16[32,3072]{1,0:T(8,128)(2,1)} async-done(((bf16[256,3072]{1,0:T(8,128)(2,1)}), bf16[32,3072]{1,0:T(8,128)(2,1)}) %reduce-scatter.9.cloned.1.call-update) | async-done | bytes 196624 | tf_op jit(solution)/shard_map/reduce_scatter | solution.py:101
  342.7 32.7 %all-gather.12.cloned.1.call-done = bf16[256,2048]{1,0:T(8,128)(2,1)} async-done(((bf16[32,2048]{1,0:T(8,128)(2,1)}), bf16[256,2048]{1,0:T(8,128)(2,1)}) %all-gather.12.cloned.1.call-update) | async-done | bytes 1048592 | tf_op jit(solution)/shard_map/all_gather | solution.py:106
  376.7 1.5 convolution_add_fusion.13
  381.2 15.2 %all-to-all-start.2 = ((bf16[64,4,896]{2,1,0:T(4,128)(2,1)}), bf16[64,4,896]{2,1,0:T(4,128)(2,1)S(1)}, u32[]{:S(2)}, u32[]{:S(2)}) async-start(bf16[64,4,896]{2,1,0:T(4,128)(2,1)} %reshape.586), calls=%async_computation.2 | async-start | bytes 917504 | tf_op jit(solution)/shard_map/all_to_all | solution.py:115
  396.3 12.2 %all-gather.14.cloned.1.call-done = bf16[256,2048]{1,0:T(8,128)(2,1)} async-done(((bf16[32,2048]{1,0:T(8,128)(2,1)}), bf16[256,2048]{1,0:T(8,128)(2,1)}) %all-gather.14.cloned.1.call-update) | async-done | bytes 1048592 | tf_op jit(solution)/shard_map/all_gather | solution.py:106
  409.9 1.5 convolution_add_fusion.6
  414.3 9.2 %all-to-all-done.2 = bf16[64,4,896]{2,1,0:T(4,128)(2,1)S(1)} async-done(((bf16[64,4,896]{2,1,0:T(4,128)(2,1)}), bf16[64,4,896]{2,1,0:T(4,128)(2,1)S(1)}, u32[]{:S(2)}, u32[]{:S(2)}) %all-to-all-start.2) | async-done | bytes 458784 | tf_op jit(solution)/shard_map/all_to_all | solution.py:115
  423.5 8.0 %all-to-all-start.4 = ((bf16[64,4,896]{2,1,0:T(4,128)(2,1)}), bf16[64,4,896]{2,1,0:T(4,128)(2,1)S(1)}, u32[]{:S(2)}, u32[]{:S(2)}) async-start(bf16[64,4,896]{2,1,0:T(4,128)(2,1)} %reshape.592), calls=%async_computation.4 | async-start | bytes 917504 | tf_op jit(solution)/shard_map/all_to_all | solution.py:115
  432.0 25.4 %all-to-all-done.4 = bf16[64,4,896]{2,1,0:T(4,128)(2,1)S(1)} async-done(((bf16[64,4,896]{2,1,0:T(4,128)(2,1)}), bf16[64,4,896]{2,1,0:T(4,128)(2,1)S(1)}, u32[]{:S(2)}, u32[]{:S(2)}) %all-to-all-start.4) | async-done | bytes 458784 | tf_op jit(solution)/shard_map/all_to_all | solution.py:115
  458.9 7.3 %all-to-all-start.5 = ((bf16[8,64,896]{2,1,0:T(8,128)(2,1)}), bf16[8,64,896]{2,1,0:T(8,128)(2,1)S(1)}, u32[]{:S(2)}, u32[]{:S(2)}) async-start(bf16[8,64,896]{2,1,0:T(8,128)(2,1)} %pad_maximum_fusion.1), calls=%async_computation.5 | async-start | bytes 1835008 | tf_op jit(solution)/shard_map/all_to_all | solution.py:122
  466.2 13.7 %all-to-all-done.5 = bf16[8,64,896]{2,1,0:T(8,128)(2,1)S(1)} async-done(((bf16[8,64,896]{2,1,0:T(8,128)(2,1)}), bf16[8,64,896]{2,1,0:T(8,128)(2,1)S(1)}, u32[]{:S(2)}, u32[]{:S(2)}) %all-to-all-start.5) | async-done | bytes 917536 | tf_op jit(solution)/shard_map/all_to_all | solution.py:122
  (141 shorter events, 36.1 us)
Async XLA Ops:
  6.5 2.5 copy-start.7
  9.4 1.5 copy-start.8
  13.8 33.9 %all-to-all-start = ((bf16[8,128,896]{2,1,0:T(8,128)(2,1)}), bf16[8,128,896]{2,1,0:T(8,128)(2,1)S(1)}, u32[]{:S(2)}, u32[]{:S(2)}) async-start(bf16[8,128,896]{2,1,0:T(8,128)(2,1)} %pad_maximum_fusion), calls=%async_computation | async-start | bytes 3670016 | tf_op jit(solution)/shard_map/all_to_all | solution.py:73
  24.1 108.7 %all-gather.6.cloned.1.call-start = ((), (), s32[]{:S(2)}) async-start(), calls=%async_computation.8 | async-start | bytes 2293760 | tf_op jit(solution)/shard_map/all_gather | solution.py:47
  49.5 69.8 %all-to-all-start.1 = ((bf16[64,8,896]{2,1,0:T(8,128)(2,1)}), bf16[64,8,896]{2,1,0:T(8,128)(2,1)S(1)}, u32[]{:S(2)}, u32[]{:S(2)}) async-start(bf16[64,8,896]{2,1,0:T(8,128)(2,1)} %fusion.1), calls=%async_computation.1 | async-start | bytes 1835008 | tf_op jit(solution)/shard_map/all_to_all | solution.py:89
  63.4 139.4 %all-gather.8.cloned.1.call-start = ((), (), s32[]{:S(2)}) async-start(), calls=%async_computation.9 | async-start | bytes 2293760 | tf_op jit(solution)/shard_map/all_gather | solution.py:48
  64.2 190.6 %all-gather.10.cloned.1.call-start = ((), (), s32[]{:S(2)}) async-start(), calls=%async_computation.10 | async-start | bytes 2293760 | tf_op jit(solution)/shard_map/all_gather | solution.py:49
  119.3 141.3 %all-to-all-start.3 = ((bf16[64,8,896]{2,1,0:T(8,128)(2,1)}), bf16[64,8,896]{2,1,0:T(8,128)(2,1)}, u32[]{:S(2)}, u32[]{:S(2)}) async-start(bf16[64,8,896]{2,1,0:T(8,128)(2,1)} %fusion.2), calls=%async_computation.3 | async-start | bytes 1835008 | tf_op jit(solution)/shard_map/all_to_all | solution.py:89
  131.1 167.9 %reduce-scatter.7.cloned.1.call-start = ((), (), s32[]{:S(2)}) async-start(), calls=%async_computation.13 | async-start | bytes 1769472 | tf_op jit(solution)/shard_map/reduce_scatter | solution.py:101
  132.8 3.2 copy-start
  132.8 4.6 copy-start.12
  202.8 3.2 copy-start.1
  202.8 4.6 copy-start.13
  254.8 3.1 copy-start.10
  254.8 3.2 copy-start.14
  260.4 80.6 %reduce-scatter.9.cloned.1.call-start = ((), (), s32[]{:S(2)}) async-start(), calls=%async_computation.14 | async-start | bytes 1769472 | tf_op jit(solution)/shard_map/reduce_scatter | solution.py:101
  262.9 1.5 copy-start.2
  264.8 1.5 copy-start.11
  269.4 106.0 %all-gather.12.cloned.1.call-start = ((), (), s32[]{:S(2)}) async-start(), calls=%async_computation.11 | async-start | bytes 1179648 | tf_op jit(solution)/shard_map/all_gather | solution.py:106
  300.7 107.8 %all-gather.14.cloned.1.call-start = ((), (), s32[]{:S(2)}) async-start(), calls=%async_computation.12 | async-start | bytes 1179648 | tf_op jit(solution)/shard_map/all_gather | solution.py:106
  375.4 2.9 copy-start.6
  376.7 1.9 copy-start.3
  381.2 42.4 %all-to-all-start.2 = ((bf16[64,4,896]{2,1,0:T(4,128)(2,1)}), bf16[64,4,896]{2,1,0:T(4,128)(2,1)S(1)}, u32[]{:S(2)}, u32[]{:S(2)}) async-start(bf16[64,4,896]{2,1,0:T(4,128)(2,1)} %reshape.586), calls=%async_computation.2 | async-start | bytes 917504 | tf_op jit(solution)/shard_map/all_to_all | solution.py:115
  408.5 2.9 copy-start.5
  409.9 1.9 copy-start.4
  423.5 33.9 %all-to-all-start.4 = ((bf16[64,4,896]{2,1,0:T(4,128)(2,1)}), bf16[64,4,896]{2,1,0:T(4,128)(2,1)S(1)}, u32[]{:S(2)}, u32[]{:S(2)}) async-start(bf16[64,4,896]{2,1,0:T(4,128)(2,1)} %reshape.592), calls=%async_computation.4 | async-start | bytes 917504 | tf_op jit(solution)/shard_map/all_to_all | solution.py:115
  458.9 21.0 %all-to-all-start.5 = ((bf16[8,64,896]{2,1,0:T(8,128)(2,1)}), bf16[8,64,896]{2,1,0:T(8,128)(2,1)S(1)}, u32[]{:S(2)}, u32[]{:S(2)}) async-start(bf16[8,64,896]{2,1,0:T(8,128)(2,1)} %pad_maximum_fusion.1), calls=%async_computation.5 | async-start | bytes 1835008 | tf_op jit(solution)/shard_map/all_to_all | solution.py:122
  483.1 0.9 copy-start.9
Sparse Core Ops, SparseCore 0:
  27.1 83.8 all-gather.5
  113.0 89.7 all-gather.7
  204.9 49.7 all-gather.9
  260.5 38.4 reduce-scatter.6
  301.7 39.2 reduce-scatter.8
  343.0 32.3 all-gather.11
  377.5 30.9 all-gather.13

commit v2 on v1

v2 whole, which is shorter than its diff:
```python
import jax
import jax.numpy as jnp
from jax import lax
from jax.experimental import pallas as pl
from jax.experimental.pallas import tpu as pltpu
from jax.sharding import Mesh, PartitionSpec as P

BLOCK = 128
CAP = 4
QUARTERS = 4

PLANE = ("y", "x", "h", "l")
bf16 = jnp.bfloat16
f32 = jnp.float32


def mm(left, right):
    return jnp.dot(left, right, preferred_element_type=f32)


def mm_t(left, right):
    return lax.dot_general(left, right, (((1,), (1,)), ((), ())), preferred_element_type=f32)


def shift(array, axis, k):
    n = lax.axis_size(axis)
    return lax.ppermute(array, axis, [(i, (i + k) % n) for i in range(n)])


def swiglu_grads(gate_val, up_val, hidden_grad):
    sigmoid_gate = jax.nn.sigmoid(gate_val)
    gate_grad = hidden_grad * up_val * sigmoid_gate * (1.0 + gate_val * (1.0 - sigmoid_gate))
    up_grad = hidden_grad * gate_val * sigmoid_gate
    return gate_grad.astype(bf16), up_grad.astype(bf16)


def weight_copies(core, own, other, held, sems, kinds):
    return [
        [
            pltpu.make_async_copy(
                piece.at[:, kind], held.at[half, kind, k], sems.at[side, kind, k]
            )
            for side, (half, pieces) in enumerate(((core, own), (1 - core, other)))
            for k, piece in enumerate(pieces)
        ]
        for kind in range(kinds)
    ]


def forward_kernel(place, x_ref, g_ref, *refs):
    own, other = refs[:QUARTERS], refs[QUARTERS : 2 * QUARTERS]
    out_ref, held, sems = refs[2 * QUARTERS :]
    copies = weight_copies(place[1], own, other, held, sems, 3)
    for group in copies:
        for copy in group:
            copy.start()
    n_y, rows, _ = out_ref.shape
    _, _, n_k, n_m, units, cols = held.shape
    span = n_m * units
    for kind, rows_ref in enumerate((x_ref, x_ref, g_ref)):
        for copy in copies[kind]:
            copy.wait()
        for k in range(n_k):
            part = mm_t(rows_ref[:, :cols], held[0, kind, k].reshape(span, cols))
            part = part + mm_t(rows_ref[:, cols:], held[1, kind, k].reshape(span, cols))
            at = (kind * n_k + k) * span
            out_ref[:, :, at : at + span] = part.astype(bf16).reshape(n_y, rows, span)


def backward_kernel(place, *refs):
    acts = refs[:QUARTERS]
    own, other = refs[QUARTERS : 2 * QUARTERS], refs[2 * QUARTERS : 3 * QUARTERS]
    out_ref, held, acts_held, sems, act_sems = refs[3 * QUARTERS :]
    copies = weight_copies(place[1], own, other, held, sems, 2)
    act_copies = [
        pltpu.make_async_copy(act, acts_held.at[(place[0] - k + QUARTERS) % QUARTERS], act_sems.at[k])
        for k, act in enumerate(acts)
    ]
    for copy in act_copies:
        copy.start()
    for group in copies:
        for copy in group:
            copy.start()
    for copy in act_copies:
        copy.wait()
    for group in copies:
        for copy in group:
            copy.wait()
    n_y, rows, width = acts_held.shape
    _, _, n_k, n_m, units, cols = held.shape
    hidden = n_k * n_m * units
    both = acts_held[...].reshape(n_y * rows, width)
    for half in range(2):
        part = mm(both[:, :hidden], held[half, 0].reshape(hidden, cols))
        part = part + mm(both[:, hidden:], held[half, 1].reshape(hidden, cols))
        out_ref[:, half * cols : (half + 1) * cols] = part.astype(bf16)


ANY = pl.BlockSpec(memory_space=pl.ANY)
VMEM = pl.BlockSpec(memory_space=pltpu.VMEM)
SMEM = pl.BlockSpec(memory_space=pltpu.SMEM)
PARAMS = pltpu.CompilerParams(vmem_limit_bytes=40 * 1024 * 1024)


def forward_parts(place, x_rows, g_rows, own, other, n_y):
    total, width = x_rows.shape
    n_m, _, units, cols = own[0].shape
    hidden = QUARTERS * n_m * units
    return pl.pallas_call(
        forward_kernel,
        out_shape=jax.ShapeDtypeStruct((n_y, total // n_y, 3 * hidden), bf16),
        in_specs=[SMEM, VMEM, VMEM] + [ANY] * (2 * QUARTERS),
        out_specs=VMEM,
        scratch_shapes=[
            pltpu.VMEM((2, 3, QUARTERS, n_m, units, cols), bf16),
            pltpu.SemaphoreType.DMA((2, 3, QUARTERS)),
        ],
        compiler_params=PARAMS,
        cost_estimate=pl.CostEstimate(
            flops=6 * total * width * hidden,
            bytes_accessed=6 * width * hidden,
            transcendentals=0,
        ),
    )(place, x_rows, g_rows, *own, *other)


def backward_parts(place, acts, own, other):
    rows, double = acts[0].shape
    n_m, _, units, cols = own[0].shape
    total = QUARTERS * rows
    return pl.pallas_call(
        backward_kernel,
        out_shape=jax.ShapeDtypeStruct((total, 2 * cols), bf16),
        in_specs=[SMEM] + [ANY] * (3 * QUARTERS),
        out_specs=VMEM,
        scratch_shapes=[
            pltpu.VMEM((2, 2, QUARTERS, n_m, units, cols), bf16),
            pltpu.VMEM((QUARTERS, rows, double), bf16),
            pltpu.SemaphoreType.DMA((2, 2, QUARTERS)),
            pltpu.SemaphoreType.DMA((QUARTERS,)),
        ],
        compiler_params=PARAMS,
        cost_estimate=pl.CostEstimate(
            flops=4 * total * double * cols,
            bytes_accessed=4 * double * cols,
            transcendentals=0,
        ),
    )(place, *acts, *own, *other)


def moved_weights(gate, up, down):
    x, l = lax.axis_index("x"), lax.axis_index("l")
    hq, cols = down.shape
    units = hq // QUARTERS
    joined = jnp.stack([gate.T, up.T, down]).reshape(3, QUARTERS, units, cols).transpose(1, 0, 2, 3)

    def pick(array, index):
        return lax.dynamic_index_in_dim(array, index % QUARTERS, 0, keepdims=False)

    along_x = jnp.stack(
        [pick(joined, x)] + [shift(pick(joined, x + k), "x", k) for k in range(1, QUARTERS)]
    )
    along_l = jnp.stack(
        [pick(along_x, x - l + QUARTERS)]
        + [shift(pick(along_x, x - l - m + 2 * QUARTERS), "l", m) for m in range(1, QUARTERS)]
    )
    own = [along_l] + [shift(along_l, "x", k) for k in range(1, QUARTERS)]
    return own, [shift(piece, "c", 1) for piece in own]


def per_device(
    input_rows, row_scales, output_grad, expert_ids, combine_weights, gate_proj, up_proj, down_proj
):
    tokens, width = input_rows.shape
    n_y, n_ex = lax.axis_size("y"), lax.axis_size(("x", "h", "l"))
    window = n_ex // QUARTERS
    cols = width // n_y

    hits = (expert_ids[:, :, None] == jnp.arange(window, dtype=jnp.int32)).astype(f32)
    member = jnp.sum(hits, axis=1)
    pick_weight = jnp.sum(combine_weights[:, :, None] * hits, axis=1)
    before = jnp.cumsum(member, axis=0) - member
    select = member[:, :, None] * (
        before[:, :, None] == jnp.arange(CAP, dtype=f32)
    ).astype(f32)

    def by_device(array):
        split = array.reshape(tokens, QUARTERS, window // QUARTERS, CAP)
        return split.transpose(0, 3, 2, 1).reshape(tokens, n_ex)

    weighting = by_device(select * pick_weight[:, :, None])
    select = by_device(select).T.astype(bf16)

    x = (input_rows.astype(f32) * jnp.repeat(row_scales, BLOCK, axis=1)).astype(bf16)

    def picked(array, y):
        return mm(select, array[:, y * cols : (y + 1) * cols]).astype(bf16)

    sent = jnp.stack(
        [jnp.stack([picked(x, y), picked(output_grad, y)], axis=1) for y in range(n_y)]
    ).reshape(n_y * n_ex, 2, cols)
    there = lax.all_to_all(sent, PLANE, split_axis=0, concat_axis=0, tiled=True)

    own, other = moved_weights(gate_proj[0], up_proj[0], down_proj[0])
    place = jnp.stack([lax.axis_index("y"), lax.axis_index("c")]).astype(jnp.int32)
    parts = forward_parts(place, there[:, 0], there[:, 1], own, other, n_y)
    parts = lax.all_to_all(parts, "y", split_axis=0, concat_axis=0, tiled=True)
    summed = jnp.sum(parts.astype(f32), axis=0)
    hidden = summed.shape[1] // 3
    acts = jnp.concatenate(
        swiglu_grads(
            summed[:, :hidden], summed[:, hidden : 2 * hidden], summed[:, 2 * hidden :]
        ),
        axis=1,
    )
    acts = [acts] + [shift(acts, "y", k) for k in range(1, QUARTERS)]
    part = backward_parts(place, acts, own, other)
    home = lax.all_to_all(
        part.reshape(n_y * n_ex, 1, cols), PLANE, split_axis=0, concat_axis=0, tiled=True
    ).reshape(n_y, n_ex, cols)
    high = weighting.astype(bf16)
    low = (weighting - high.astype(f32)).astype(bf16)
    return jnp.concatenate(
        [(mm(high, home[y]) + mm(low, home[y])).astype(bf16) for y in range(n_y)], axis=1
    )


def solution(mesh):
    n_dp, n_ex = mesh.devices.shape
    fine = Mesh(
        mesh.devices.reshape(n_dp // 2, 2, QUARTERS, n_ex // QUARTERS**2, QUARTERS),
        ("y", "c", "x", "h", "l"),
    )
    tok = P(("y", "c", "x", "h", "l"), None)
    ex, dp = ("x", "h", "l"), ("y", "c")
    return jax.shard_map(
        per_device,
        mesh=fine,
        in_specs=(tok, tok, tok, tok, tok, P(ex, dp, None), P(ex, dp, None), P(ex, None, dp)),
        out_specs=tok,
        check_vma=False,
    )
```

time: 493 us -> 358 us (0.73)
  the two profiles are of different devices: /device:TPU:1 before, /device:TPU:32 now
where the time goes in v2:
time: 358 us; the launch traced here: 357 us
  waiting for transfers between devices  194 us (54%)
  starting transfers between devices  95 us (27%)
  blocking collectives  25.9 us (7%)
  local copies, waits for them, and re-layouts  16.4 us (5%)
  Pallas kernels  12.4 us (3%)
  other arithmetic  6.2 us (2%)
  matrix products  5.42 us (2%)
    ppermute x16, waiting for transfers between devices, shift(): return lax.ppermute(array, axis, [(i, (i + k) % n) for i in range(n)])  142 us
    all_to_all x1, waiting for transfers between devices, per_device(): lax.all_to_all(part.reshape(n_y * n_ex, 1, cols), PLANE, split_axis=0, co...  52.5 us
    ppermute x16, starting transfers between devices, shift(): return lax.ppermute(array, axis, [(i, (i + k) % n) for i in range(n)])  49.8 us
    all_to_all x1, blocking collectives, per_device(): parts = lax.all_to_all(parts, 'y', split_axis=0, concat_axis=0, tiled=True)  25.9 us
    all_to_all x1, starting transfers between devices, per_device(): there = lax.all_to_all(sent, PLANE, split_axis=0, concat_axis=0, tiled=True)  24.1 us
    all_to_all x1, starting transfers between devices, per_device(): lax.all_to_all(part.reshape(n_y * n_ex, 1, cols), PLANE, split_axis=0, co...  21.1 us
  transfers between devices with their start and end apart: 18, of which 9 were waited for; matrix products, arithmetic and copies ran while one was open for 2% of the time, Pallas kernels for 0%

profile of v2, /device:TPU:32, one launch (start us, length us, event | category | flops | bytes accessed | tf_op | source)
XLA Modules:
  0.0 356.5 jit_solution(9405030552376560266)
XLA Ops:
  6.8 3.1 copy.68
  9.9 24.1 %all-to-all-start = ((bf16[256,2,1792]{2,1,0:T(2,128)(2,1)}), bf16[256,2,1792]{2,1,0:T(2,128)(2,1)}, u32[]{:S(2)}, u32[]{:S(2)}) async-start(bf16[256,2,1792]{2,1,0:T(2,128)(2,1)} %copy.68), calls=%async_computation | async-start | bytes 3670016 | tf_op jit(solution)/shard_map/all_to_all | solution.py:202
  35.4 4.8 %collective-permute-start.2 = (bf16[3,64,896]{2,1,0:T(8,128)(2,1)S(1)}, bf16[3,64,896]{2,1,0:T(8,128)(2,1)S(1)}, u32[]{:S(2)}, u32[]{:S(2)}) collective-permute-start(bf16[3,64,896]{2,1,0:T(8,128)(2,1)S(1)} %get-tuple-element.18), channel_id=1, source_target_pairs={{0,48},{16,0},{32,16},{48,32},{1,49},{17,1},{33,17},{49,33},{2,50}... | collective-permute-start | bytes 1032200 | tf_op jit(solution)/shard_map/ppermute | solution.py:27
  40.2 2.6 collective-permute-start.1
  42.7 2.9 collective-permute-start
  45.7 13.0 %collective-permute-done.2 = bf16[3,64,896]{2,1,0:T(8,128)(2,1)S(1)} collective-permute-done((bf16[3,64,896]{2,1,0:T(8,128)(2,1)S(1)}, bf16[3,64,896]{2,1,0:T(8,128)(2,1)S(1)}, u32[]{:S(2)}, u32[]{:S(2)}) %collective-permute-start.2) | collective-permute-done | bytes 344096 | tf_op jit(solution)/shard_map/ppermute | solution.py:27
  58.6 5.6 %collective-permute-done = bf16[3,64,896]{2,1,0:T(8,128)(2,1)S(1)} collective-permute-done((bf16[3,64,896]{2,1,0:T(8,128)(2,1)S(1)}, bf16[3,64,896]{2,1,0:T(8,128)(2,1)S(1)}, u32[]{:S(2)}, u32[]{:S(2)}) %collective-permute-start) | collective-permute-done | bytes 344096 | tf_op jit(solution)/shard_map/ppermute | solution.py:27
  64.5 2.8 collective-permute-start.5
  67.4 4.0 %collective-permute-start.4 = (bf16[3,64,896]{2,1,0:T(8,128)(2,1)S(1)}, bf16[3,64,896]{2,1,0:T(8,128)(2,1)S(1)}, u32[]{:S(2)}, u32[]{:S(2)}) collective-permute-start(bf16[3,64,896]{2,1,0:T(8,128)(2,1)S(1)} %get-tuple-element.15), channel_id=1, source_target_pairs={{0,2},{1,3},{2,0},{3,1},{4,6},{5,7},{6,4},{7,5},{8,10},{9,11},{10,... | collective-permute-start | bytes 1032200 | tf_op jit(solution)/shard_map/ppermute | solution.py:27
  71.3 3.8 %collective-permute-start.3 = (bf16[3,64,896]{2,1,0:T(8,128)(2,1)S(1)}, bf16[3,64,896]{2,1,0:T(8,128)(2,1)S(1)}, u32[]{:S(2)}, u32[]{:S(2)}) collective-permute-start(bf16[3,64,896]{2,1,0:T(8,128)(2,1)S(1)} %get-tuple-element.16), channel_id=1, source_target_pairs={{0,1},{1,2},{2,3},{3,0},{4,5},{5,6},{6,7},{7,4},{8,9},{9,10},{10,1... | collective-permute-start | bytes 1032200 | tf_op jit(solution)/shard_map/ppermute | solution.py:27
  75.2 59.7 %collective-permute-done.5 = bf16[3,64,896]{2,1,0:T(8,128)(2,1)S(1)} collective-permute-done((bf16[3,64,896]{2,1,0:T(8,128)(2,1)S(1)}, bf16[3,64,896]{2,1,0:T(8,128)(2,1)S(1)}, u32[]{:S(2)}, u32[]{:S(2)}) %collective-permute-start.5) | collective-permute-done | bytes 344096 | tf_op jit(solution)/shard_map/ppermute | solution.py:27
  134.9 4.4 %collective-permute-done.3 = bf16[3,64,896]{2,1,0:T(8,128)(2,1)S(1)} collective-permute-done((bf16[3,64,896]{2,1,0:T(8,128)(2,1)S(1)}, bf16[3,64,896]{2,1,0:T(8,128)(2,1)S(1)}, u32[]{:S(2)}, u32[]{:S(2)}) %collective-permute-start.3) | collective-permute-done | bytes 344096 | tf_op jit(solution)/shard_map/ppermute | solution.py:27
  139.5 3.4 collective-permute-start.6
  142.9 4.8 %collective-permute-start.7 = (bf16[4,3,64,896]{3,2,1,0:T(8,128)(2,1)S(1)}, bf16[4,3,64,896]{3,2,1,0:T(8,128)(2,1)}, u32[]{:S(2)}, u32[]{:S(2)}) collective-permute-start(bf16[4,3,64,896]{3,2,1,0:T(8,128)(2,1)S(1)} %pad_maximum_fusion.3.refs_0_.refs_4_), channel_id=1, source_target_pairs={{0,32},{16,48},{32,0},{48,16},{1,33},{17,49},{33,1},{49,17},{2,34}... | collective-permute-start | bytes 4128776 | tf_op jit(solution)/shard_map/ppermute | solution.py:27
  147.7 3.3 collective-permute-start.8
  151.0 1.9 collective-permute-start.9
  152.9 21.7 %collective-permute-done.6.refs_1_.refs_5_ = bf16[4,3,64,896]{3,2,1,0:T(8,128)(2,1)S(1)} collective-permute-done((bf16[4,3,64,896]{3,2,1,0:T(8,128)(2,1)S(1)}, bf16[4,3,64,896]{3,2,1,0:T(8,128)(2,1)S(1)}, u32[]{:S(2)}, u32[]{:S(2)}) %collective-permute-start.6) | collective-permute-done | bytes 1376288 | tf_op jit(solution)/shard_map/ppermute | solution.py:27
  174.6 1.9 collective-permute-start.10
  176.5 28.9 %collective-permute-done.7.refs_2_.refs_6_ = bf16[4,3,64,896]{3,2,1,0:T(8,128)(2,1)} collective-permute-done((bf16[4,3,64,896]{3,2,1,0:T(8,128)(2,1)S(1)}, bf16[4,3,64,896]{3,2,1,0:T(8,128)(2,1)}, u32[]{:S(2)}, u32[]{:S(2)}) %collective-permute-start.7) | collective-permute-done | bytes 1376288 | tf_op jit(solution)/shard_map/ppermute | solution.py:27
  207.3 2.6 collective-permute-start.12
  210.0 5.2 %fusion.31 = (bf16[256,1,1792]{2,1,0:T(2,128)(2,1)S(1)}, bf16[256,1,1792]{2,1,0:T(2,128)(2,1)S(1)}) fusion(bf16[256,2,1792]{2,1,0:T(2,128)(2,1)} %all-to-all-done), kind=kLoop, calls=%fused_computation.81 | loop fusion | bytes 3670016 | tf_op jit(solution)/shard_map/slice | solution.py:206
  215.4 6.5 %shard_map.82 = bf16[4,64,3072]{2,1,0:T(8,128)(2,1)S(1)} custom-call(s32[2]{0:T(128)S(1)} %pad_add_fusion.place, bf16[256,1792]{1,0:T(8,128)(2,1)S(1)} %bitcast.116, bf16[256,1792]{1,0:T(8,128)(2,1)S(1)} %bitcast.117, bf16[4,3,64,896]{3,2,1,0:T(8,128)(2,1)S(1)} %pad_maximum_fusion.3.refs_0_.refs_4_, ...), custom_call_target="tpu_custom_call" | custom-call | flops 2818572288 | bytes 11010048 | tf_op jit(solution)/shard_map/pallas_call | solution.py:109
  222.0 25.9 %all_to_all.15 = bf16[4,64,3072]{2,1,0:T(8,128)(2,1)S(1)} all-to-all(bf16[4,64,3072]{2,1,0:T(8,128)(2,1)S(1)} %shard_map.82), channel_id=1, replica_groups=mesh['y'=4,'c'=2,'x'=4,'h'=4,'l'=4] {'y'}, dimensions={0} | all-to-all | bytes 3145728 | tf_op jit(solution)/shard_map/all_to_all | solution.py:207
  248.3 2.5 collective-permute-start.13
  250.8 4.0 %collective-permute-start.14 = (bf16[64,2048]{1,0:T(8,128)(2,1)S(1)}, bf16[64,2048]{1,0:T(8,128)(2,1)S(1)}, u32[]{:S(2)}, u32[]{:S(2)}) collective-permute-start(bf16[64,2048]{1,0:T(8,128)(2,1)S(1)} %pad_maximum_fusion.5.refs_0_), channel_id=1, source_target_pairs={{0,256},{128,384},{256,0},{384,128},{1,257},{129,385},{257,1},{385... | collective-permute-start | bytes 786440 | tf_op jit(solution)/shard_map/ppermute | solution.py:27
  254.8 2.7 collective-permute-start.15
  257.5 6.3 %collective-permute-done.13.refs_1_ = bf16[64,2048]{1,0:T(8,128)(2,1)S(1)} collective-permute-done((bf16[64,2048]{1,0:T(8,128)(2,1)S(1)}, bf16[64,2048]{1,0:T(8,128)(2,1)S(1)}, u32[]{:S(2)}, u32[]{:S(2)}) %collective-permute-start.13) | collective-permute-done | bytes 262176 | tf_op jit(solution)/shard_map/ppermute | solution.py:27
  263.8 2.5 collective-permute-done.15.refs_3_
  266.3 5.9 %shard_map.83 = bf16[256,1792]{1,0:T(8,128)(2,1)S(1)} custom-call(s32[2]{0:T(128)S(1)} %pad_add_fusion.place, bf16[64,2048]{1,0:T(8,128)(2,1)S(1)} %pad_maximum_fusion.5.refs_0_, bf16[64,2048]{1,0:T(8,128)(2,1)S(1)} %collective-permute-done.13.refs_1_, bf16[64,2048]{1,0:T(8,128)(2,1)S(1)} %collective-permute-done.14.refs_2_, ...), custom_call_target="tpu_custom_call" | custom-call | flops 1879048192 | bytes 7340032 | tf_op jit(solution)/shard_map/pallas_call | solution.py:131
  273.7 2.5 reduce
  277.3 21.1 %all-to-all-start.2 = ((bf16[256,2,896]{2,1,0:T(2,128)(2,1)}), bf16[256,2,896]{2,1,0:T(2,128)(2,1)S(1)}, u32[]{:S(2)}, u32[]{:S(2)}) async-start(bf16[256,2,896]{2,1,0:T(2,128)(2,1)} %reshape.240), calls=%async_computation.2 | async-start | bytes 1835008 | tf_op jit(solution)/shard_map/all_to_all | solution.py:218
  298.4 52.5 %all-to-all-done.2 = bf16[256,2,896]{2,1,0:T(2,128)(2,1)S(1)} async-done(((bf16[256,2,896]{2,1,0:T(2,128)(2,1)}), bf16[256,2,896]{2,1,0:T(2,128)(2,1)S(1)}, u32[]{:S(2)}, u32[]{:S(2)}) %all-to-all-start.2) | async-done | bytes 917536 | tf_op jit(solution)/shard_map/all_to_all | solution.py:218
  (77 shorter events, 19.2 us)
Async XLA Ops:
  0.0 3.6 %copy-start.6 = (f32[64,56]{0,1:T(8,128)S(1)}, f32[64,56]{0,1:T(8,128)}, u32[]{:S(2)}) copy-start(f32[64,56]{0,1:T(8,128)} %param.9) | copy-start | bytes 43012
  1.0 3.2 copy-start.1
  4.2 1.2 copy-start.2
  9.9 24.2 %copy-start.3 = (bf16[1,896,256]{2,1,0:T(8,128)(2,1)S(1)}, bf16[1,896,256]{2,1,0:T(8,128)(2,1)}, u32[]{:S(2)}) copy-start(bf16[1,896,256]{2,1,0:T(8,128)(2,1)} %param.14) | copy-start | bytes 1376260
  9.9 24.5 %copy-start.4 = (bf16[1,896,256]{2,1,0:T(8,128)(2,1)S(1)}, bf16[1,896,256]{2,1,0:T(8,128)(2,1)}, u32[]{:S(2)}) copy-start(bf16[1,896,256]{2,1,0:T(8,128)(2,1)} %param.13) | copy-start | bytes 1376260
  9.9 200.1 %all-to-all-start = ((bf16[256,2,1792]{2,1,0:T(2,128)(2,1)}), bf16[256,2,1792]{2,1,0:T(2,128)(2,1)}, u32[]{:S(2)}, u32[]{:S(2)}) async-start(bf16[256,2,1792]{2,1,0:T(2,128)(2,1)} %copy.68), calls=%async_computation | async-start | bytes 3670016 | tf_op jit(solution)/shard_map/all_to_all | solution.py:202
  34.0 1.0 copy-start.5
  35.4 23.3 %collective-permute-start.2 = (bf16[3,64,896]{2,1,0:T(8,128)(2,1)S(1)}, bf16[3,64,896]{2,1,0:T(8,128)(2,1)S(1)}, u32[]{:S(2)}, u32[]{:S(2)}) collective-permute-start(bf16[3,64,896]{2,1,0:T(8,128)(2,1)S(1)} %get-tuple-element.18), channel_id=1, source_target_pairs={{0,48},{16,0},{32,16},{48,32},{1,49},{17,1},{33,17},{49,33},{2,50}... | collective-permute-start | bytes 1032200 | tf_op jit(solution)/shard_map/ppermute | solution.py:27
  40.2 18.5 %collective-permute-start.1 = (bf16[3,64,896]{2,1,0:T(8,128)(2,1)S(1)}, bf16[3,64,896]{2,1,0:T(8,128)(2,1)S(1)}, u32[]{:S(2)}, u32[]{:S(2)}) collective-permute-start(bf16[3,64,896]{2,1,0:T(8,128)(2,1)S(1)} %get-tuple-element.19), channel_id=1, source_target_pairs={{0,32},{16,48},{32,0},{48,16},{1,33},{17,49},{33,1},{49,17},{2,34}... | collective-permute-start | bytes 1032200 | tf_op jit(solution)/shard_map/ppermute | solution.py:27
  42.7 21.4 %collective-permute-start = (bf16[3,64,896]{2,1,0:T(8,128)(2,1)S(1)}, bf16[3,64,896]{2,1,0:T(8,128)(2,1)S(1)}, u32[]{:S(2)}, u32[]{:S(2)}) collective-permute-start(bf16[3,64,896]{2,1,0:T(8,128)(2,1)S(1)} %get-tuple-element.20), channel_id=1, source_target_pairs={{0,16},{16,32},{32,48},{48,0},{1,17},{17,33},{33,49},{49,1},{2,18}... | collective-permute-start | bytes 1032200 | tf_op jit(solution)/shard_map/ppermute | solution.py:27
  64.5 70.4 %collective-permute-start.5 = (bf16[3,64,896]{2,1,0:T(8,128)(2,1)S(1)}, bf16[3,64,896]{2,1,0:T(8,128)(2,1)S(1)}, u32[]{:S(2)}, u32[]{:S(2)}) collective-permute-start(bf16[3,64,896]{2,1,0:T(8,128)(2,1)S(1)} %get-tuple-element.14), channel_id=1, source_target_pairs={{0,3},{1,0},{2,1},{3,2},{4,7},{5,4},{6,5},{7,6},{8,11},{9,8},{10,9... | collective-permute-start | bytes 1032200 | tf_op jit(solution)/shard_map/ppermute | solution.py:27
  67.4 67.5 %collective-permute-start.4 = (bf16[3,64,896]{2,1,0:T(8,128)(2,1)S(1)}, bf16[3,64,896]{2,1,0:T(8,128)(2,1)S(1)}, u32[]{:S(2)}, u32[]{:S(2)}) collective-permute-start(bf16[3,64,896]{2,1,0:T(8,128)(2,1)S(1)} %get-tuple-element.15), channel_id=1, source_target_pairs={{0,2},{1,3},{2,0},{3,1},{4,6},{5,7},{6,4},{7,5},{8,10},{9,11},{10,... | collective-permute-start | bytes 1032200 | tf_op jit(solution)/shard_map/ppermute | solution.py:27
  71.3 68.0 %collective-permute-start.3 = (bf16[3,64,896]{2,1,0:T(8,128)(2,1)S(1)}, bf16[3,64,896]{2,1,0:T(8,128)(2,1)S(1)}, u32[]{:S(2)}, u32[]{:S(2)}) collective-permute-start(bf16[3,64,896]{2,1,0:T(8,128)(2,1)S(1)} %get-tuple-element.16), channel_id=1, source_target_pairs={{0,1},{1,2},{2,3},{3,0},{4,5},{5,6},{6,7},{7,4},{8,9},{9,10},{10,1... | collective-permute-start | bytes 1032200 | tf_op jit(solution)/shard_map/ppermute | solution.py:27
  139.5 35.1 %collective-permute-start.6 = (bf16[4,3,64,896]{3,2,1,0:T(8,128)(2,1)S(1)}, bf16[4,3,64,896]{3,2,1,0:T(8,128)(2,1)S(1)}, u32[]{:S(2)}, u32[]{:S(2)}) collective-permute-start(bf16[4,3,64,896]{3,2,1,0:T(8,128)(2,1)S(1)} %pad_maximum_fusion.3.refs_0_.refs_4_), channel_id=1, source_target_pairs={{0,16},{16,32},{32,48},{48,0},{1,17},{17,33},{33,49},{49,1},{2,18}... | collective-permute-start | bytes 4128776 | tf_op jit(solution)/shard_map/ppermute | solution.py:27
  142.9 62.5 %collective-permute-start.7 = (bf16[4,3,64,896]{3,2,1,0:T(8,128)(2,1)S(1)}, bf16[4,3,64,896]{3,2,1,0:T(8,128)(2,1)}, u32[]{:S(2)}, u32[]{:S(2)}) collective-permute-start(bf16[4,3,64,896]{3,2,1,0:T(8,128)(2,1)S(1)} %pad_maximum_fusion.3.refs_0_.refs_4_), channel_id=1, source_target_pairs={{0,32},{16,48},{32,0},{48,16},{1,33},{17,49},{33,1},{49,17},{2,34}... | collective-permute-start | bytes 4128776 | tf_op jit(solution)/shard_map/ppermute | solution.py:27
  147.7 59.6 %collective-permute-start.8 = (bf16[4,3,64,896]{3,2,1,0:T(8,128)(2,1)S(1)}, bf16[4,3,64,896]{3,2,1,0:T(8,128)(2,1)}, u32[]{:S(2)}, u32[]{:S(2)}) collective-permute-start(bf16[4,3,64,896]{3,2,1,0:T(8,128)(2,1)S(1)} %pad_maximum_fusion.3.refs_0_.refs_4_), channel_id=1, source_target_pairs={{0,48},{16,0},{32,16},{48,32},{1,49},{17,1},{33,17},{49,33},{2,50}... | collective-permute-start | bytes 4128776 | tf_op jit(solution)/shard_map/ppermute | solution.py:27
  151.0 64.4 %collective-permute-start.9 = (bf16[4,3,64,896]{3,2,1,0:T(8,128)(2,1)S(1)}, bf16[4,3,64,896]{3,2,1,0:T(8,128)(2,1)}, u32[]{:S(2)}, u32[]{:S(2)}) collective-permute-start(bf16[4,3,64,896]{3,2,1,0:T(8,128)(2,1)S(1)} %pad_maximum_fusion.3.refs_0_.refs_4_), channel_id=1, source_target_pairs={{0,64},{64,0},{1,65},{65,1},{2,66},{66,2},{3,67},{67,3},{4,68},{68... | collective-permute-start | bytes 4128776 | tf_op jit(solution)/shard_map/ppermute | solution.py:27
  174.6 40.8 %collective-permute-start.10 = (bf16[4,3,64,896]{3,2,1,0:T(8,128)(2,1)S(1)}, bf16[4,3,64,896]{3,2,1,0:T(8,128)(2,1)}, u32[]{:S(2)}, u32[]{:S(2)}) collective-permute-start(bf16[4,3,64,896]{3,2,1,0:T(8,128)(2,1)S(1)} %collective-permute-done.6.refs_1_.refs_5_), channel_id=1, source_target_pairs={{0,64},{64,0},{1,65},{65,1},{2,66},{66,2},{3,67},{67,3},{4,68},{68... | collective-permute-start | bytes 4128776 | tf_op jit(solution)/shard_map/ppermute | solution.py:27
  205.4 10.1 %collective-permute-start.11 = (bf16[4,3,64,896]{3,2,1,0:T(8,128)(2,1)}, bf16[4,3,64,896]{3,2,1,0:T(8,128)(2,1)}, u32[]{:S(2)}, u32[]{:S(2)}) collective-permute-start(bf16[4,3,64,896]{3,2,1,0:T(8,128)(2,1)} %collective-permute-done.7.refs_2_.refs_6_), channel_id=1, source_target_pairs={{0,64},{64,0},{1,65},{65,1},{2,66},{66,2},{3,67},{67,3},{4,68},{68... | collective-permute-start | bytes 4128776 | tf_op jit(solution)/shard_map/ppermute | solution.py:27
  207.3 8.1 %collective-permute-start.12 = (bf16[4,3,64,896]{3,2,1,0:T(8,128)(2,1)}, bf16[4,3,64,896]{3,2,1,0:T(8,128)(2,1)}, u32[]{:S(2)}, u32[]{:S(2)}) collective-permute-start(bf16[4,3,64,896]{3,2,1,0:T(8,128)(2,1)} %collective-permute-done.8.refs_3_.refs_7_), channel_id=1, source_target_pairs={{0,64},{64,0},{1,65},{65,1},{2,66},{66,2},{3,67},{67,3},{4,68},{68... | collective-permute-start | bytes 4128776 | tf_op jit(solution)/shard_map/ppermute | solution.py:27
  248.3 15.5 %collective-permute-start.13 = (bf16[64,2048]{1,0:T(8,128)(2,1)S(1)}, bf16[64,2048]{1,0:T(8,128)(2,1)S(1)}, u32[]{:S(2)}, u32[]{:S(2)}) collective-permute-start(bf16[64,2048]{1,0:T(8,128)(2,1)S(1)} %pad_maximum_fusion.5.refs_0_), channel_id=1, source_target_pairs={{0,128},{128,256},{256,384},{384,0},{1,129},{129,257},{257,385},{3... | collective-permute-start | bytes 786440 | tf_op jit(solution)/shard_map/ppermute | solution.py:27
  250.8 13.0 %collective-permute-start.14 = (bf16[64,2048]{1,0:T(8,128)(2,1)S(1)}, bf16[64,2048]{1,0:T(8,128)(2,1)S(1)}, u32[]{:S(2)}, u32[]{:S(2)}) collective-permute-start(bf16[64,2048]{1,0:T(8,128)(2,1)S(1)} %pad_maximum_fusion.5.refs_0_), channel_id=1, source_target_pairs={{0,256},{128,384},{256,0},{384,128},{1,257},{129,385},{257,1},{385... | collective-permute-start | bytes 786440 | tf_op jit(solution)/shard_map/ppermute | solution.py:27
  254.8 11.5 %collective-permute-start.15 = (bf16[64,2048]{1,0:T(8,128)(2,1)S(1)}, bf16[64,2048]{1,0:T(8,128)(2,1)S(1)}, u32[]{:S(2)}, u32[]{:S(2)}) collective-permute-start(bf16[64,2048]{1,0:T(8,128)(2,1)S(1)} %pad_maximum_fusion.5.refs_0_), channel_id=1, source_target_pairs={{0,384},{128,0},{256,128},{384,256},{1,385},{129,1},{257,129},{385... | collective-permute-start | bytes 786440 | tf_op jit(solution)/shard_map/ppermute | solution.py:27
  272.2 0.9 copy-start
  277.3 73.6 %all-to-all-start.2 = ((bf16[256,2,896]{2,1,0:T(2,128)(2,1)}), bf16[256,2,896]{2,1,0:T(2,128)(2,1)S(1)}, u32[]{:S(2)}, u32[]{:S(2)}) async-start(bf16[256,2,896]{2,1,0:T(2,128)(2,1)} %reshape.240), calls=%async_computation.2 | async-start | bytes 1835008 | tf_op jit(solution)/shard_map/all_to_all | solution.py:218

commit v3 on v2

--- a/solution.py
+++ b/solution.py
@@ -164,7 +164,11 @@
         [pick(along_x, x - l + QUARTERS)]
         + [shift(pick(along_x, x - l - m + 2 * QUARTERS), "l", m) for m in range(1, QUARTERS)]
     )
-    own = [along_l] + [shift(along_l, "x", k) for k in range(1, QUARTERS)]
+    return along_l
+
+
+def spread_weights(piece):
+    own = [piece] + [shift(piece, "x", k) for k in range(1, QUARTERS)]
     return own, [shift(piece, "c", 1) for piece in own]
 
 
@@ -199,9 +203,11 @@
     sent = jnp.stack(
         [jnp.stack([picked(x, y), picked(output_grad, y)], axis=1) for y in range(n_y)]
     ).reshape(n_y * n_ex, 2, cols)
+    piece = moved_weights(gate_proj[0], up_proj[0], down_proj[0])
+    sent, piece = lax.optimization_barrier((sent, piece))
     there = lax.all_to_all(sent, PLANE, split_axis=0, concat_axis=0, tiled=True)
 
-    own, other = moved_weights(gate_proj[0], up_proj[0], down_proj[0])
+    own, other = spread_weights(piece)
     place = jnp.stack([lax.axis_index("y"), lax.axis_index("c")]).astype(jnp.int32)
     parts = forward_parts(place, there[:, 0], there[:, 1], own, other, n_y)
     parts = lax.all_to_all(parts, "y", split_axis=0, concat_axis=0, tiled=True)

time: 358 us -> 323 us (0.902)
  waiting for transfers between devices: 194 us -> 163 us
    ppermute x16, waiting for transfers between devices: 142 us -> 107 us  [shift(): return lax.ppermute(array, axis, [(i, (i + k) % n) for i in range(n)])]
  transfers between devices with their start and end apart: 18 -> 18, of which waited for: 9 -> 11; matrix products, arithmetic and copies ran while one was open for 2% -> 3% of each run, Pallas kernels for 0% -> 0%
where the time goes in v3:
time: 323 us; the launch traced here: 322 us
  waiting for transfers between devices  163 us (50%)
  starting transfers between devices  94.4 us (29%)
  blocking collectives  22.9 us (7%)
  local copies, waits for them, and re-layouts  18.8 us (6%)
  Pallas kernels  12.4 us (4%)
  other arithmetic  6.65 us (2%)
  matrix products  3.55 us (1%)
    ppermute x16, waiting for transfers between devices, shift(): return lax.ppermute(array, axis, [(i, (i + k) % n) for i in range(n)])  107 us
    all_to_all x1, waiting for transfers between devices, per_device(): lax.all_to_all(part.reshape(n_y * n_ex, 1, cols), PLANE, split_axis=0, co...  52.5 us
    ppermute x16, starting transfers between devices, shift(): return lax.ppermute(array, axis, [(i, (i + k) % n) for i in range(n)])  51.5 us
    all_to_all x1, starting transfers between devices, per_device(): there = lax.all_to_all(sent, PLANE, split_axis=0, concat_axis=0, tiled=True)  24.2 us
    all_to_all x1, blocking collectives, per_device(): parts = lax.all_to_all(parts, 'y', split_axis=0, concat_axis=0, tiled=True)  22.9 us
    all_to_all x1, starting transfers between devices, per_device(): lax.all_to_all(part.reshape(n_y * n_ex, 1, cols), PLANE, split_axis=0, co...  18.8 us
    pallas_call x1, Pallas kernels, forward_parts(): pl.pallas_call(forward_kernel, out_shape=jax.ShapeDtypeStruct((n_y, total...  6.52 us
  transfers between devices with their start and end apart: 18, of which 11 were waited for; matrix products, arithmetic and copies ran while one was open for 3% of the time, Pallas kernels for 0%

profile of v3, /device:TPU:32, one launch (start us, length us, event | category | flops | bytes accessed | tf_op | source)
XLA Modules:
  0.0 322.3 jit_solution(3697972717438799641)
XLA Ops:
  3.8 3.5 %collective-permute-start = (bf16[3,64,896]{2,1,0:T(8,128)(2,1)}, bf16[3,64,896]{2,1,0:T(8,128)(2,1)}, u32[]{:S(2)}, u32[]{:S(2)}) collective-permute-start(bf16[3,64,896]{2,1,0:T(8,128)(2,1)} %get-tuple-element.24), channel_id=1, source_target_pairs={{0,16},{16,32},{32,48},{48,0},{1,17},{17,33},{33,49},{49,1},{2,18}... | collective-permute-start | bytes 1032200 | tf_op jit(solution)/shard_map/ppermute | solution.py:27
  7.4 4.6 %collective-permute-start.1 = (bf16[3,64,896]{2,1,0:T(8,128)(2,1)}, bf16[3,64,896]{2,1,0:T(8,128)(2,1)}, u32[]{:S(2)}, u32[]{:S(2)}) collective-permute-start(bf16[3,64,896]{2,1,0:T(8,128)(2,1)} %get-tuple-element.23), channel_id=1, source_target_pairs={{0,32},{16,48},{32,0},{48,16},{1,33},{17,49},{33,1},{49,17},{2,34}... | collective-permute-start | bytes 1032200 | tf_op jit(solution)/shard_map/ppermute | solution.py:27
  12.0 3.3 %collective-permute-start.2 = (bf16[3,64,896]{2,1,0:T(8,128)(2,1)S(1)}, bf16[3,64,896]{2,1,0:T(8,128)(2,1)}, u32[]{:S(2)}, u32[]{:S(2)}) collective-permute-start(bf16[3,64,896]{2,1,0:T(8,128)(2,1)S(1)} %get-tuple-element.22), channel_id=1, source_target_pairs={{0,48},{16,0},{32,16},{48,32},{1,49},{17,1},{33,17},{49,33},{2,50}... | collective-permute-start | bytes 1032200 | tf_op jit(solution)/shard_map/ppermute | solution.py:27
  19.0 6.5 %collective-permute-done.1 = bf16[3,64,896]{2,1,0:T(8,128)(2,1)} collective-permute-done((bf16[3,64,896]{2,1,0:T(8,128)(2,1)}, bf16[3,64,896]{2,1,0:T(8,128)(2,1)}, u32[]{:S(2)}, u32[]{:S(2)}) %collective-permute-start.1) | collective-permute-done | bytes 344096 | tf_op jit(solution)/shard_map/ppermute | solution.py:27
  28.6 3.8 %collective-permute-start.3 = (bf16[3,64,896]{2,1,0:T(8,128)(2,1)S(1)}, bf16[3,64,896]{2,1,0:T(8,128)(2,1)S(1)}, u32[]{:S(2)}, u32[]{:S(2)}) collective-permute-start(bf16[3,64,896]{2,1,0:T(8,128)(2,1)S(1)} %get-tuple-element.20), channel_id=1, source_target_pairs={{0,1},{1,2},{2,3},{3,0},{4,5},{5,6},{6,7},{7,4},{8,9},{9,10},{10,1... | collective-permute-start | bytes 1032200 | tf_op jit(solution)/shard_map/ppermute | solution.py:27
  32.5 3.3 %collective-permute-start.4 = (bf16[3,64,896]{2,1,0:T(8,128)(2,1)S(1)}, bf16[3,64,896]{2,1,0:T(8,128)(2,1)S(1)}, u32[]{:S(2)}, u32[]{:S(2)}) collective-permute-start(bf16[3,64,896]{2,1,0:T(8,128)(2,1)S(1)} %get-tuple-element.19), channel_id=1, source_target_pairs={{0,2},{1,3},{2,0},{3,1},{4,6},{5,7},{6,4},{7,5},{8,10},{9,11},{10,... | collective-permute-start | bytes 1032200 | tf_op jit(solution)/shard_map/ppermute | solution.py:27
  35.7 3.9 %collective-permute-start.5 = (bf16[3,64,896]{2,1,0:T(8,128)(2,1)S(1)}, bf16[3,64,896]{2,1,0:T(8,128)(2,1)S(1)}, u32[]{:S(2)}, u32[]{:S(2)}) collective-permute-start(bf16[3,64,896]{2,1,0:T(8,128)(2,1)S(1)} %get-tuple-element.18), channel_id=1, source_target_pairs={{0,3},{1,0},{2,1},{3,2},{4,7},{5,4},{6,5},{7,6},{8,11},{9,8},{10,9... | collective-permute-start | bytes 1032200 | tf_op jit(solution)/shard_map/ppermute | solution.py:27
  40.1 15.6 %collective-permute-done.3 = bf16[3,64,896]{2,1,0:T(8,128)(2,1)S(1)} collective-permute-done((bf16[3,64,896]{2,1,0:T(8,128)(2,1)S(1)}, bf16[3,64,896]{2,1,0:T(8,128)(2,1)S(1)}, u32[]{:S(2)}, u32[]{:S(2)}) %collective-permute-start.3) | collective-permute-done | bytes 344096 | tf_op jit(solution)/shard_map/ppermute | solution.py:27
  55.7 5.2 %collective-permute-done.4 = bf16[3,64,896]{2,1,0:T(8,128)(2,1)S(1)} collective-permute-done((bf16[3,64,896]{2,1,0:T(8,128)(2,1)S(1)}, bf16[3,64,896]{2,1,0:T(8,128)(2,1)S(1)}, u32[]{:S(2)}, u32[]{:S(2)}) %collective-permute-start.4) | collective-permute-done | bytes 344096 | tf_op jit(solution)/shard_map/ppermute | solution.py:27
  60.9 2.1 collective-permute-done.5
  63.2 3.1 copy.70
  66.3 24.2 %all-to-all-start = ((bf16[256,2,1792]{2,1,0:T(2,128)(2,1)}), bf16[256,2,1792]{2,1,0:T(2,128)(2,1)}, u32[]{:S(2)}, u32[]{:S(2)}) async-start(bf16[256,2,1792]{2,1,0:T(2,128)(2,1)} %copy.70), calls=%async_computation | async-start | bytes 3670016 | tf_op jit(solution)/shard_map/all_to_all | solution.py:208
  90.5 3.4 %collective-permute-start.6 = (bf16[4,3,64,896]{3,2,1,0:T(8,128)(2,1)S(1)}, bf16[4,3,64,896]{3,2,1,0:T(8,128)(2,1)S(1)}, u32[]{:S(2)}, u32[]{:S(2)}) collective-permute-start(bf16[4,3,64,896]{3,2,1,0:T(8,128)(2,1)S(1)} %pad_maximum_fusion.3.refs_0_.refs_4_), channel_id=1, source_target_pairs={{0,16},{16,32},{32,48},{48,0},{1,17},{17,33},{33,49},{49,1},{2,18}... | collective-permute-start | bytes 4128776 | tf_op jit(solution)/shard_map/ppermute | solution.py:27
  93.9 4.8 %collective-permute-start.7 = (bf16[4,3,64,896]{3,2,1,0:T(8,128)(2,1)S(1)}, bf16[4,3,64,896]{3,2,1,0:T(8,128)(2,1)}, u32[]{:S(2)}, u32[]{:S(2)}) collective-permute-start(bf16[4,3,64,896]{3,2,1,0:T(8,128)(2,1)S(1)} %pad_maximum_fusion.3.refs_0_.refs_4_), channel_id=1, source_target_pairs={{0,32},{16,48},{32,0},{48,16},{1,33},{17,49},{33,1},{49,17},{2,34}... | collective-permute-start | bytes 4128776 | tf_op jit(solution)/shard_map/ppermute | solution.py:27
  98.7 3.3 %collective-permute-start.8 = (bf16[4,3,64,896]{3,2,1,0:T(8,128)(2,1)S(1)}, bf16[4,3,64,896]{3,2,1,0:T(8,128)(2,1)}, u32[]{:S(2)}, u32[]{:S(2)}) collective-permute-start(bf16[4,3,64,896]{3,2,1,0:T(8,128)(2,1)S(1)} %pad_maximum_fusion.3.refs_0_.refs_4_), channel_id=1, source_target_pairs={{0,48},{16,0},{32,16},{48,32},{1,49},{17,1},{33,17},{49,33},{2,50}... | collective-permute-start | bytes 4128776 | tf_op jit(solution)/shard_map/ppermute | solution.py:27
  101.9 1.9 collective-permute-start.9
  103.9 30.7 %collective-permute-done.6.refs_1_.refs_5_ = bf16[4,3,64,896]{3,2,1,0:T(8,128)(2,1)S(1)} collective-permute-done((bf16[4,3,64,896]{3,2,1,0:T(8,128)(2,1)S(1)}, bf16[4,3,64,896]{3,2,1,0:T(8,128)(2,1)S(1)}, u32[]{:S(2)}, u32[]{:S(2)}) %collective-permute-start.6) | collective-permute-done | bytes 1376288 | tf_op jit(solution)/shard_map/ppermute | solution.py:27
  136.5 37.2 %collective-permute-done.7.refs_2_.refs_6_ = bf16[4,3,64,896]{3,2,1,0:T(8,128)(2,1)} collective-permute-done((bf16[4,3,64,896]{3,2,1,0:T(8,128)(2,1)S(1)}, bf16[4,3,64,896]{3,2,1,0:T(8,128)(2,1)}, u32[]{:S(2)}, u32[]{:S(2)}) %collective-permute-start.7) | collective-permute-done | bytes 1376288 | tf_op jit(solution)/shard_map/ppermute | solution.py:27
  175.6 2.6 collective-permute-start.12
  178.3 3.1 all-to-all-done
  181.3 5.2 %fusion.31 = (bf16[256,1,1792]{2,1,0:T(2,128)(2,1)S(1)}, bf16[256,1,1792]{2,1,0:T(2,128)(2,1)S(1)}) fusion(bf16[256,2,1792]{2,1,0:T(2,128)(2,1)} %all-to-all-done), kind=kLoop, calls=%fused_computation.81 | loop fusion | bytes 3670016 | tf_op jit(solution)/shard_map/slice | solution.py:212
  186.8 6.5 %shard_map.82 = bf16[4,64,3072]{2,1,0:T(8,128)(2,1)S(1)} custom-call(s32[2]{0:T(128)S(1)} %pad_add_fusion.place, bf16[256,1792]{1,0:T(8,128)(2,1)S(1)} %bitcast.117, bf16[256,1792]{1,0:T(8,128)(2,1)S(1)} %bitcast.116, bf16[4,3,64,896]{3,2,1,0:T(8,128)(2,1)S(1)} %pad_maximum_fusion.3.refs_0_.refs_4_, ...), custom_call_target="tpu_custom_call" | custom-call | flops 2818572288 | bytes 11010048 | tf_op jit(solution)/shard_map/pallas_call | solution.py:109
  193.3 22.9 %all_to_all.15 = bf16[4,64,3072]{2,1,0:T(8,128)(2,1)S(1)} all-to-all(bf16[4,64,3072]{2,1,0:T(8,128)(2,1)S(1)} %shard_map.82), channel_id=1, replica_groups=mesh['y'=4,'c'=2,'x'=4,'h'=4,'l'=4] {'y'}, dimensions={0} | all-to-all | bytes 3145728 | tf_op jit(solution)/shard_map/all_to_all | solution.py:213
  216.6 2.5 collective-permute-start.13
  219.1 4.0 %collective-permute-start.14 = (bf16[64,2048]{1,0:T(8,128)(2,1)S(1)}, bf16[64,2048]{1,0:T(8,128)(2,1)S(1)}, u32[]{:S(2)}, u32[]{:S(2)}) collective-permute-start(bf16[64,2048]{1,0:T(8,128)(2,1)S(1)} %pad_maximum_fusion.5.refs_0_), channel_id=1, source_target_pairs={{0,256},{128,384},{256,0},{384,128},{1,257},{129,385},{257,1},{385... | collective-permute-start | bytes 786440 | tf_op jit(solution)/shard_map/ppermute | solution.py:27
  223.1 2.7 collective-permute-start.15
  225.8 6.1 %collective-permute-done.13.refs_1_ = bf16[64,2048]{1,0:T(8,128)(2,1)S(1)} collective-permute-done((bf16[64,2048]{1,0:T(8,128)(2,1)S(1)}, bf16[64,2048]{1,0:T(8,128)(2,1)S(1)}, u32[]{:S(2)}, u32[]{:S(2)}) %collective-permute-start.13) | collective-permute-done | bytes 262176 | tf_op jit(solution)/shard_map/ppermute | solution.py:27
  231.9 2.5 collective-permute-done.15.refs_3_
  234.4 5.9 %shard_map.83 = bf16[256,1792]{1,0:T(8,128)(2,1)S(1)} custom-call(s32[2]{0:T(128)S(1)} %pad_add_fusion.place, bf16[64,2048]{1,0:T(8,128)(2,1)S(1)} %pad_maximum_fusion.5.refs_0_, bf16[64,2048]{1,0:T(8,128)(2,1)S(1)} %collective-permute-done.13.refs_1_, bf16[64,2048]{1,0:T(8,128)(2,1)S(1)} %collective-permute-done.14.refs_2_, ...), custom_call_target="tpu_custom_call" | custom-call | flops 1879048192 | bytes 7340032 | tf_op jit(solution)/shard_map/pallas_call | solution.py:131
  241.8 2.5 reduce
  245.4 18.8 %all-to-all-start.2 = ((bf16[256,2,896]{2,1,0:T(2,128)(2,1)}), bf16[256,2,896]{2,1,0:T(2,128)(2,1)S(1)}, u32[]{:S(2)}, u32[]{:S(2)}) async-start(bf16[256,2,896]{2,1,0:T(2,128)(2,1)} %reshape.240), calls=%async_computation.2 | async-start | bytes 1835008 | tf_op jit(solution)/shard_map/all_to_all | solution.py:224
  264.2 52.5 %all-to-all-done.2 = bf16[256,2,896]{2,1,0:T(2,128)(2,1)S(1)} async-done(((bf16[256,2,896]{2,1,0:T(2,128)(2,1)}), bf16[256,2,896]{2,1,0:T(2,128)(2,1)S(1)}, u32[]{:S(2)}, u32[]{:S(2)}) %all-to-all-start.2) | async-done | bytes 917536 | tf_op jit(solution)/shard_map/all_to_all | solution.py:224
  (77 shorter events, 23.6 us)
Async XLA Ops:
  0.0 2.6 copy-start.3
  2.8 12.6 %copy-start.5 = (s32[64,8]{0,1:T(8,128)S(1)}, s32[64,8]{0,1:T(8,128)}, u32[]{:S(2)}) copy-start(s32[64,8]{0,1:T(8,128)} %param.11) | copy-start | bytes 6148
  2.8 12.6 %copy-start.6 = (f32[64,8]{0,1:T(8,128)S(1)}, f32[64,8]{0,1:T(8,128)}, u32[]{:S(2)}) copy-start(f32[64,8]{0,1:T(8,128)} %param.12) | copy-start | bytes 6148
  2.8 13.1 %copy-start.4 = (f32[64,56]{0,1:T(8,128)S(1)}, f32[64,56]{0,1:T(8,128)}, u32[]{:S(2)}) copy-start(f32[64,56]{0,1:T(8,128)} %param.9) | copy-start | bytes 43012
  3.8 12.7 %copy-start.1 = (bf16[64,7168]{1,0:T(8,128)(2,1)S(1)}, bf16[64,7168]{1,0:T(8,128)(2,1)}, u32[]{:S(2)}) copy-start(bf16[64,7168]{1,0:T(8,128)(2,1)} %param.8) | copy-start | bytes 2752516
  3.8 15.2 %collective-permute-start = (bf16[3,64,896]{2,1,0:T(8,128)(2,1)}, bf16[3,64,896]{2,1,0:T(8,128)(2,1)}, u32[]{:S(2)}, u32[]{:S(2)}) collective-permute-start(bf16[3,64,896]{2,1,0:T(8,128)(2,1)} %get-tuple-element.24), channel_id=1, source_target_pairs={{0,16},{16,32},{32,48},{48,0},{1,17},{17,33},{33,49},{49,1},{2,18}... | collective-permute-start | bytes 1032200 | tf_op jit(solution)/shard_map/ppermute | solution.py:27
  7.4 18.2 %collective-permute-start.1 = (bf16[3,64,896]{2,1,0:T(8,128)(2,1)}, bf16[3,64,896]{2,1,0:T(8,128)(2,1)}, u32[]{:S(2)}, u32[]{:S(2)}) collective-permute-start(bf16[3,64,896]{2,1,0:T(8,128)(2,1)} %get-tuple-element.23), channel_id=1, source_target_pairs={{0,32},{16,48},{32,0},{48,16},{1,33},{17,49},{33,1},{49,17},{2,34}... | collective-permute-start | bytes 1032200 | tf_op jit(solution)/shard_map/ppermute | solution.py:27
  12.0 15.1 %collective-permute-start.2 = (bf16[3,64,896]{2,1,0:T(8,128)(2,1)S(1)}, bf16[3,64,896]{2,1,0:T(8,128)(2,1)}, u32[]{:S(2)}, u32[]{:S(2)}) collective-permute-start(bf16[3,64,896]{2,1,0:T(8,128)(2,1)S(1)} %get-tuple-element.22), channel_id=1, source_target_pairs={{0,48},{16,0},{32,16},{48,32},{1,49},{17,1},{33,17},{49,33},{2,50}... | collective-permute-start | bytes 1032200 | tf_op jit(solution)/shard_map/ppermute | solution.py:27
  16.5 1.2 copy-start.2
  28.6 27.1 %collective-permute-start.3 = (bf16[3,64,896]{2,1,0:T(8,128)(2,1)S(1)}, bf16[3,64,896]{2,1,0:T(8,128)(2,1)S(1)}, u32[]{:S(2)}, u32[]{:S(2)}) collective-permute-start(bf16[3,64,896]{2,1,0:T(8,128)(2,1)S(1)} %get-tuple-element.20), channel_id=1, source_target_pairs={{0,1},{1,2},{2,3},{3,0},{4,5},{5,6},{6,7},{7,4},{8,9},{9,10},{10,1... | collective-permute-start | bytes 1032200 | tf_op jit(solution)/shard_map/ppermute | solution.py:27
  32.5 28.4 %collective-permute-start.4 = (bf16[3,64,896]{2,1,0:T(8,128)(2,1)S(1)}, bf16[3,64,896]{2,1,0:T(8,128)(2,1)S(1)}, u32[]{:S(2)}, u32[]{:S(2)}) collective-permute-start(bf16[3,64,896]{2,1,0:T(8,128)(2,1)S(1)} %get-tuple-element.19), channel_id=1, source_target_pairs={{0,2},{1,3},{2,0},{3,1},{4,6},{5,7},{6,4},{7,5},{8,10},{9,11},{10,... | collective-permute-start | bytes 1032200 | tf_op jit(solution)/shard_map/ppermute | solution.py:27
  35.7 27.3 %collective-permute-start.5 = (bf16[3,64,896]{2,1,0:T(8,128)(2,1)S(1)}, bf16[3,64,896]{2,1,0:T(8,128)(2,1)S(1)}, u32[]{:S(2)}, u32[]{:S(2)}) collective-permute-start(bf16[3,64,896]{2,1,0:T(8,128)(2,1)S(1)} %get-tuple-element.18), channel_id=1, source_target_pairs={{0,3},{1,0},{2,1},{3,2},{4,7},{5,4},{6,5},{7,6},{8,11},{9,8},{10,9... | collective-permute-start | bytes 1032200 | tf_op jit(solution)/shard_map/ppermute | solution.py:27
  66.3 115.0 %all-to-all-start = ((bf16[256,2,1792]{2,1,0:T(2,128)(2,1)}), bf16[256,2,1792]{2,1,0:T(2,128)(2,1)}, u32[]{:S(2)}, u32[]{:S(2)}) async-start(bf16[256,2,1792]{2,1,0:T(2,128)(2,1)} %copy.70), calls=%async_computation | async-start | bytes 3670016 | tf_op jit(solution)/shard_map/all_to_all | solution.py:208
  90.5 44.0 %collective-permute-start.6 = (bf16[4,3,64,896]{3,2,1,0:T(8,128)(2,1)S(1)}, bf16[4,3,64,896]{3,2,1,0:T(8,128)(2,1)S(1)}, u32[]{:S(2)}, u32[]{:S(2)}) collective-permute-start(bf16[4,3,64,896]{3,2,1,0:T(8,128)(2,1)S(1)} %pad_maximum_fusion.3.refs_0_.refs_4_), channel_id=1, source_target_pairs={{0,16},{16,32},{32,48},{48,0},{1,17},{17,33},{33,49},{49,1},{2,18}... | collective-permute-start | bytes 4128776 | tf_op jit(solution)/shard_map/ppermute | solution.py:27
  93.9 79.8 %collective-permute-start.7 = (bf16[4,3,64,896]{3,2,1,0:T(8,128)(2,1)S(1)}, bf16[4,3,64,896]{3,2,1,0:T(8,128)(2,1)}, u32[]{:S(2)}, u32[]{:S(2)}) collective-permute-start(bf16[4,3,64,896]{3,2,1,0:T(8,128)(2,1)S(1)} %pad_maximum_fusion.3.refs_0_.refs_4_), channel_id=1, source_target_pairs={{0,32},{16,48},{32,0},{48,16},{1,33},{17,49},{33,1},{49,17},{2,34}... | collective-permute-start | bytes 4128776 | tf_op jit(solution)/shard_map/ppermute | solution.py:27
  98.7 76.9 %collective-permute-start.8 = (bf16[4,3,64,896]{3,2,1,0:T(8,128)(2,1)S(1)}, bf16[4,3,64,896]{3,2,1,0:T(8,128)(2,1)}, u32[]{:S(2)}, u32[]{:S(2)}) collective-permute-start(bf16[4,3,64,896]{3,2,1,0:T(8,128)(2,1)S(1)} %pad_maximum_fusion.3.refs_0_.refs_4_), channel_id=1, source_target_pairs={{0,48},{16,0},{32,16},{48,32},{1,49},{17,1},{33,17},{49,33},{2,50}... | collective-permute-start | bytes 4128776 | tf_op jit(solution)/shard_map/ppermute | solution.py:27
  101.9 84.8 %collective-permute-start.9 = (bf16[4,3,64,896]{3,2,1,0:T(8,128)(2,1)S(1)}, bf16[4,3,64,896]{3,2,1,0:T(8,128)(2,1)}, u32[]{:S(2)}, u32[]{:S(2)}) collective-permute-start(bf16[4,3,64,896]{3,2,1,0:T(8,128)(2,1)S(1)} %pad_maximum_fusion.3.refs_0_.refs_4_), channel_id=1, source_target_pairs={{0,64},{64,0},{1,65},{65,1},{2,66},{66,2},{3,67},{67,3},{4,68},{68... | collective-permute-start | bytes 4128776 | tf_op jit(solution)/shard_map/ppermute | solution.py:27
  134.5 52.2 %collective-permute-start.10 = (bf16[4,3,64,896]{3,2,1,0:T(8,128)(2,1)S(1)}, bf16[4,3,64,896]{3,2,1,0:T(8,128)(2,1)}, u32[]{:S(2)}, u32[]{:S(2)}) collective-permute-start(bf16[4,3,64,896]{3,2,1,0:T(8,128)(2,1)S(1)} %collective-permute-done.6.refs_1_.refs_5_), channel_id=1, source_target_pairs={{0,64},{64,0},{1,65},{65,1},{2,66},{66,2},{3,67},{67,3},{4,68},{68... | collective-permute-start | bytes 4128776 | tf_op jit(solution)/shard_map/ppermute | solution.py:27
  173.7 13.1 %collective-permute-start.11 = (bf16[4,3,64,896]{3,2,1,0:T(8,128)(2,1)}, bf16[4,3,64,896]{3,2,1,0:T(8,128)(2,1)}, u32[]{:S(2)}, u32[]{:S(2)}) collective-permute-start(bf16[4,3,64,896]{3,2,1,0:T(8,128)(2,1)} %collective-permute-done.7.refs_2_.refs_6_), channel_id=1, source_target_pairs={{0,64},{64,0},{1,65},{65,1},{2,66},{66,2},{3,67},{67,3},{4,68},{68... | collective-permute-start | bytes 4128776 | tf_op jit(solution)/shard_map/ppermute | solution.py:27
  175.6 11.2 %collective-permute-start.12 = (bf16[4,3,64,896]{3,2,1,0:T(8,128)(2,1)}, bf16[4,3,64,896]{3,2,1,0:T(8,128)(2,1)}, u32[]{:S(2)}, u32[]{:S(2)}) collective-permute-start(bf16[4,3,64,896]{3,2,1,0:T(8,128)(2,1)} %collective-permute-done.8.refs_3_.refs_7_), channel_id=1, source_target_pairs={{0,64},{64,0},{1,65},{65,1},{2,66},{66,2},{3,67},{67,3},{4,68},{68... | collective-permute-start | bytes 4128776 | tf_op jit(solution)/shard_map/ppermute | solution.py:27
  216.6 15.3 %collective-permute-start.13 = (bf16[64,2048]{1,0:T(8,128)(2,1)S(1)}, bf16[64,2048]{1,0:T(8,128)(2,1)S(1)}, u32[]{:S(2)}, u32[]{:S(2)}) collective-permute-start(bf16[64,2048]{1,0:T(8,128)(2,1)S(1)} %pad_maximum_fusion.5.refs_0_), channel_id=1, source_target_pairs={{0,128},{128,256},{256,384},{384,0},{1,129},{129,257},{257,385},{3... | collective-permute-start | bytes 786440 | tf_op jit(solution)/shard_map/ppermute | solution.py:27
  219.1 12.8 %collective-permute-start.14 = (bf16[64,2048]{1,0:T(8,128)(2,1)S(1)}, bf16[64,2048]{1,0:T(8,128)(2,1)S(1)}, u32[]{:S(2)}, u32[]{:S(2)}) collective-permute-start(bf16[64,2048]{1,0:T(8,128)(2,1)S(1)} %pad_maximum_fusion.5.refs_0_), channel_id=1, source_target_pairs={{0,256},{128,384},{256,0},{384,128},{1,257},{129,385},{257,1},{385... | collective-permute-start | bytes 786440 | tf_op jit(solution)/shard_map/ppermute | solution.py:27
  223.1 11.3 %collective-permute-start.15 = (bf16[64,2048]{1,0:T(8,128)(2,1)S(1)}, bf16[64,2048]{1,0:T(8,128)(2,1)S(1)}, u32[]{:S(2)}, u32[]{:S(2)}) collective-permute-start(bf16[64,2048]{1,0:T(8,128)(2,1)S(1)} %pad_maximum_fusion.5.refs_0_), channel_id=1, source_target_pairs={{0,384},{128,0},{256,128},{384,256},{1,385},{129,1},{257,129},{385... | collective-permute-start | bytes 786440 | tf_op jit(solution)/shard_map/ppermute | solution.py:27
  240.3 0.9 copy-start
  245.4 71.3 %all-to-all-start.2 = ((bf16[256,2,896]{2,1,0:T(2,128)(2,1)}), bf16[256,2,896]{2,1,0:T(2,128)(2,1)S(1)}, u32[]{:S(2)}, u32[]{:S(2)}) async-start(bf16[256,2,896]{2,1,0:T(2,128)(2,1)} %reshape.240), calls=%async_computation.2 | async-start | bytes 1835008 | tf_op jit(solution)/shard_map/all_to_all | solution.py:224

commit v4 on v2

v4 whole, which is shorter than its diff:
```python
import jax
import jax.numpy as jnp
from jax import lax
from jax.experimental import pallas as pl
from jax.experimental.pallas import tpu as pltpu
from jax.sharding import Mesh, PartitionSpec as P

BLOCK = 128
CAP = 4
QUARTERS = 4

PARTS = 1
EX = ("x", "h", "l")
bf16 = jnp.bfloat16
f32 = jnp.float32


def mm(left, right):
    return jnp.dot(left, right, preferred_element_type=f32)


def mm_t(left, right):
    return lax.dot_general(left, right, (((1,), (1,)), ((), ())), preferred_element_type=f32)


def shift(array, axis, k):
    n = lax.axis_size(axis)
    return lax.ppermute(array, axis, [(i, (i + k) % n) for i in range(n)])


def swiglu_grads(gate_val, up_val, hidden_grad):
    sigmoid_gate = jax.nn.sigmoid(gate_val)
    gate_grad = hidden_grad * up_val * sigmoid_gate * (1.0 + gate_val * (1.0 - sigmoid_gate))
    up_grad = hidden_grad * gate_val * sigmoid_gate
    return gate_grad.astype(bf16), up_grad.astype(bf16)


def weight_copies(core, pieces, held, sems, kinds):
    parts = len(pieces) // 2
    return [
        [
            pltpu.make_async_copy(
                piece.at[:, :, kind],
                held.at[core if n < parts else 1 - core, kind, n % parts],
                sems.at[kind, n],
            )
            for n, piece in enumerate(pieces)
        ]
        for kind in range(kinds)
    ]


def forward_kernel(place, x_ref, g_ref, *refs):
    pieces = refs[: 2 * PARTS]
    out_ref, held, sems = refs[2 * PARTS :]
    copies = weight_copies(place[1], pieces, held, sems, 3)
    for group in copies:
        for copy in group:
            copy.start()
    n_y, rows, _ = out_ref.shape
    _, _, n_p, n_k, n_m, units, cols = held.shape
    span = 2 * n_m * units
    for kind, rows_ref in enumerate((x_ref, x_ref, g_ref)):
        for copy in copies[kind]:
            copy.wait()
        for block in range(n_p * n_k // 2):
            p, k = block // (n_k // 2), block % (n_k // 2) * 2
            part = mm_t(rows_ref[:, :cols], held[0, kind, p, k : k + 2].reshape(span, cols))
            part = part + mm_t(rows_ref[:, cols:], held[1, kind, p, k : k + 2].reshape(span, cols))
            at = (kind * (n_p * n_k // 2) + block) * span
            part = part.astype(bf16).reshape(n_y, rows, span)
            for y in range(n_y):
                out_ref[(y - place[0] + n_y) % n_y, :, at : at + span] = part[y]


def backward_kernel(place, *refs):
    acts, pieces = refs[:QUARTERS], refs[QUARTERS : QUARTERS + 2 * PARTS]
    out_ref, held, acts_held, sems, act_sems = refs[QUARTERS + 2 * PARTS :]
    copies = weight_copies(place[1], pieces, held, sems, 2)
    act_copies = [
        pltpu.make_async_copy(act, acts_held.at[(place[0] - k + QUARTERS) % QUARTERS], act_sems.at[k])
        for k, act in enumerate(acts)
    ]
    for copy in act_copies:
        copy.start()
    for group in copies:
        for copy in group:
            copy.start()
    for copy in act_copies:
        copy.wait()
    for group in copies:
        for copy in group:
            copy.wait()
    n_y, rows, width = acts_held.shape
    _, _, n_p, n_k, n_m, units, cols = held.shape
    hidden = n_p * n_k * n_m * units
    both = acts_held[...].reshape(n_y * rows, width)
    for half in range(2):
        part = mm(both[:, :hidden], held[half, 0].reshape(hidden, cols))
        part = part + mm(both[:, hidden:], held[half, 1].reshape(hidden, cols))
        out_ref[:, half * cols : (half + 1) * cols] = part.astype(bf16)


ANY = pl.BlockSpec(memory_space=pl.ANY)
VMEM = pl.BlockSpec(memory_space=pltpu.VMEM)
SMEM = pl.BlockSpec(memory_space=pltpu.SMEM)
PARAMS = pltpu.CompilerParams(vmem_limit_bytes=40 * 1024 * 1024)


def forward_parts(place, x_rows, g_rows, pieces, n_y):
    total, width = x_rows.shape
    n_k, n_m, _, units, cols = pieces[0].shape
    hidden = PARTS * n_k * n_m * units
    return pl.pallas_call(
        forward_kernel,
        out_shape=jax.ShapeDtypeStruct((n_y, total // n_y, 3 * hidden), bf16),
        in_specs=[SMEM, VMEM, VMEM] + [ANY] * (2 * PARTS),
        out_specs=VMEM,
        scratch_shapes=[
            pltpu.VMEM((2, 3, PARTS, n_k, n_m, units, cols), bf16),
            pltpu.SemaphoreType.DMA((3, 2 * PARTS)),
        ],
        compiler_params=PARAMS,
        cost_estimate=pl.CostEstimate(
            flops=6 * total * width * hidden,
            bytes_accessed=6 * width * hidden,
            transcendentals=0,
        ),
    )(place, x_rows, g_rows, *pieces)


def backward_parts(place, acts, pieces):
    rows, double = acts[0].shape
    n_k, n_m, _, units, cols = pieces[0].shape
    total = QUARTERS * rows
    return pl.pallas_call(
        backward_kernel,
        out_shape=jax.ShapeDtypeStruct((total, 2 * cols), bf16),
        in_specs=[SMEM] + [ANY] * (QUARTERS + 2 * PARTS),
        out_specs=VMEM,
        scratch_shapes=[
            pltpu.VMEM((2, 2, PARTS, n_k, n_m, units, cols), bf16),
            pltpu.VMEM((QUARTERS, rows, double), bf16),
            pltpu.SemaphoreType.DMA((2, 2 * PARTS)),
            pltpu.SemaphoreType.DMA((QUARTERS,)),
        ],
        compiler_params=PARAMS,
        cost_estimate=pl.CostEstimate(
            flops=4 * total * double * cols,
            bytes_accessed=4 * double * cols,
            transcendentals=0,
        ),
    )(place, *acts, *pieces)


def combine_kernel(high_ref, low_ref, home_ref, out_ref):
    cols = home_ref.shape[2]
    for y in range(home_ref.shape[0]):
        total = mm(high_ref[...], home_ref[y]) + mm(low_ref[...], home_ref[y])
        out_ref[:, y * cols : (y + 1) * cols] = total.astype(bf16)


def combined(high, low, home):
    n_y, slots, cols = home.shape
    tokens = high.shape[0]
    return pl.pallas_call(
        combine_kernel,
        out_shape=jax.ShapeDtypeStruct((tokens, n_y * cols), bf16),
        in_specs=[VMEM] * 3,
        out_specs=VMEM,
        compiler_params=PARAMS,
        cost_estimate=pl.CostEstimate(
            flops=4 * tokens * slots * n_y * cols,
            bytes_accessed=4 * slots * n_y * cols,
            transcendentals=0,
        ),
    )(high, low, home)


def pick(array, index):
    return lax.dynamic_index_in_dim(array, index % QUARTERS, 0, keepdims=False)


def weights_along_x(joined):
    x = lax.axis_index("x")
    return jnp.stack(
        [pick(joined, x)] + [shift(pick(joined, x + k), "x", k) for k in range(1, QUARTERS)]
    )


def weights_along_l(along_x):
    x, l = lax.axis_index("x"), lax.axis_index("l")
    return jnp.stack(
        [pick(along_x, x - l + QUARTERS)]
        + [shift(pick(along_x, x - l - m + 2 * QUARTERS), "l", m) for m in range(1, QUARTERS)]
    )


def weights_spread(along_l):
    return lax.all_gather(along_l, "x")


def one_hot_rows(source):
    count = source.shape[0]
    return (source[:, None] == jnp.arange(count, dtype=jnp.int32)[None, :]).astype(bf16)


def per_device(
    input_rows, row_scales, output_grad, expert_ids, combine_weights, gate_proj, up_proj, down_proj
):
    tokens, width = input_rows.shape
    n_y, n_ex = lax.axis_size("y"), lax.axis_size(EX)
    window = n_ex // QUARTERS
    cols = width // n_y

    hits = (expert_ids[:, :, None] == jnp.arange(window, dtype=jnp.int32)).astype(f32)
    member = jnp.sum(hits, axis=1)
    pick_weight = jnp.sum(combine_weights[:, :, None] * hits, axis=1)
    before = jnp.cumsum(member, axis=0) - member
    select = member[:, :, None] * (
        before[:, :, None] == jnp.arange(CAP, dtype=f32)
    ).astype(f32)

    def by_device(array):
        split = array.reshape(tokens, QUARTERS, window // QUARTERS, CAP)
        return split.transpose(0, 3, 2, 1).reshape(tokens, n_ex)

    weighting = by_device(select * pick_weight[:, :, None])
    select = by_device(select).T.astype(bf16)

    x = (input_rows.astype(f32) * jnp.repeat(row_scales, BLOCK, axis=1)).astype(bf16)

    def picked(array):
        return jnp.stack(
            [mm(select, array[:, y * cols : (y + 1) * cols]).astype(bf16) for y in range(n_y)]
        )

    hq, wide = down_proj.shape[1:]
    units = hq // QUARTERS // PARTS
    joined = jnp.stack([gate_proj[0].T, up_proj[0].T, down_proj[0]])
    joined = joined.reshape(3, QUARTERS, PARTS, units, wide).transpose(2, 1, 0, 3, 4)
    along_x = [weights_along_x(joined[p]) for p in range(PARTS)]

    sent = jnp.concatenate([picked(x), picked(output_grad)], axis=1)
    sent, *along_x = lax.optimization_barrier((sent, *along_x))
    got = lax.all_to_all(sent, "y", split_axis=0, concat_axis=0, tiled=True)

    along_l = [weights_along_l(piece) for piece in along_x]
    got, *along_l = lax.optimization_barrier((got, *along_l))
    own = [weights_spread(piece) for piece in along_l]
    pieces = own + [shift(piece, "c", 1) for piece in own]
    place = jnp.stack([lax.axis_index("y"), lax.axis_index("c")]).astype(jnp.int32)

    total = n_y * n_ex
    at = jnp.arange(2 * total, dtype=jnp.int32)
    device, kind, source = at // (2 * n_y), at // n_y % 2, at % n_y
    to_send = one_hot_rows(source * (2 * n_ex) + kind * n_ex + device)
    kind, source, device = at // total, at // n_ex % n_y, at % n_ex
    to_split = one_hot_rows(device * (2 * n_y) + kind * n_y + source)

    mine = mm(to_send, got.reshape(2 * total, cols)).astype(bf16).reshape(n_ex, 2 * n_y, cols)
    there = lax.all_to_all(mine, EX, split_axis=0, concat_axis=0, tiled=True)
    rows = mm(to_split, there.reshape(2 * total, cols)).astype(bf16)

    parts = forward_parts(place, rows[:total], rows[total:], pieces, n_y)
    summed = parts[0].astype(f32)
    for k in range(1, n_y):
        summed = summed + shift(parts[k], "y", k).astype(f32)
    hidden = summed.shape[1] // 3
    acts = jnp.concatenate(
        swiglu_grads(summed[:, :hidden], summed[:, hidden : 2 * hidden], summed[:, 2 * hidden :]),
        axis=1,
    )
    acts = [acts] + [shift(acts, "y", k) for k in range(1, n_y)]
    part = backward_parts(place, acts, pieces)
    home = lax.all_to_all(
        part.reshape(total, 1, cols), ("y",) + EX, split_axis=0, concat_axis=0, tiled=True
    )
    high = weighting.astype(bf16)
    low = (weighting - high.astype(f32)).astype(bf16)
    return combined(high, low, home.reshape(n_y, n_ex, cols))


def solution(mesh):
    n_dp, n_ex = mesh.devices.shape
    fine = Mesh(
        mesh.devices.reshape(n_dp // 2, 2, QUARTERS, n_ex // QUARTERS**2, QUARTERS),
        ("y", "c", "x", "h", "l"),
    )
    tok = P(("y", "c", "x", "h", "l"), None)
    dp = ("y", "c")
    return jax.shard_map(
        per_device,
        mesh=fine,
        in_specs=(tok, tok, tok, tok, tok, P(EX, dp, None), P(EX, dp, None), P(EX, None, dp)),
        out_specs=tok,
        check_vma=False,
    )
```

time: 358 us -> 323 us (0.902)
  blocking collectives: 25.9 us -> 0 us
  starting transfers between devices: 95 us -> 76.6 us
  between operations: 0.68 us -> 13.9 us
  local copies, waits for them, and re-layouts: 16.4 us -> 10.1 us
    ppermute x16 -> x13, waiting for transfers between devices: 142 us -> 59.2 us  [shift(): return lax.ppermute(array, axis, [(i, (i + k) % n) for i in range(n)])]
    all_gather x0 -> x1, waiting for transfers between devices: none -> 63.7 us  [weights_spread(): return lax.all_gather(along_l, 'x')]
    all_to_all x1 -> x0, blocking collectives: 25.9 us -> none  [per_device(): parts = lax.all_to_all(parts, 'y', split_axis=0, concat_axis=0, tiled=True)]
    all_to_all x2 -> x3, waiting for transfers between devices: 52.5 us -> 73.4 us  [the longest x1 52.4 us: per_device(): lax.all_to_all(part.reshape(total, 1, cols), ('y',) + EX, split_axis=0, c...]
    all_to_all x2 -> x3, starting transfers between devices: 45.2 us -> 32.7 us  [the longest x1 14.8 us: per_device(): there = lax.all_to_all(mine, EX, split_axis=0, concat_axis=0, tiled=True)]
    slice x2 -> x1, local copies, waits for them, and re-layouts: 7.09 us -> 0.12 us  [per_device(): parts = forward_parts(place, rows[:total], rows[total:], pieces, n_y)]
    ppermute x16 -> x13, starting transfers between devices: 49.8 us -> 43.9 us  [shift(): return lax.ppermute(array, axis, [(i, (i + k) % n) for i in range(n)])]
    unnamed x21 -> x20, local copies, waits for them, and re-layouts: 4.38 us -> 7.2 us
  transfers between devices with their start and end apart: 18 -> 17, of which waited for: 9 -> 12; matrix products, arithmetic and copies ran while one was open for 2% -> 3% of each run, Pallas kernels for 0% -> 0%
where the time goes in v4:
time: 323 us; the launch traced here: 322 us
  waiting for transfers between devices  196 us (61%)
  starting transfers between devices  76.6 us (24%)
  between operations  13.9 us (4%)
  Pallas kernels  12.9 us (4%)
  local copies, waits for them, and re-layouts  10.1 us (3%)
  other arithmetic  6.48 us (2%)
  matrix products  5.6 us (2%)
    all_gather x1, waiting for transfers between devices, weights_spread(): return lax.all_gather(along_l, 'x')  63.7 us
    ppermute x13, waiting for transfers between devices, shift(): return lax.ppermute(array, axis, [(i, (i + k) % n) for i in range(n)])  59.2 us
    all_to_all x1, waiting for transfers between devices, per_device(): lax.all_to_all(part.reshape(total, 1, cols), ('y',) + EX, split_axis=0, c...  52.4 us
    ppermute x13, starting transfers between devices, shift(): return lax.ppermute(array, axis, [(i, (i + k) % n) for i in range(n)])  43.9 us
    all_to_all x1, waiting for transfers between devices, per_device(): there = lax.all_to_all(mine, EX, split_axis=0, concat_axis=0, tiled=True)  21 us
    all_to_all x1, starting transfers between devices, per_device(): there = lax.all_to_all(mine, EX, split_axis=0, concat_axis=0, tiled=True)  14.8 us
    all_to_all x1, starting transfers between devices, per_device(): lax.all_to_all(part.reshape(total, 1, cols), ('y',) + EX, split_axis=0, c...  13.5 us
    unnamed x20, local copies, waits for them, and re-layouts  7.2 us
  transfers between devices with their start and end apart: 17, of which 12 were waited for; matrix products, arithmetic and copies ran while one was open for 3% of the time, Pallas kernels for 0%

profile of v4, /device:TPU:32, one launch (start us, length us, event | category | flops | bytes accessed | tf_op | source)
XLA Modules:
  0.0 321.9 jit_solution(15549347477559226762)
XLA Ops:
  10.4 4.8 %collective-permute-start.2 = (bf16[3,64,896]{2,1,0:T(8,128)(2,1)}, bf16[3,64,896]{2,1,0:T(8,128)(2,1)}, u32[]{:S(2)}, u32[]{:S(2)}) collective-permute-start(bf16[3,64,896]{2,1,0:T(8,128)(2,1)} %get-tuple-element.27), channel_id=1, source_target_pairs={{0,48},{16,0},{32,16},{48,32},{1,49},{17,1},{33,17},{49,33},{2,50}... | collective-permute-start | bytes 1032200 | tf_op jit(solution)/shard_map/ppermute | solution.py:28
  15.2 2.7 collective-permute-start.1
  17.9 2.8 collective-permute-start
  25.8 4.4 %collective-permute-done.2 = bf16[3,64,896]{2,1,0:T(8,128)(2,1)} collective-permute-done((bf16[3,64,896]{2,1,0:T(8,128)(2,1)}, bf16[3,64,896]{2,1,0:T(8,128)(2,1)}, u32[]{:S(2)}, u32[]{:S(2)}) %collective-permute-start.2) | collective-permute-done | bytes 344096 | tf_op jit(solution)/shard_map/ppermute | solution.py:28
  30.2 5.6 %collective-permute-done = bf16[3,64,896]{2,1,0:T(8,128)(2,1)} collective-permute-done((bf16[3,64,896]{2,1,0:T(8,128)(2,1)S(1)}, bf16[3,64,896]{2,1,0:T(8,128)(2,1)}, u32[]{:S(2)}, u32[]{:S(2)}) %collective-permute-start) | collective-permute-done | bytes 344096 | tf_op jit(solution)/shard_map/ppermute | solution.py:28
  37.2 4.5 %all-to-all-start = ((bf16[4,128,1792]{2,1,0:T(8,128)(2,1)}), bf16[4,128,1792]{2,1,0:T(8,128)(2,1)S(1)}, u32[]{:S(2)}, u32[]{:S(2)}) async-start(bf16[4,128,1792]{2,1,0:T(8,128)(2,1)} %maximum_maximum_fusion), calls=%async_computation | async-start | bytes 3670016 | tf_op jit(solution)/shard_map/all_to_all | solution.py:246
  41.8 2.0 collective-permute-start.5
  43.8 5.2 %collective-permute-start.4 = (bf16[3,64,896]{2,1,0:T(8,128)(2,1)S(1)}, bf16[3,64,896]{2,1,0:T(8,128)(2,1)S(1)}, u32[]{:S(2)}, u32[]{:S(2)}) collective-permute-start(bf16[3,64,896]{2,1,0:T(8,128)(2,1)S(1)} %get-tuple-element.24), channel_id=1, source_target_pairs={{0,2},{1,3},{2,0},{3,1},{4,6},{5,7},{6,4},{7,5},{8,10},{9,11},{10,... | collective-permute-start | bytes 1032200 | tf_op jit(solution)/shard_map/ppermute | solution.py:28
  49.0 4.7 %collective-permute-start.3 = (bf16[3,64,896]{2,1,0:T(8,128)(2,1)S(1)}, bf16[3,64,896]{2,1,0:T(8,128)(2,1)S(1)}, u32[]{:S(2)}, u32[]{:S(2)}) collective-permute-start(bf16[3,64,896]{2,1,0:T(8,128)(2,1)S(1)} %get-tuple-element.25), channel_id=1, source_target_pairs={{0,1},{1,2},{2,3},{3,0},{4,5},{5,6},{6,7},{7,4},{8,9},{9,10},{10,1... | collective-permute-start | bytes 1032200 | tf_op jit(solution)/shard_map/ppermute | solution.py:28
  53.7 1.6 collective-permute-done.5
  55.3 14.6 %collective-permute-done.4 = bf16[3,64,896]{2,1,0:T(8,128)(2,1)S(1)} collective-permute-done((bf16[3,64,896]{2,1,0:T(8,128)(2,1)S(1)}, bf16[3,64,896]{2,1,0:T(8,128)(2,1)S(1)}, u32[]{:S(2)}, u32[]{:S(2)}) %collective-permute-start.4) | collective-permute-done | bytes 344096 | tf_op jit(solution)/shard_map/ppermute | solution.py:28
  69.9 7.3 %collective-permute-done.3 = bf16[3,64,896]{2,1,0:T(8,128)(2,1)S(1)} collective-permute-done((bf16[3,64,896]{2,1,0:T(8,128)(2,1)S(1)}, bf16[3,64,896]{2,1,0:T(8,128)(2,1)S(1)}, u32[]{:S(2)}, u32[]{:S(2)}) %collective-permute-start.3) | collective-permute-done | bytes 344096 | tf_op jit(solution)/shard_map/ppermute | solution.py:28
  78.6 2.5 fusion
  81.1 14.8 %all-to-all-start.1 = ((bf16[64,8,1792]{2,1,0:T(8,128)(2,1)}), bf16[64,8,1792]{2,1,0:T(8,128)(2,1)S(1)}, u32[]{:S(2)}, u32[]{:S(2)}) async-start(bf16[64,8,1792]{2,1,0:T(8,128)(2,1)} %fusion), calls=%async_computation.1 | async-start | bytes 3670016 | tf_op jit(solution)/shard_map/all_to_all | solution.py:262
  95.8 63.7 %all-gather.3.cloned.1.call-done = bf16[16,3,64,896]{3,2,1,0:T(8,128)(2,1)} async-done(((bf16[4,3,64,896]{3,2,1,0:T(8,128)(2,1)}), bf16[16,3,64,896]{3,2,1,0:T(8,128)(2,1)}) %all-gather.3.cloned.1.call-update) | async-done | bytes 5505040 | tf_op jit(solution)/shard_map/all_gather | solution.py:200
  159.5 1.9 collective-permute-start.6
  161.5 21.0 %all-to-all-done.1 = bf16[64,8,1792]{2,1,0:T(8,128)(2,1)S(1)} async-done(((bf16[64,8,1792]{2,1,0:T(8,128)(2,1)}), bf16[64,8,1792]{2,1,0:T(8,128)(2,1)S(1)}, u32[]{:S(2)}, u32[]{:S(2)}) %all-to-all-start.1) | async-done | bytes 1835040 | tf_op jit(solution)/shard_map/all_to_all | solution.py:262
  183.9 2.6 copy-done
  186.5 6.1 %shard_map.82 = bf16[4,64,3072]{2,1,0:T(8,128)(2,1)S(1)} custom-call(s32[2]{0:T(128)S(1)} %pad_add_fusion.place, bf16[256,1792]{1,0:T(8,128)(2,1)S(1)} %get-tuple-element.18.x_ref, bf16[256,1792]{1,0:T(8,128)(2,1)S(1)} %get-tuple-element.17.g_ref, bf16[4,4,3,64,896]{4,3,2,1,0:T(8,128)(2,1)S(1)} %bitcast.96, ...), custom_call_target="tpu_custom_call" | custom-call | flops 2818572288 | bytes 11010048 | tf_op jit(solution)/shard_map/pallas_call | solution.py:114
  192.6 4.8 %collective-permute-start.9 = (bf16[64,3072]{1,0:T(8,128)(2,1)S(1)}, bf16[64,3072]{1,0:T(8,128)(2,1)S(1)}, u32[]{:S(2)}, u32[]{:S(2)}) collective-permute-start(bf16[64,3072]{1,0:T(8,128)(2,1)S(1)} %get-tuple-element.20), channel_id=1, source_target_pairs={{0,384},{128,0},{256,128},{384,256},{1,385},{129,1},{257,129},{385... | collective-permute-start | bytes 1179656 | tf_op jit(solution)/shard_map/ppermute | solution.py:28
  197.5 2.8 collective-permute-start.8
  200.2 2.8 collective-permute-start.7
  203.0 10.0 %collective-permute-done.9 = bf16[64,3072]{1,0:T(8,128)(2,1)S(1)} collective-permute-done((bf16[64,3072]{1,0:T(8,128)(2,1)S(1)}, bf16[64,3072]{1,0:T(8,128)(2,1)S(1)}, u32[]{:S(2)}, u32[]{:S(2)}) %collective-permute-start.9) | collective-permute-done | bytes 393248 | tf_op jit(solution)/shard_map/ppermute | solution.py:28
  213.0 5.6 %collective-permute-done.7 = bf16[64,3072]{1,0:T(8,128)(2,1)S(1)} collective-permute-done((bf16[64,3072]{1,0:T(8,128)(2,1)S(1)}, bf16[64,3072]{1,0:T(8,128)(2,1)S(1)}, u32[]{:S(2)}, u32[]{:S(2)}) %collective-permute-start.7) | collective-permute-done | bytes 393248 | tf_op jit(solution)/shard_map/ppermute | solution.py:28
  219.0 1.9 collective-permute-start.10
  220.9 4.0 %collective-permute-start.11 = (bf16[64,2048]{1,0:T(8,128)(2,1)S(1)}, bf16[64,2048]{1,0:T(8,128)(2,1)S(1)}, u32[]{:S(2)}, u32[]{:S(2)}) collective-permute-start(bf16[64,2048]{1,0:T(8,128)(2,1)S(1)} %pad_maximum_fusion.3.refs_0_), channel_id=1, source_target_pairs={{0,256},{128,384},{256,0},{384,128},{1,257},{129,385},{257,1},{385... | collective-permute-start | bytes 786440 | tf_op jit(solution)/shard_map/ppermute | solution.py:28
  224.9 3.5 %collective-permute-start.12 = (bf16[64,2048]{1,0:T(8,128)(2,1)S(1)}, bf16[64,2048]{1,0:T(8,128)(2,1)S(1)}, u32[]{:S(2)}, u32[]{:S(2)}) collective-permute-start(bf16[64,2048]{1,0:T(8,128)(2,1)S(1)} %pad_maximum_fusion.3.refs_0_), channel_id=1, source_target_pairs={{0,384},{128,0},{256,128},{384,256},{1,385},{129,1},{257,129},{385... | collective-permute-start | bytes 786440 | tf_op jit(solution)/shard_map/ppermute | solution.py:28
  228.4 7.5 %collective-permute-done.10.refs_1_ = bf16[64,2048]{1,0:T(8,128)(2,1)S(1)} collective-permute-done((bf16[64,2048]{1,0:T(8,128)(2,1)S(1)}, bf16[64,2048]{1,0:T(8,128)(2,1)S(1)}, u32[]{:S(2)}, u32[]{:S(2)}) %collective-permute-start.10) | collective-permute-done | bytes 262176 | tf_op jit(solution)/shard_map/ppermute | solution.py:28
  235.9 2.5 collective-permute-done.12.refs_3_
  238.5 5.3 %shard_map.83 = bf16[256,1792]{1,0:T(8,128)(2,1)S(1)} custom-call(s32[2]{0:T(128)S(1)} %pad_add_fusion.place, bf16[64,2048]{1,0:T(8,128)(2,1)S(1)} %pad_maximum_fusion.3.refs_0_, bf16[64,2048]{1,0:T(8,128)(2,1)S(1)} %collective-permute-done.10.refs_1_, bf16[64,2048]{1,0:T(8,128)(2,1)S(1)} %collective-permute-done.11.refs_2_, ...), custom_call_target="tpu_custom_call" | custom-call | flops 1879048192 | bytes 7340032 | tf_op jit(solution)/shard_map/pallas_call | solution.py:136
  246.7 13.5 %all-to-all-start.2 = ((bf16[256,2,896]{2,1,0:T(2,128)(2,1)}), bf16[256,2,896]{2,1,0:T(2,128)(2,1)S(1)}, u32[]{:S(2)}, u32[]{:S(2)}) async-start(bf16[256,2,896]{2,1,0:T(2,128)(2,1)} %reshape.167), calls=%async_computation.2 | async-start | bytes 1835008 | tf_op jit(solution)/shard_map/all_to_all | solution.py:276
  260.3 52.4 %all-to-all-done.2 = bf16[256,2,896]{2,1,0:T(2,128)(2,1)S(1)} async-done(((bf16[256,2,896]{2,1,0:T(2,128)(2,1)}), bf16[256,2,896]{2,1,0:T(2,128)(2,1)S(1)}, u32[]{:S(2)}, u32[]{:S(2)}) %all-to-all-start.2) | async-done | bytes 917536 | tf_op jit(solution)/shard_map/all_to_all | solution.py:276
  (70 shorter events, 18.8 us)
Async XLA Ops:
  6.5 2.6 copy-start.3
  9.3 11.3 %copy-start.5 = (f32[64,8]{0,1:T(8,128)S(1)}, f32[64,8]{0,1:T(8,128)}, u32[]{:S(2)}) copy-start(f32[64,8]{0,1:T(8,128)} %param.12) | copy-start | bytes 6148
  9.4 11.3 %copy-start.6 = (s32[64,8]{0,1:T(8,128)S(1)}, s32[64,8]{0,1:T(8,128)}, u32[]{:S(2)}) copy-start(s32[64,8]{0,1:T(8,128)} %param.11) | copy-start | bytes 6148
  9.4 12.0 %copy-start.2 = (bf16[64,7168]{1,0:T(8,128)(2,1)S(1)}, bf16[64,7168]{1,0:T(8,128)(2,1)}, u32[]{:S(2)}) copy-start(bf16[64,7168]{1,0:T(8,128)(2,1)} %param.10) | copy-start | bytes 2752516
  10.4 12.0 %copy-start.4 = (f32[64,56]{0,1:T(8,128)S(1)}, f32[64,56]{0,1:T(8,128)}, u32[]{:S(2)}) copy-start(f32[64,56]{0,1:T(8,128)} %param.9) | copy-start | bytes 43012
  10.4 19.8 %collective-permute-start.2 = (bf16[3,64,896]{2,1,0:T(8,128)(2,1)}, bf16[3,64,896]{2,1,0:T(8,128)(2,1)}, u32[]{:S(2)}, u32[]{:S(2)}) collective-permute-start(bf16[3,64,896]{2,1,0:T(8,128)(2,1)} %get-tuple-element.27), channel_id=1, source_target_pairs={{0,48},{16,0},{32,16},{48,32},{1,49},{17,1},{33,17},{49,33},{2,50}... | collective-permute-start | bytes 1032200 | tf_op jit(solution)/shard_map/ppermute | solution.py:28
  15.2 15.0 %collective-permute-start.1 = (bf16[3,64,896]{2,1,0:T(8,128)(2,1)}, bf16[3,64,896]{2,1,0:T(8,128)(2,1)}, u32[]{:S(2)}, u32[]{:S(2)}) collective-permute-start(bf16[3,64,896]{2,1,0:T(8,128)(2,1)} %get-tuple-element.28), channel_id=1, source_target_pairs={{0,32},{16,48},{32,0},{48,16},{1,33},{17,49},{33,1},{49,17},{2,34}... | collective-permute-start | bytes 1032200 | tf_op jit(solution)/shard_map/ppermute | solution.py:28
  17.9 17.9 %collective-permute-start = (bf16[3,64,896]{2,1,0:T(8,128)(2,1)S(1)}, bf16[3,64,896]{2,1,0:T(8,128)(2,1)}, u32[]{:S(2)}, u32[]{:S(2)}) collective-permute-start(bf16[3,64,896]{2,1,0:T(8,128)(2,1)S(1)} %get-tuple-element.29), channel_id=1, source_target_pairs={{0,16},{16,32},{32,48},{48,0},{1,17},{17,33},{33,49},{49,1},{2,18}... | collective-permute-start | bytes 1032200 | tf_op jit(solution)/shard_map/ppermute | solution.py:28
  21.4 1.6 copy-start.1
  37.2 41.4 %all-to-all-start = ((bf16[4,128,1792]{2,1,0:T(8,128)(2,1)}), bf16[4,128,1792]{2,1,0:T(8,128)(2,1)S(1)}, u32[]{:S(2)}, u32[]{:S(2)}) async-start(bf16[4,128,1792]{2,1,0:T(8,128)(2,1)} %maximum_maximum_fusion), calls=%async_computation | async-start | bytes 3670016 | tf_op jit(solution)/shard_map/all_to_all | solution.py:246
  41.6 117.9 %all-gather.3.cloned.1.call-start = ((), (), s32[]{:S(2)}) async-start(), calls=%async_computation.3 | async-start | bytes 6881280 | tf_op jit(solution)/shard_map/all_gather | solution.py:200
  41.8 13.6 %collective-permute-start.5 = (bf16[3,64,896]{2,1,0:T(8,128)(2,1)S(1)}, bf16[3,64,896]{2,1,0:T(8,128)(2,1)S(1)}, u32[]{:S(2)}, u32[]{:S(2)}) collective-permute-start(bf16[3,64,896]{2,1,0:T(8,128)(2,1)S(1)} %get-tuple-element.23), channel_id=1, source_target_pairs={{0,3},{1,0},{2,1},{3,2},{4,7},{5,4},{6,5},{7,6},{8,11},{9,8},{10,9... | collective-permute-start | bytes 1032200 | tf_op jit(solution)/shard_map/ppermute | solution.py:28
  43.8 26.1 %collective-permute-start.4 = (bf16[3,64,896]{2,1,0:T(8,128)(2,1)S(1)}, bf16[3,64,896]{2,1,0:T(8,128)(2,1)S(1)}, u32[]{:S(2)}, u32[]{:S(2)}) collective-permute-start(bf16[3,64,896]{2,1,0:T(8,128)(2,1)S(1)} %get-tuple-element.24), channel_id=1, source_target_pairs={{0,2},{1,3},{2,0},{3,1},{4,6},{5,7},{6,4},{7,5},{8,10},{9,11},{10,... | collective-permute-start | bytes 1032200 | tf_op jit(solution)/shard_map/ppermute | solution.py:28
  49.0 28.2 %collective-permute-start.3 = (bf16[3,64,896]{2,1,0:T(8,128)(2,1)S(1)}, bf16[3,64,896]{2,1,0:T(8,128)(2,1)S(1)}, u32[]{:S(2)}, u32[]{:S(2)}) collective-permute-start(bf16[3,64,896]{2,1,0:T(8,128)(2,1)S(1)} %get-tuple-element.25), channel_id=1, source_target_pairs={{0,1},{1,2},{2,3},{3,0},{4,5},{5,6},{6,7},{7,4},{8,9},{9,10},{10,1... | collective-permute-start | bytes 1032200 | tf_op jit(solution)/shard_map/ppermute | solution.py:28
  81.1 101.5 %all-to-all-start.1 = ((bf16[64,8,1792]{2,1,0:T(8,128)(2,1)}), bf16[64,8,1792]{2,1,0:T(8,128)(2,1)S(1)}, u32[]{:S(2)}, u32[]{:S(2)}) async-start(bf16[64,8,1792]{2,1,0:T(8,128)(2,1)} %fusion), calls=%async_computation.1 | async-start | bytes 3670016 | tf_op jit(solution)/shard_map/all_to_all | solution.py:262
  159.5 24.4 %collective-permute-start.6 = (bf16[4,4,3,64,896]{4,3,2,1,0:T(8,128)(2,1)}, bf16[4,4,3,64,896]{4,3,2,1,0:T(8,128)(2,1)}, u32[]{:S(2)}, u32[]{:S(2)}) collective-permute-start(bf16[4,4,3,64,896]{4,3,2,1,0:T(8,128)(2,1)} %bitcast.95), channel_id=1, source_target_pairs={{0,64},{64,0},{1,65},{65,1},{2,66},{66,2},{3,67},{67,3},{4,68},{68... | collective-permute-start | bytes 16515080 | tf_op jit(solution)/shard_map/ppermute | solution.py:28
  183.9 2.6 copy-start
  192.6 20.4 %collective-permute-start.9 = (bf16[64,3072]{1,0:T(8,128)(2,1)S(1)}, bf16[64,3072]{1,0:T(8,128)(2,1)S(1)}, u32[]{:S(2)}, u32[]{:S(2)}) collective-permute-start(bf16[64,3072]{1,0:T(8,128)(2,1)S(1)} %get-tuple-element.20), channel_id=1, source_target_pairs={{0,384},{128,0},{256,128},{384,256},{1,385},{129,1},{257,129},{385... | collective-permute-start | bytes 1179656 | tf_op jit(solution)/shard_map/ppermute | solution.py:28
  197.5 15.6 %collective-permute-start.8 = (bf16[64,3072]{1,0:T(8,128)(2,1)S(1)}, bf16[64,3072]{1,0:T(8,128)(2,1)S(1)}, u32[]{:S(2)}, u32[]{:S(2)}) collective-permute-start(bf16[64,3072]{1,0:T(8,128)(2,1)S(1)} %get-tuple-element.21), channel_id=1, source_target_pairs={{0,256},{128,384},{256,0},{384,128},{1,257},{129,385},{257,1},{385... | collective-permute-start | bytes 1179656 | tf_op jit(solution)/shard_map/ppermute | solution.py:28
  200.2 18.4 %collective-permute-start.7 = (bf16[64,3072]{1,0:T(8,128)(2,1)S(1)}, bf16[64,3072]{1,0:T(8,128)(2,1)S(1)}, u32[]{:S(2)}, u32[]{:S(2)}) collective-permute-start(bf16[64,3072]{1,0:T(8,128)(2,1)S(1)} %get-tuple-element.19), channel_id=1, source_target_pairs={{0,128},{128,256},{256,384},{384,0},{1,129},{129,257},{257,385},{3... | collective-permute-start | bytes 1179656 | tf_op jit(solution)/shard_map/ppermute | solution.py:28
  219.0 16.9 %collective-permute-start.10 = (bf16[64,2048]{1,0:T(8,128)(2,1)S(1)}, bf16[64,2048]{1,0:T(8,128)(2,1)S(1)}, u32[]{:S(2)}, u32[]{:S(2)}) collective-permute-start(bf16[64,2048]{1,0:T(8,128)(2,1)S(1)} %pad_maximum_fusion.3.refs_0_), channel_id=1, source_target_pairs={{0,128},{128,256},{256,384},{384,0},{1,129},{129,257},{257,385},{3... | collective-permute-start | bytes 786440 | tf_op jit(solution)/shard_map/ppermute | solution.py:28
  220.9 15.0 %collective-permute-start.11 = (bf16[64,2048]{1,0:T(8,128)(2,1)S(1)}, bf16[64,2048]{1,0:T(8,128)(2,1)S(1)}, u32[]{:S(2)}, u32[]{:S(2)}) collective-permute-start(bf16[64,2048]{1,0:T(8,128)(2,1)S(1)} %pad_maximum_fusion.3.refs_0_), channel_id=1, source_target_pairs={{0,256},{128,384},{256,0},{384,128},{1,257},{129,385},{257,1},{385... | collective-permute-start | bytes 786440 | tf_op jit(solution)/shard_map/ppermute | solution.py:28
  224.9 13.6 %collective-permute-start.12 = (bf16[64,2048]{1,0:T(8,128)(2,1)S(1)}, bf16[64,2048]{1,0:T(8,128)(2,1)S(1)}, u32[]{:S(2)}, u32[]{:S(2)}) collective-permute-start(bf16[64,2048]{1,0:T(8,128)(2,1)S(1)} %pad_maximum_fusion.3.refs_0_), channel_id=1, source_target_pairs={{0,384},{128,0},{256,128},{384,256},{1,385},{129,1},{257,129},{385... | collective-permute-start | bytes 786440 | tf_op jit(solution)/shard_map/ppermute | solution.py:28
  246.7 66.0 %all-to-all-start.2 = ((bf16[256,2,896]{2,1,0:T(2,128)(2,1)}), bf16[256,2,896]{2,1,0:T(2,128)(2,1)S(1)}, u32[]{:S(2)}, u32[]{:S(2)}) async-start(bf16[256,2,896]{2,1,0:T(2,128)(2,1)} %reshape.167), calls=%async_computation.2 | async-start | bytes 1835008 | tf_op jit(solution)/shard_map/all_to_all | solution.py:276
Sparse Core Ops, SparseCore 0:
  78.7 80.7 all-gather.2

commit v5 on v4

--- a/solution.py
+++ b/solution.py
@@ -9,7 +9,6 @@
 CAP = 4
 QUARTERS = 4
 
-PARTS = 1
 EX = ("x", "h", "l")
 bf16 = jnp.bfloat16
 f32 = jnp.float32
@@ -36,46 +35,46 @@
 
 
 def weight_copies(core, pieces, held, sems, kinds):
-    parts = len(pieces) // 2
-    return [
-        [
-            pltpu.make_async_copy(
-                piece.at[:, :, kind],
-                held.at[core if n < parts else 1 - core, kind, n % parts],
-                sems.at[kind, n],
-            )
-            for n, piece in enumerate(pieces)
-        ]
-        for kind in range(kinds)
-    ]
-
-
-def forward_kernel(place, x_ref, g_ref, *refs):
-    pieces = refs[: 2 * PARTS]
-    out_ref, held, sems = refs[2 * PARTS :]
+    half = len(pieces) // 2
+    copies = [[] for _ in range(kinds)]
+    for side in range(2):
+        first = 0
+        for n in range(side * half, side * half + half):
+            groups = pieces[n].shape[0]
+            for kind in range(kinds):
+                target = held.at[core if side == 0 else 1 - core, kind, first : first + groups]
+                copies[kind].append(
+                    pltpu.make_async_copy(pieces[n].at[:, kind], target, sems.at[kind, n])
+                )
+            first += groups
+    return copies
+
+
+def forward_kernel(place, order_ref, there_ref, *refs):
+    pieces, (out_ref, held, rows_held, sems) = refs[:-4], refs[-4:]
     copies = weight_copies(place[1], pieces, held, sems, 3)
     for group in copies:
         for copy in group:
             copy.start()
     n_y, rows, _ = out_ref.shape
-    _, _, n_p, n_k, n_m, units, cols = held.shape
-    span = 2 * n_m * units
+    rows_held[...] = mm(order_ref[...], there_ref[...]).astype(bf16)
+    x_ref, g_ref = rows_held.at[: n_y * rows], rows_held.at[n_y * rows :]
+    _, _, groups, units, cols = held.shape
+    span = QUARTERS * units
     for kind, rows_ref in enumerate((x_ref, x_ref, g_ref)):
         for copy in copies[kind]:
             copy.wait()
-        for block in range(n_p * n_k // 2):
-            p, k = block // (n_k // 2), block % (n_k // 2) * 2
-            part = mm_t(rows_ref[:, :cols], held[0, kind, p, k : k + 2].reshape(span, cols))
-            part = part + mm_t(rows_ref[:, cols:], held[1, kind, p, k : k + 2].reshape(span, cols))
-            at = (kind * (n_p * n_k // 2) + block) * span
-            part = part.astype(bf16).reshape(n_y, rows, span)
-            for y in range(n_y):
-                out_ref[(y - place[0] + n_y) % n_y, :, at : at + span] = part[y]
+        for block in range(groups // QUARTERS):
+            now = slice(block * QUARTERS, (block + 1) * QUARTERS)
+            part = mm_t(rows_ref[:, :cols], held[0, kind, now].reshape(span, cols))
+            part = part + mm_t(rows_ref[:, cols:], held[1, kind, now].reshape(span, cols))
+            at = (kind * (groups // QUARTERS) + block) * span
+            out_ref[:, :, at : at + span] = part.astype(bf16).reshape(n_y, rows, span)
 
 
 def backward_kernel(place, *refs):
-    acts, pieces = refs[:QUARTERS], refs[QUARTERS : QUARTERS + 2 * PARTS]
-    out_ref, held, acts_held, sems, act_sems = refs[QUARTERS + 2 * PARTS :]
+    acts, pieces = refs[:QUARTERS], refs[QUARTERS:-5]
+    out_ref, held, acts_held, sems, act_sems = refs[-5:]
     copies = weight_copies(place[1], pieces, held, sems, 2)
     act_copies = [
         pltpu.make_async_copy(act, acts_held.at[(place[0] - k + QUARTERS) % QUARTERS], act_sems.at[k])
@@ -92,13 +91,13 @@
         for copy in group:
             copy.wait()
     n_y, rows, width = acts_held.shape
-    _, _, n_p, n_k, n_m, units, cols = held.shape
-    hidden = n_p * n_k * n_m * units
+    _, _, groups, units, cols = held.shape
+    hidden = groups * units
     both = acts_held[...].reshape(n_y * rows, width)
     for half in range(2):
         part = mm(both[:, :hidden], held[half, 0].reshape(hidden, cols))
         part = part + mm(both[:, hidden:], held[half, 1].reshape(hidden, cols))
-        out_ref[:, half * cols : (half + 1) * cols] = part.astype(bf16)
+        out_ref[:, half] = part.astype(bf16)
 
 
 ANY = pl.BlockSpec(memory_space=pl.ANY)
@@ -107,41 +106,48 @@
 PARAMS = pltpu.CompilerParams(vmem_limit_bytes=40 * 1024 * 1024)
 
 
-def forward_parts(place, x_rows, g_rows, pieces, n_y):
-    total, width = x_rows.shape
-    n_k, n_m, _, units, cols = pieces[0].shape
-    hidden = PARTS * n_k * n_m * units
+def held_shape(pieces, kinds):
+    groups = sum(piece.shape[0] for piece in pieces) // 2
+    return (2, kinds, groups) + pieces[0].shape[2:]
+
+
+def forward_parts(place, order, there, pieces, n_y):
+    both, width = there.shape
+    total = both // 2
+    held = held_shape(pieces, 3)
+    hidden = held[2] * held[3]
     return pl.pallas_call(
         forward_kernel,
         out_shape=jax.ShapeDtypeStruct((n_y, total // n_y, 3 * hidden), bf16),
-        in_specs=[SMEM, VMEM, VMEM] + [ANY] * (2 * PARTS),
+        in_specs=[SMEM, VMEM, VMEM] + [ANY] * len(pieces),
         out_specs=VMEM,
         scratch_shapes=[
-            pltpu.VMEM((2, 3, PARTS, n_k, n_m, units, cols), bf16),
-            pltpu.SemaphoreType.DMA((3, 2 * PARTS)),
+            pltpu.VMEM(held, bf16),
+            pltpu.VMEM((both, width), bf16),
+            pltpu.SemaphoreType.DMA((3, len(pieces))),
         ],
         compiler_params=PARAMS,
         cost_estimate=pl.CostEstimate(
-            flops=6 * total * width * hidden,
+            flops=6 * total * width * hidden + 2 * both * both * width,
             bytes_accessed=6 * width * hidden,
             transcendentals=0,
         ),
-    )(place, x_rows, g_rows, *pieces)
+    )(place, order, there, *pieces)
 
 
 def backward_parts(place, acts, pieces):
     rows, double = acts[0].shape
-    n_k, n_m, _, units, cols = pieces[0].shape
-    total = QUARTERS * rows
+    held = held_shape(pieces, 2)
+    total, cols = QUARTERS * rows, held[4]
     return pl.pallas_call(
         backward_kernel,
-        out_shape=jax.ShapeDtypeStruct((total, 2 * cols), bf16),
-        in_specs=[SMEM] + [ANY] * (QUARTERS + 2 * PARTS),
+        out_shape=jax.ShapeDtypeStruct((total, 2, cols), bf16),
+        in_specs=[SMEM] + [ANY] * (QUARTERS + len(pieces)),
         out_specs=VMEM,
         scratch_shapes=[
-            pltpu.VMEM((2, 2, PARTS, n_k, n_m, units, cols), bf16),
+            pltpu.VMEM(held, bf16),
             pltpu.VMEM((QUARTERS, rows, double), bf16),
-            pltpu.SemaphoreType.DMA((2, 2 * PARTS)),
+            pltpu.SemaphoreType.DMA((2, len(pieces))),
             pltpu.SemaphoreType.DMA((QUARTERS,)),
         ],
         compiler_params=PARAMS,
@@ -183,9 +189,7 @@
 
 def weights_along_x(joined):
     x = lax.axis_index("x")
-    return jnp.stack(
-        [pick(joined, x)] + [shift(pick(joined, x + k), "x", k) for k in range(1, QUARTERS)]
-    )
+    return [pick(joined, x)] + [shift(pick(joined, x + k), "x", k) for k in range(1, QUARTERS)]
 
 
 def weights_along_l(along_x):
@@ -197,7 +201,10 @@
 
 
 def weights_spread(along_l):
-    return lax.all_gather(along_l, "x")
+    left, right = shift(along_l, "x", 1), shift(along_l, "x", -1)
+    half = along_l.shape[0] // 2
+    own = [along_l, left, right, shift(left[:half], "x", 1), shift(right[half:], "x", -1)]
+    return own + [shift(piece, "c", 1) for piece in own]
 
 
 def one_hot_rows(source):
@@ -213,6 +220,10 @@
     window = n_ex // QUARTERS
     cols = width // n_y
 
+    hq, wide = down_proj.shape[1:]
+    joined = jnp.stack([gate_proj[0].T, up_proj[0].T, down_proj[0]])
+    joined = joined.reshape(3, QUARTERS, hq // QUARTERS, wide).transpose(1, 0, 2, 3)
+
     hits = (expert_ids[:, :, None] == jnp.arange(window, dtype=jnp.int32)).astype(f32)
     member = jnp.sum(hits, axis=1)
     pick_weight = jnp.sum(combine_weights[:, :, None] * hits, axis=1)
@@ -235,20 +246,14 @@
             [mm(select, array[:, y * cols : (y + 1) * cols]).astype(bf16) for y in range(n_y)]
         )
 
-    hq, wide = down_proj.shape[1:]
-    units = hq // QUARTERS // PARTS
-    joined = jnp.stack([gate_proj[0].T, up_proj[0].T, down_proj[0]])
-    joined = joined.reshape(3, QUARTERS, PARTS, units, wide).transpose(2, 1, 0, 3, 4)
-    along_x = [weights_along_x(joined[p]) for p in range(PARTS)]
-
     sent = jnp.concatenate([picked(x), picked(output_grad)], axis=1)
+    along_x = weights_along_x(joined)
     sent, *along_x = lax.optimization_barrier((sent, *along_x))
     got = lax.all_to_all(sent, "y", split_axis=0, concat_axis=0, tiled=True)
 
-    along_l = [weights_along_l(piece) for piece in along_x]
-    got, *along_l = lax.optimization_barrier((got, *along_l))
-    own = [weights_spread(piece) for piece in along_l]
-    pieces = own + [shift(piece, "c", 1) for piece in own]
+    along_l = weights_along_l(jnp.stack(along_x))
+    got, along_l = lax.optimization_barrier((got, along_l))
+    pieces = weights_spread(along_l)
     place = jnp.stack([lax.axis_index("y"), lax.axis_index("c")]).astype(jnp.int32)
 
     total = n_y * n_ex
@@ -260,12 +265,9 @@
 
     mine = mm(to_send, got.reshape(2 * total, cols)).astype(bf16).reshape(n_ex, 2 * n_y, cols)
     there = lax.all_to_all(mine, EX, split_axis=0, concat_axis=0, tiled=True)
-    rows = mm(to_split, there.reshape(2 * total, cols)).astype(bf16)
-
-    parts = forward_parts(place, rows[:total], rows[total:], pieces, n_y)
-    summed = parts[0].astype(f32)
-    for k in range(1, n_y):
-        summed = summed + shift(parts[k], "y", k).astype(f32)
+    parts = forward_parts(place, to_split, there.reshape(2 * total, cols), pieces, n_y)
+    parts = lax.all_to_all(parts, "y", split_axis=0, concat_axis=0, tiled=True)
+    summed = jnp.sum(parts.astype(f32), axis=0)
     hidden = summed.shape[1] // 3
     acts = jnp.concatenate(
         swiglu_grads(summed[:, :hidden], summed[:, hidden : 2 * hidden], summed[:, 2 * hidden :]),
@@ -274,7 +276,7 @@
     acts = [acts] + [shift(acts, "y", k) for k in range(1, n_y)]
     part = backward_parts(place, acts, pieces)
     home = lax.all_to_all(
-        part.reshape(total, 1, cols), ("y",) + EX, split_axis=0, concat_axis=0, tiled=True
+        part, ("y",) + EX, split_axis=0, concat_axis=0, tiled=True
     )
     high = weighting.astype(bf16)
     low = (weighting - high.astype(f32)).astype(bf16)

time: 323 us -> 300 us (0.929)
  waiting for transfers between devices: 196 us -> 154 us
  blocking collectives: 0 us -> 23.8 us
  between operations: 13.9 us -> 0.54 us
  starting transfers between devices: 76.6 us -> 87.9 us
    all_gather x1 -> x0, waiting for transfers between devices: 63.7 us -> none  [weights_spread(): return lax.all_gather(along_l, 'x')]
    ppermute x13 -> x18, waiting for transfers between devices: 59.2 us -> 93.7 us  [shift(): return lax.ppermute(array, axis, [(i, (i + k) % n) for i in range(n)])]
    all_to_all x0 -> x1, blocking collectives: none -> 23.8 us  [per_device(): parts = lax.all_to_all(parts, 'y', split_axis=0, concat_axis=0, tiled=True)]
    all_to_all x1, waiting for transfers between devices: 21 us -> 8.67 us  [per_device(): there = lax.all_to_all(mine, EX, split_axis=0, concat_axis=0, tiled=True)]
    ppermute x13 -> x18, starting transfers between devices: 43.9 us -> 54.9 us  [shift(): return lax.ppermute(array, axis, [(i, (i + k) % n) for i in range(n)])]
    unnamed x20 -> x19, local copies, waits for them, and re-layouts: 7.2 us -> 4.65 us
  transfers between devices with their start and end apart: 17 -> 21, of which waited for: 12 -> 14; matrix products, arithmetic and copies ran while one was open for 3% -> 3% of each run, Pallas kernels for 0% -> 0%
where the time goes in v5:
time: 300 us; the launch traced here: 299 us
  waiting for transfers between devices  154 us (51%)
  starting transfers between devices  87.9 us (29%)
  blocking collectives  23.8 us (8%)
  Pallas kernels  15.3 us (5%)
  local copies, waits for them, and re-layouts  8.68 us (3%)
  other arithmetic  5.05 us (2%)
  matrix products  4.35 us (1%)
    ppermute x18, waiting for transfers between devices, shift(): return lax.ppermute(array, axis, [(i, (i + k) % n) for i in range(n)])  93.7 us
    ppermute x18, starting transfers between devices, shift(): return lax.ppermute(array, axis, [(i, (i + k) % n) for i in range(n)])  54.9 us
    all_to_all x1, waiting for transfers between devices, per_device(): lax.all_to_all(part, ('y',) + EX, split_axis=0, concat_axis=0, tiled=True)  51.3 us
    all_to_all x1, blocking collectives, per_device(): parts = lax.all_to_all(parts, 'y', split_axis=0, concat_axis=0, tiled=True)  23.8 us
    all_to_all x1, starting transfers between devices, per_device(): there = lax.all_to_all(mine, EX, split_axis=0, concat_axis=0, tiled=True)  14.9 us
    all_to_all x1, starting transfers between devices, per_device(): lax.all_to_all(part, ('y',) + EX, split_axis=0, concat_axis=0, tiled=True)  13.6 us
    all_to_all x1, waiting for transfers between devices, per_device(): there = lax.all_to_all(mine, EX, split_axis=0, concat_axis=0, tiled=True)  8.67 us
    pallas_call x1, Pallas kernels, forward_parts(): pl.pallas_call(forward_kernel, out_shape=jax.ShapeDtypeStruct((n_y, total...  7.74 us
  transfers between devices with their start and end apart: 21, of which 14 were waited for; matrix products, arithmetic and copies ran while one was open for 3% of the time, Pallas kernels for 0%

profile of v5, /device:TPU:32, one launch (start us, length us, event | category | flops | bytes accessed | tf_op | source)
XLA Modules:
  0.0 299.3 jit_solution(8783041824500906795)
XLA Ops:
  3.8 4.8 %collective-permute-start.2 = (bf16[3,64,896]{2,1,0:T(8,128)(2,1)}, bf16[3,64,896]{2,1,0:T(8,128)(2,1)}, u32[]{:S(2)}, u32[]{:S(2)}) collective-permute-start(bf16[3,64,896]{2,1,0:T(8,128)(2,1)} %get-tuple-element.27), channel_id=1, source_target_pairs={{0,48},{16,0},{32,16},{48,32},{1,49},{17,1},{33,17},{49,33},{2,50}... | collective-permute-start | bytes 1032200 | tf_op jit(solution)/shard_map/ppermute | solution.py:27
  8.6 2.7 collective-permute-start.1
  11.3 2.8 collective-permute-start
  19.2 4.4 %collective-permute-done.2 = bf16[3,64,896]{2,1,0:T(8,128)(2,1)} collective-permute-done((bf16[3,64,896]{2,1,0:T(8,128)(2,1)}, bf16[3,64,896]{2,1,0:T(8,128)(2,1)}, u32[]{:S(2)}, u32[]{:S(2)}) %collective-permute-start.2) | collective-permute-done | bytes 344096 | tf_op jit(solution)/shard_map/ppermute | solution.py:27
  23.6 5.6 %collective-permute-done = bf16[3,64,896]{2,1,0:T(8,128)(2,1)} collective-permute-done((bf16[3,64,896]{2,1,0:T(8,128)(2,1)S(1)}, bf16[3,64,896]{2,1,0:T(8,128)(2,1)}, u32[]{:S(2)}, u32[]{:S(2)}) %collective-permute-start) | collective-permute-done | bytes 344096 | tf_op jit(solution)/shard_map/ppermute | solution.py:27
  29.2 4.5 %all-to-all-start = ((bf16[4,128,1792]{2,1,0:T(8,128)(2,1)}), bf16[4,128,1792]{2,1,0:T(8,128)(2,1)S(1)}, u32[]{:S(2)}, u32[]{:S(2)}) async-start(bf16[4,128,1792]{2,1,0:T(8,128)(2,1)} %maximum_maximum_fusion), calls=%async_computation | async-start | bytes 3670016 | tf_op jit(solution)/shard_map/all_to_all | solution.py:252
  35.2 2.0 collective-permute-start.5
  37.2 5.2 %collective-permute-start.4 = (bf16[3,64,896]{2,1,0:T(8,128)(2,1)S(1)}, bf16[3,64,896]{2,1,0:T(8,128)(2,1)S(1)}, u32[]{:S(2)}, u32[]{:S(2)}) collective-permute-start(bf16[3,64,896]{2,1,0:T(8,128)(2,1)S(1)} %get-tuple-element.25), channel_id=1, source_target_pairs={{0,2},{1,3},{2,0},{3,1},{4,6},{5,7},{6,4},{7,5},{8,10},{9,11},{10,... | collective-permute-start | bytes 1032200 | tf_op jit(solution)/shard_map/ppermute | solution.py:27
  42.4 4.7 %collective-permute-start.3 = (bf16[3,64,896]{2,1,0:T(8,128)(2,1)S(1)}, bf16[3,64,896]{2,1,0:T(8,128)(2,1)S(1)}, u32[]{:S(2)}, u32[]{:S(2)}) collective-permute-start(bf16[3,64,896]{2,1,0:T(8,128)(2,1)S(1)} %get-tuple-element.26), channel_id=1, source_target_pairs={{0,1},{1,2},{2,3},{3,0},{4,5},{5,6},{6,7},{7,4},{8,9},{9,10},{10,1... | collective-permute-start | bytes 1032200 | tf_op jit(solution)/shard_map/ppermute | solution.py:27
  48.8 14.6 %collective-permute-done.4 = bf16[3,64,896]{2,1,0:T(8,128)(2,1)S(1)} collective-permute-done((bf16[3,64,896]{2,1,0:T(8,128)(2,1)S(1)}, bf16[3,64,896]{2,1,0:T(8,128)(2,1)S(1)}, u32[]{:S(2)}, u32[]{:S(2)}) %collective-permute-start.4) | collective-permute-done | bytes 344096 | tf_op jit(solution)/shard_map/ppermute | solution.py:27
  63.4 7.3 %collective-permute-done.3 = bf16[3,64,896]{2,1,0:T(8,128)(2,1)S(1)} collective-permute-done((bf16[3,64,896]{2,1,0:T(8,128)(2,1)S(1)}, bf16[3,64,896]{2,1,0:T(8,128)(2,1)S(1)}, u32[]{:S(2)}, u32[]{:S(2)}) %collective-permute-start.3) | collective-permute-done | bytes 344096 | tf_op jit(solution)/shard_map/ppermute | solution.py:27
  70.9 2.4 fusion
  73.3 14.9 %all-to-all-start.1 = ((bf16[64,8,1792]{2,1,0:T(8,128)(2,1)}), bf16[64,8,1792]{2,1,0:T(8,128)(2,1)}, u32[]{:S(2)}, u32[]{:S(2)}) async-start(bf16[64,8,1792]{2,1,0:T(8,128)(2,1)} %fusion), calls=%async_computation.1 | async-start | bytes 3670016 | tf_op jit(solution)/shard_map/all_to_all | solution.py:267
  88.2 4.8 %collective-permute-start.7 = (bf16[4,3,64,896]{3,2,1,0:T(8,128)(2,1)S(1)}, bf16[4,3,64,896]{3,2,1,0:T(8,128)(2,1)S(1)}, u32[]{:S(2)}, u32[]{:S(2)}) collective-permute-start(bf16[4,3,64,896]{3,2,1,0:T(8,128)(2,1)S(1)} %pad_maximum_fusion.2.refs_0_.refs_4_), channel_id=1, source_target_pairs={{0,48},{16,0},{32,16},{48,32},{1,49},{17,1},{33,17},{49,33},{2,50}... | collective-permute-start | bytes 4128776 | tf_op jit(solution)/shard_map/ppermute | solution.py:27
  93.0 1.9 collective-permute-start.6
  95.0 1.9 collective-permute-start.10
  96.9 33.6 %collective-permute-done.7.refs_2_.refs_6_ = bf16[4,3,64,896]{3,2,1,0:T(8,128)(2,1)S(1)} collective-permute-done((bf16[4,3,64,896]{3,2,1,0:T(8,128)(2,1)S(1)}, bf16[4,3,64,896]{3,2,1,0:T(8,128)(2,1)S(1)}, u32[]{:S(2)}, u32[]{:S(2)}) %collective-permute-start.7) | collective-permute-done | bytes 1376288 | tf_op jit(solution)/shard_map/ppermute | solution.py:27
  130.5 5.6 %collective-permute-start.9 = (bf16[2,3,64,896]{3,2,1,0:T(8,128)(2,1)S(1)}, bf16[2,3,64,896]{3,2,1,0:T(8,128)(2,1)S(1)}, u32[]{:S(2)}, u32[]{:S(2)}) collective-permute-start(bf16[2,3,64,896]{3,2,1,0:T(8,128)(2,1)S(1)} %slice.57), channel_id=1, source_target_pairs={{0,48},{16,0},{32,16},{48,32},{1,49},{17,1},{33,17},{49,33},{2,50}... | collective-permute-start | bytes 2064392 | tf_op jit(solution)/shard_map/ppermute | solution.py:27
  137.3 1.9 collective-permute-start.8
  141.1 2.4 collective-permute-start.11
  143.6 10.2 %collective-permute-done.9.refs_4_.refs_8_ = bf16[2,3,64,896]{3,2,1,0:T(8,128)(2,1)S(1)} collective-permute-done((bf16[2,3,64,896]{3,2,1,0:T(8,128)(2,1)S(1)}, bf16[2,3,64,896]{3,2,1,0:T(8,128)(2,1)S(1)}, u32[]{:S(2)}, u32[]{:S(2)}) %collective-permute-start.9) | collective-permute-done | bytes 688160 | tf_op jit(solution)/shard_map/ppermute | solution.py:27
  155.6 6.2 %collective-permute-done.8.refs_3_.refs_7_ = bf16[2,3,64,896]{3,2,1,0:T(8,128)(2,1)} collective-permute-done((bf16[2,3,64,896]{3,2,1,0:T(8,128)(2,1)S(1)}, bf16[2,3,64,896]{3,2,1,0:T(8,128)(2,1)}, u32[]{:S(2)}, u32[]{:S(2)}) %collective-permute-start.8) | collective-permute-done | bytes 688160 | tf_op jit(solution)/shard_map/ppermute | solution.py:27
  166.2 8.7 %all-to-all-done.1 = bf16[64,8,1792]{2,1,0:T(8,128)(2,1)} async-done(((bf16[64,8,1792]{2,1,0:T(8,128)(2,1)}), bf16[64,8,1792]{2,1,0:T(8,128)(2,1)}, u32[]{:S(2)}, u32[]{:S(2)}) %all-to-all-start.1) | async-done | bytes 1835040 | tf_op jit(solution)/shard_map/all_to_all | solution.py:267
  176.0 7.7 %shard_map.82 = bf16[4,64,3072]{2,1,0:T(8,128)(2,1)S(1)} custom-call(s32[2]{0:T(128)S(1)} %pad_add_fusion.place, bf16[512,512]{1,0:T(8,128)(2,1)S(1)} %copy-done.1, bf16[512,1792]{1,0:T(8,128)(2,1)} %bitcast.41.there_ref, bf16[4,3,64,896]{3,2,1,0:T(8,128)(2,1)S(1)} %pad_maximum_fusion.2.refs_0_.refs_4_, ...), custom_call_target="tpu_custom_call" | custom-call | flops 3758096384 | bytes 11010048 | tf_op jit(solution)/shard_map/pallas_call | solution.py:119
  183.7 23.8 %all_to_all.20 = bf16[4,64,3072]{2,1,0:T(8,128)(2,1)S(1)} all-to-all(bf16[4,64,3072]{2,1,0:T(8,128)(2,1)S(1)} %shard_map.82), channel_id=1, replica_groups=mesh['y'=4,'c'=2,'x'=4,'h'=4,'l'=4] {'y'}, dimensions={0} | all-to-all | bytes 3145728 | tf_op jit(solution)/shard_map/all_to_all | solution.py:269
  207.9 3.1 %collective-permute-start.17 = (bf16[64,2048]{1,0:T(8,128)(2,1)S(1)}, bf16[64,2048]{1,0:T(8,128)(2,1)S(1)}, u32[]{:S(2)}, u32[]{:S(2)}) collective-permute-start(bf16[64,2048]{1,0:T(8,128)(2,1)S(1)} %pad_maximum_fusion.3.refs_0_), channel_id=1, source_target_pairs={{0,384},{128,0},{256,128},{384,256},{1,385},{129,1},{257,129},{385... | collective-permute-start | bytes 786440 | tf_op jit(solution)/shard_map/ppermute | solution.py:27
  211.0 3.4 %collective-permute-start.16 = (bf16[64,2048]{1,0:T(8,128)(2,1)S(1)}, bf16[64,2048]{1,0:T(8,128)(2,1)S(1)}, u32[]{:S(2)}, u32[]{:S(2)}) collective-permute-start(bf16[64,2048]{1,0:T(8,128)(2,1)S(1)} %pad_maximum_fusion.3.refs_0_), channel_id=1, source_target_pairs={{0,256},{128,384},{256,0},{384,128},{1,257},{129,385},{257,1},{385... | collective-permute-start | bytes 786440 | tf_op jit(solution)/shard_map/ppermute | solution.py:27
  218.0 4.7 %collective-permute-done.16.refs_2_ = bf16[64,2048]{1,0:T(8,128)(2,1)S(1)} collective-permute-done((bf16[64,2048]{1,0:T(8,128)(2,1)S(1)}, bf16[64,2048]{1,0:T(8,128)(2,1)S(1)}, u32[]{:S(2)}, u32[]{:S(2)}) %collective-permute-start.16) | collective-permute-done | bytes 262176 | tf_op jit(solution)/shard_map/ppermute | solution.py:27
  222.7 2.5 collective-permute-done.15.refs_1_
  225.1 6.0 %shard_map.83 = bf16[256,2,896]{2,1,0:T(2,128)(2,1)S(1)} custom-call(s32[2]{0:T(128)S(1)} %pad_add_fusion.place, bf16[64,2048]{1,0:T(8,128)(2,1)S(1)} %pad_maximum_fusion.3.refs_0_, bf16[64,2048]{1,0:T(8,128)(2,1)S(1)} %collective-permute-done.15.refs_1_, bf16[64,2048]{1,0:T(8,128)(2,1)S(1)} %collective-permute-done.16.refs_2_, ...), custom_call_target="tpu_custom_call" | custom-call | flops 1879048192 | bytes 7340032 | tf_op jit(solution)/shard_map/pallas_call | solution.py:142
  232.1 13.6 %all-to-all-start.3 = ((bf16[256,2,896]{2,1,0:T(2,128)(2,1)}), bf16[256,2,896]{2,1,0:T(2,128)(2,1)S(1)}, u32[]{:S(2)}, u32[]{:S(2)}) async-start(bf16[256,2,896]{2,1,0:T(2,128)(2,1)} %copy-done), calls=%async_computation.3 | async-start | bytes 1835008 | tf_op jit(solution)/shard_map/all_to_all | solution.py:278
  245.8 51.3 %all-to-all-done.3 = bf16[256,2,896]{2,1,0:T(2,128)(2,1)S(1)} async-done(((bf16[256,2,896]{2,1,0:T(2,128)(2,1)}), bf16[256,2,896]{2,1,0:T(2,128)(2,1)S(1)}, u32[]{:S(2)}, u32[]{:S(2)}) %all-to-all-start.3) | async-done | bytes 917536 | tf_op jit(solution)/shard_map/all_to_all | solution.py:278
  (76 shorter events, 29.7 us)
Async XLA Ops:
  0.0 2.6 copy-start.4
  2.8 11.4 %copy-start.6 = (f32[64,8]{0,1:T(8,128)S(1)}, f32[64,8]{0,1:T(8,128)}, u32[]{:S(2)}) copy-start(f32[64,8]{0,1:T(8,128)} %param.12) | copy-start | bytes 6148
  2.8 11.4 %copy-start.7 = (s32[64,8]{0,1:T(8,128)S(1)}, s32[64,8]{0,1:T(8,128)}, u32[]{:S(2)}) copy-start(s32[64,8]{0,1:T(8,128)} %param.11) | copy-start | bytes 6148
  2.8 12.0 %copy-start.3 = (bf16[64,7168]{1,0:T(8,128)(2,1)S(1)}, bf16[64,7168]{1,0:T(8,128)(2,1)}, u32[]{:S(2)}) copy-start(bf16[64,7168]{1,0:T(8,128)(2,1)} %param.10) | copy-start | bytes 2752516
  3.8 12.0 %copy-start.5 = (f32[64,56]{0,1:T(8,128)S(1)}, f32[64,56]{0,1:T(8,128)}, u32[]{:S(2)}) copy-start(f32[64,56]{0,1:T(8,128)} %param.9) | copy-start | bytes 43012
  3.8 19.8 %collective-permute-start.2 = (bf16[3,64,896]{2,1,0:T(8,128)(2,1)}, bf16[3,64,896]{2,1,0:T(8,128)(2,1)}, u32[]{:S(2)}, u32[]{:S(2)}) collective-permute-start(bf16[3,64,896]{2,1,0:T(8,128)(2,1)} %get-tuple-element.27), channel_id=1, source_target_pairs={{0,48},{16,0},{32,16},{48,32},{1,49},{17,1},{33,17},{49,33},{2,50}... | collective-permute-start | bytes 1032200 | tf_op jit(solution)/shard_map/ppermute | solution.py:27
  8.6 15.0 %collective-permute-start.1 = (bf16[3,64,896]{2,1,0:T(8,128)(2,1)}, bf16[3,64,896]{2,1,0:T(8,128)(2,1)}, u32[]{:S(2)}, u32[]{:S(2)}) collective-permute-start(bf16[3,64,896]{2,1,0:T(8,128)(2,1)} %get-tuple-element.28), channel_id=1, source_target_pairs={{0,32},{16,48},{32,0},{48,16},{1,33},{17,49},{33,1},{49,17},{2,34}... | collective-permute-start | bytes 1032200 | tf_op jit(solution)/shard_map/ppermute | solution.py:27
  11.3 17.9 %collective-permute-start = (bf16[3,64,896]{2,1,0:T(8,128)(2,1)S(1)}, bf16[3,64,896]{2,1,0:T(8,128)(2,1)}, u32[]{:S(2)}, u32[]{:S(2)}) collective-permute-start(bf16[3,64,896]{2,1,0:T(8,128)(2,1)S(1)} %get-tuple-element.29), channel_id=1, source_target_pairs={{0,16},{16,32},{32,48},{48,0},{1,17},{17,33},{33,49},{49,1},{2,18}... | collective-permute-start | bytes 1032200 | tf_op jit(solution)/shard_map/ppermute | solution.py:27
  14.8 1.6 copy-start.2
  29.2 41.6 %all-to-all-start = ((bf16[4,128,1792]{2,1,0:T(8,128)(2,1)}), bf16[4,128,1792]{2,1,0:T(8,128)(2,1)S(1)}, u32[]{:S(2)}, u32[]{:S(2)}) async-start(bf16[4,128,1792]{2,1,0:T(8,128)(2,1)} %maximum_maximum_fusion), calls=%async_computation | async-start | bytes 3670016 | tf_op jit(solution)/shard_map/all_to_all | solution.py:252
  35.2 13.6 %collective-permute-start.5 = (bf16[3,64,896]{2,1,0:T(8,128)(2,1)S(1)}, bf16[3,64,896]{2,1,0:T(8,128)(2,1)S(1)}, u32[]{:S(2)}, u32[]{:S(2)}) collective-permute-start(bf16[3,64,896]{2,1,0:T(8,128)(2,1)S(1)} %get-tuple-element.24), channel_id=1, source_target_pairs={{0,3},{1,0},{2,1},{3,2},{4,7},{5,4},{6,5},{7,6},{8,11},{9,8},{10,9... | collective-permute-start | bytes 1032200 | tf_op jit(solution)/shard_map/ppermute | solution.py:27
  37.2 26.1 %collective-permute-start.4 = (bf16[3,64,896]{2,1,0:T(8,128)(2,1)S(1)}, bf16[3,64,896]{2,1,0:T(8,128)(2,1)S(1)}, u32[]{:S(2)}, u32[]{:S(2)}) collective-permute-start(bf16[3,64,896]{2,1,0:T(8,128)(2,1)S(1)} %get-tuple-element.25), channel_id=1, source_target_pairs={{0,2},{1,3},{2,0},{3,1},{4,6},{5,7},{6,4},{7,5},{8,10},{9,11},{10,... | collective-permute-start | bytes 1032200 | tf_op jit(solution)/shard_map/ppermute | solution.py:27
  42.4 28.2 %collective-permute-start.3 = (bf16[3,64,896]{2,1,0:T(8,128)(2,1)S(1)}, bf16[3,64,896]{2,1,0:T(8,128)(2,1)S(1)}, u32[]{:S(2)}, u32[]{:S(2)}) collective-permute-start(bf16[3,64,896]{2,1,0:T(8,128)(2,1)S(1)} %get-tuple-element.26), channel_id=1, source_target_pairs={{0,1},{1,2},{2,3},{3,0},{4,5},{5,6},{6,7},{7,4},{8,9},{9,10},{10,1... | collective-permute-start | bytes 1032200 | tf_op jit(solution)/shard_map/ppermute | solution.py:27
  73.3 101.6 %all-to-all-start.1 = ((bf16[64,8,1792]{2,1,0:T(8,128)(2,1)}), bf16[64,8,1792]{2,1,0:T(8,128)(2,1)}, u32[]{:S(2)}, u32[]{:S(2)}) async-start(bf16[64,8,1792]{2,1,0:T(8,128)(2,1)} %fusion), calls=%async_computation.1 | async-start | bytes 3670016 | tf_op jit(solution)/shard_map/all_to_all | solution.py:267
  88.2 42.2 %collective-permute-start.7 = (bf16[4,3,64,896]{3,2,1,0:T(8,128)(2,1)S(1)}, bf16[4,3,64,896]{3,2,1,0:T(8,128)(2,1)S(1)}, u32[]{:S(2)}, u32[]{:S(2)}) collective-permute-start(bf16[4,3,64,896]{3,2,1,0:T(8,128)(2,1)S(1)} %pad_maximum_fusion.2.refs_0_.refs_4_), channel_id=1, source_target_pairs={{0,48},{16,0},{32,16},{48,32},{1,49},{17,1},{33,17},{49,33},{2,50}... | collective-permute-start | bytes 4128776 | tf_op jit(solution)/shard_map/ppermute | solution.py:27
  93.0 43.1 %collective-permute-start.6 = (bf16[4,3,64,896]{3,2,1,0:T(8,128)(2,1)S(1)}, bf16[4,3,64,896]{3,2,1,0:T(8,128)(2,1)}, u32[]{:S(2)}, u32[]{:S(2)}) collective-permute-start(bf16[4,3,64,896]{3,2,1,0:T(8,128)(2,1)S(1)} %pad_maximum_fusion.2.refs_0_.refs_4_), channel_id=1, source_target_pairs={{0,16},{16,32},{32,48},{48,0},{1,17},{17,33},{33,49},{49,1},{2,18}... | collective-permute-start | bytes 4128776 | tf_op jit(solution)/shard_map/ppermute | solution.py:27
  95.0 69.9 %collective-permute-start.10 = (bf16[4,3,64,896]{3,2,1,0:T(8,128)(2,1)S(1)}, bf16[4,3,64,896]{3,2,1,0:T(8,128)(2,1)}, u32[]{:S(2)}, u32[]{:S(2)}) collective-permute-start(bf16[4,3,64,896]{3,2,1,0:T(8,128)(2,1)S(1)} %pad_maximum_fusion.2.refs_0_.refs_4_), channel_id=1, source_target_pairs={{0,64},{64,0},{1,65},{65,1},{2,66},{66,2},{3,67},{67,3},{4,68},{68... | collective-permute-start | bytes 4128776 | tf_op jit(solution)/shard_map/ppermute | solution.py:27
  130.5 23.2 %collective-permute-start.9 = (bf16[2,3,64,896]{3,2,1,0:T(8,128)(2,1)S(1)}, bf16[2,3,64,896]{3,2,1,0:T(8,128)(2,1)S(1)}, u32[]{:S(2)}, u32[]{:S(2)}) collective-permute-start(bf16[2,3,64,896]{3,2,1,0:T(8,128)(2,1)S(1)} %slice.57), channel_id=1, source_target_pairs={{0,48},{16,0},{32,16},{48,32},{1,49},{17,1},{33,17},{49,33},{2,50}... | collective-permute-start | bytes 2064392 | tf_op jit(solution)/shard_map/ppermute | solution.py:27
  137.3 24.6 %collective-permute-start.8 = (bf16[2,3,64,896]{3,2,1,0:T(8,128)(2,1)S(1)}, bf16[2,3,64,896]{3,2,1,0:T(8,128)(2,1)}, u32[]{:S(2)}, u32[]{:S(2)}) collective-permute-start(bf16[2,3,64,896]{3,2,1,0:T(8,128)(2,1)S(1)} %slice.56), channel_id=1, source_target_pairs={{0,16},{16,32},{32,48},{48,0},{1,17},{17,33},{33,49},{49,1},{2,18}... | collective-permute-start | bytes 2064392 | tf_op jit(solution)/shard_map/ppermute | solution.py:27
  139.2 27.0 %collective-permute-start.12 = (bf16[4,3,64,896]{3,2,1,0:T(8,128)(2,1)S(1)}, bf16[4,3,64,896]{3,2,1,0:T(8,128)(2,1)}, u32[]{:S(2)}, u32[]{:S(2)}) collective-permute-start(bf16[4,3,64,896]{3,2,1,0:T(8,128)(2,1)S(1)} %collective-permute-done.7.refs_2_.refs_6_), channel_id=1, source_target_pairs={{0,64},{64,0},{1,65},{65,1},{2,66},{66,2},{3,67},{67,3},{4,68},{68... | collective-permute-start | bytes 4128776 | tf_op jit(solution)/shard_map/ppermute | solution.py:27
  141.1 25.1 %collective-permute-start.11 = (bf16[4,3,64,896]{3,2,1,0:T(8,128)(2,1)}, bf16[4,3,64,896]{3,2,1,0:T(8,128)(2,1)}, u32[]{:S(2)}, u32[]{:S(2)}) collective-permute-start(bf16[4,3,64,896]{3,2,1,0:T(8,128)(2,1)} %collective-permute-done.6.refs_1_.refs_5_), channel_id=1, source_target_pairs={{0,64},{64,0},{1,65},{65,1},{2,66},{66,2},{3,67},{67,3},{4,68},{68... | collective-permute-start | bytes 4128776 | tf_op jit(solution)/shard_map/ppermute | solution.py:27
  153.7 11.1 %collective-permute-start.14 = (bf16[2,3,64,896]{3,2,1,0:T(8,128)(2,1)S(1)}, bf16[2,3,64,896]{3,2,1,0:T(8,128)(2,1)}, u32[]{:S(2)}, u32[]{:S(2)}) collective-permute-start(bf16[2,3,64,896]{3,2,1,0:T(8,128)(2,1)S(1)} %collective-permute-done.9.refs_4_.refs_8_), channel_id=1, source_target_pairs={{0,64},{64,0},{1,65},{65,1},{2,66},{66,2},{3,67},{67,3},{4,68},{68... | collective-permute-start | bytes 2064392 | tf_op jit(solution)/shard_map/ppermute | solution.py:27
  161.9 4.4 %collective-permute-start.13 = (bf16[2,3,64,896]{3,2,1,0:T(8,128)(2,1)}, bf16[2,3,64,896]{3,2,1,0:T(8,128)(2,1)}, u32[]{:S(2)}, u32[]{:S(2)}) collective-permute-start(bf16[2,3,64,896]{3,2,1,0:T(8,128)(2,1)} %collective-permute-done.8.refs_3_.refs_7_), channel_id=1, source_target_pairs={{0,64},{64,0},{1,65},{65,1},{2,66},{66,2},{3,67},{67,3},{4,68},{68... | collective-permute-start | bytes 2064392 | tf_op jit(solution)/shard_map/ppermute | solution.py:27
  174.9 1.0 copy-start.1
  207.9 10.1 %collective-permute-start.17 = (bf16[64,2048]{1,0:T(8,128)(2,1)S(1)}, bf16[64,2048]{1,0:T(8,128)(2,1)S(1)}, u32[]{:S(2)}, u32[]{:S(2)}) collective-permute-start(bf16[64,2048]{1,0:T(8,128)(2,1)S(1)} %pad_maximum_fusion.3.refs_0_), channel_id=1, source_target_pairs={{0,384},{128,0},{256,128},{384,256},{1,385},{129,1},{257,129},{385... | collective-permute-start | bytes 786440 | tf_op jit(solution)/shard_map/ppermute | solution.py:27
  211.0 11.7 %collective-permute-start.16 = (bf16[64,2048]{1,0:T(8,128)(2,1)S(1)}, bf16[64,2048]{1,0:T(8,128)(2,1)S(1)}, u32[]{:S(2)}, u32[]{:S(2)}) collective-permute-start(bf16[64,2048]{1,0:T(8,128)(2,1)S(1)} %pad_maximum_fusion.3.refs_0_), channel_id=1, source_target_pairs={{0,256},{128,384},{256,0},{384,128},{1,257},{129,385},{257,1},{385... | collective-permute-start | bytes 786440 | tf_op jit(solution)/shard_map/ppermute | solution.py:27
  214.4 10.8 %collective-permute-start.15 = (bf16[64,2048]{1,0:T(8,128)(2,1)S(1)}, bf16[64,2048]{1,0:T(8,128)(2,1)S(1)}, u32[]{:S(2)}, u32[]{:S(2)}) collective-permute-start(bf16[64,2048]{1,0:T(8,128)(2,1)S(1)} %pad_maximum_fusion.3.refs_0_), channel_id=1, source_target_pairs={{0,128},{128,256},{256,384},{384,0},{1,129},{129,257},{257,385},{3... | collective-permute-start | bytes 786440 | tf_op jit(solution)/shard_map/ppermute | solution.py:27
  231.1 0.9 copy-start
  232.1 65.1 %all-to-all-start.3 = ((bf16[256,2,896]{2,1,0:T(2,128)(2,1)}), bf16[256,2,896]{2,1,0:T(2,128)(2,1)S(1)}, u32[]{:S(2)}, u32[]{:S(2)}) async-start(bf16[256,2,896]{2,1,0:T(2,128)(2,1)} %copy-done), calls=%async_computation.3 | async-start | bytes 1835008 | tf_op jit(solution)/shard_map/all_to_all | solution.py:278

commit v6 on v5

--- a/solution.py
+++ b/solution.py
@@ -72,28 +72,19 @@
             out_ref[:, :, at : at + span] = part.astype(bf16).reshape(n_y, rows, span)
 
 
-def backward_kernel(place, *refs):
-    acts, pieces = refs[:QUARTERS], refs[QUARTERS:-5]
-    out_ref, held, acts_held, sems, act_sems = refs[-5:]
+def backward_kernel(place, acts_ref, *refs):
+    pieces, (out_ref, held, sems) = refs[:-3], refs[-3:]
     copies = weight_copies(place[1], pieces, held, sems, 2)
-    act_copies = [
-        pltpu.make_async_copy(act, acts_held.at[(place[0] - k + QUARTERS) % QUARTERS], act_sems.at[k])
-        for k, act in enumerate(acts)
-    ]
-    for copy in act_copies:
-        copy.start()
     for group in copies:
         for copy in group:
             copy.start()
-    for copy in act_copies:
-        copy.wait()
+    n_y, rows, width = acts_ref.shape
+    _, _, groups, units, cols = held.shape
+    hidden = groups * units
+    both = acts_ref[...].reshape(n_y * rows, width)
     for group in copies:
         for copy in group:
             copy.wait()
-    n_y, rows, width = acts_held.shape
-    _, _, groups, units, cols = held.shape
-    hidden = groups * units
-    both = acts_held[...].reshape(n_y * rows, width)
     for half in range(2):
         part = mm(both[:, :hidden], held[half, 0].reshape(hidden, cols))
         part = part + mm(both[:, hidden:], held[half, 1].reshape(hidden, cols))
@@ -136,27 +127,22 @@
 
 
 def backward_parts(place, acts, pieces):
-    rows, double = acts[0].shape
+    n_y, rows, double = acts.shape
     held = held_shape(pieces, 2)
-    total, cols = QUARTERS * rows, held[4]
+    total, cols = n_y * rows, held[4]
     return pl.pallas_call(
         backward_kernel,
         out_shape=jax.ShapeDtypeStruct((total, 2, cols), bf16),
-        in_specs=[SMEM] + [ANY] * (QUARTERS + len(pieces)),
+        in_specs=[SMEM, VMEM] + [ANY] * len(pieces),
         out_specs=VMEM,
-        scratch_shapes=[
-            pltpu.VMEM(held, bf16),
-            pltpu.VMEM((QUARTERS, rows, double), bf16),
-            pltpu.SemaphoreType.DMA((2, len(pieces))),
-            pltpu.SemaphoreType.DMA((QUARTERS,)),
-        ],
+        scratch_shapes=[pltpu.VMEM(held, bf16), pltpu.SemaphoreType.DMA((2, len(pieces)))],
         compiler_params=PARAMS,
         cost_estimate=pl.CostEstimate(
             flops=4 * total * double * cols,
             bytes_accessed=4 * double * cols,
             transcendentals=0,
         ),
-    )(place, *acts, *pieces)
+    )(place, acts, *pieces)
 
 
 def combine_kernel(high_ref, low_ref, home_ref, out_ref):
@@ -273,7 +259,8 @@
         swiglu_grads(summed[:, :hidden], summed[:, hidden : 2 * hidden], summed[:, 2 * hidden :]),
         axis=1,
     )
-    acts = [acts] + [shift(acts, "y", k) for k in range(1, n_y)]
+    acts = jnp.broadcast_to(acts[None], (n_y,) + acts.shape)
+    acts = lax.all_to_all(acts, "y", split_axis=0, concat_axis=0, tiled=True)
     part = backward_parts(place, acts, pieces)
     home = lax.all_to_all(
         part, ("y",) + EX, split_axis=0, concat_axis=0, tiled=True

time: 300 us -> 296 us (0.987)
  blocking collectives: 23.8 us -> 38.9 us
  waiting for transfers between devices: 154 us -> 143 us
  starting transfers between devices: 87.9 us -> 79.3 us
    all_to_all x0 -> x1, blocking collectives: none -> 15.2 us  [per_device(): acts = lax.all_to_all(acts, 'y', split_axis=0, concat_axis=0, tiled=True)]
    ppermute x18 -> x15, waiting for transfers between devices: 93.7 us -> 84.8 us  [shift(): return lax.ppermute(array, axis, [(i, (i + k) % n) for i in range(n)])]
    ppermute x18 -> x15, starting transfers between devices: 54.9 us -> 46.5 us  [shift(): return lax.ppermute(array, axis, [(i, (i + k) % n) for i in range(n)])]
  transfers between devices with their start and end apart: 21 -> 18, of which waited for: 14 -> 11; matrix products, arithmetic and copies ran while one was open for 3% -> 3% of each run, Pallas kernels for 0% -> 0%
where the time goes in v6:
time: 296 us; the launch traced here: 295 us
  waiting for transfers between devices  143 us (48%)
  starting transfers between devices  79.3 us (27%)
  blocking collectives  38.9 us (13%)
  Pallas kernels  15.1 us (5%)
  local copies, waits for them, and re-layouts  8.77 us (3%)
  other arithmetic  5.06 us (2%)
  matrix products  4.36 us (1%)
    ppermute x15, waiting for transfers between devices, shift(): return lax.ppermute(array, axis, [(i, (i + k) % n) for i in range(n)])  84.8 us
    all_to_all x1, waiting for transfers between devices, per_device(): lax.all_to_all(part, ('y',) + EX, split_axis=0, concat_axis=0, tiled=True)  49.7 us
    ppermute x15, starting transfers between devices, shift(): return lax.ppermute(array, axis, [(i, (i + k) % n) for i in range(n)])  46.5 us
    all_to_all x1, blocking collectives, per_device(): parts = lax.all_to_all(parts, 'y', split_axis=0, concat_axis=0, tiled=True)  23.8 us
    all_to_all x1, blocking collectives, per_device(): acts = lax.all_to_all(acts, 'y', split_axis=0, concat_axis=0, tiled=True)  15.2 us
    all_to_all x1, starting transfers between devices, per_device(): there = lax.all_to_all(mine, EX, split_axis=0, concat_axis=0, tiled=True)  14.9 us
    all_to_all x1, starting transfers between devices, per_device(): lax.all_to_all(part, ('y',) + EX, split_axis=0, concat_axis=0, tiled=True)  13.4 us
    all_to_all x1, waiting for transfers between devices, per_device(): there = lax.all_to_all(mine, EX, split_axis=0, concat_axis=0, tiled=True)  8.68 us
  transfers between devices with their start and end apart: 18, of which 11 were waited for; matrix products, arithmetic and copies ran while one was open for 3% of the time, Pallas kernels for 0%

profile of v6, /device:TPU:32, one launch (start us, length us, event | category | flops | bytes accessed | tf_op | source)
XLA Modules:
  0.0 295.3 jit_solution(15116584825409988103)
XLA Ops:
  3.8 4.8 %collective-permute-start.2 = (bf16[3,64,896]{2,1,0:T(8,128)(2,1)}, bf16[3,64,896]{2,1,0:T(8,128)(2,1)}, u32[]{:S(2)}, u32[]{:S(2)}) collective-permute-start(bf16[3,64,896]{2,1,0:T(8,128)(2,1)} %get-tuple-element.27), channel_id=1, source_target_pairs={{0,48},{16,0},{32,16},{48,32},{1,49},{17,1},{33,17},{49,33},{2,50}... | collective-permute-start | bytes 1032200 | tf_op jit(solution)/shard_map/ppermute | solution.py:27
  8.6 2.7 collective-permute-start.1
  11.3 2.8 collective-permute-start
  19.2 4.4 %collective-permute-done.2 = bf16[3,64,896]{2,1,0:T(8,128)(2,1)} collective-permute-done((bf16[3,64,896]{2,1,0:T(8,128)(2,1)}, bf16[3,64,896]{2,1,0:T(8,128)(2,1)}, u32[]{:S(2)}, u32[]{:S(2)}) %collective-permute-start.2) | collective-permute-done | bytes 344096 | tf_op jit(solution)/shard_map/ppermute | solution.py:27
  23.6 5.6 %collective-permute-done = bf16[3,64,896]{2,1,0:T(8,128)(2,1)} collective-permute-done((bf16[3,64,896]{2,1,0:T(8,128)(2,1)S(1)}, bf16[3,64,896]{2,1,0:T(8,128)(2,1)}, u32[]{:S(2)}, u32[]{:S(2)}) %collective-permute-start) | collective-permute-done | bytes 344096 | tf_op jit(solution)/shard_map/ppermute | solution.py:27
  29.2 4.5 %all-to-all-start = ((bf16[4,128,1792]{2,1,0:T(8,128)(2,1)}), bf16[4,128,1792]{2,1,0:T(8,128)(2,1)S(1)}, u32[]{:S(2)}, u32[]{:S(2)}) async-start(bf16[4,128,1792]{2,1,0:T(8,128)(2,1)} %maximum_maximum_fusion), calls=%async_computation | async-start | bytes 3670016 | tf_op jit(solution)/shard_map/all_to_all | solution.py:238
  35.2 2.0 collective-permute-start.5
  37.2 5.2 %collective-permute-start.4 = (bf16[3,64,896]{2,1,0:T(8,128)(2,1)S(1)}, bf16[3,64,896]{2,1,0:T(8,128)(2,1)S(1)}, u32[]{:S(2)}, u32[]{:S(2)}) collective-permute-start(bf16[3,64,896]{2,1,0:T(8,128)(2,1)S(1)} %get-tuple-element.25), channel_id=1, source_target_pairs={{0,2},{1,3},{2,0},{3,1},{4,6},{5,7},{6,4},{7,5},{8,10},{9,11},{10,... | collective-permute-start | bytes 1032200 | tf_op jit(solution)/shard_map/ppermute | solution.py:27
  42.4 4.7 %collective-permute-start.3 = (bf16[3,64,896]{2,1,0:T(8,128)(2,1)S(1)}, bf16[3,64,896]{2,1,0:T(8,128)(2,1)S(1)}, u32[]{:S(2)}, u32[]{:S(2)}) collective-permute-start(bf16[3,64,896]{2,1,0:T(8,128)(2,1)S(1)} %get-tuple-element.26), channel_id=1, source_target_pairs={{0,1},{1,2},{2,3},{3,0},{4,5},{5,6},{6,7},{7,4},{8,9},{9,10},{10,1... | collective-permute-start | bytes 1032200 | tf_op jit(solution)/shard_map/ppermute | solution.py:27
  48.8 14.6 %collective-permute-done.4 = bf16[3,64,896]{2,1,0:T(8,128)(2,1)S(1)} collective-permute-done((bf16[3,64,896]{2,1,0:T(8,128)(2,1)S(1)}, bf16[3,64,896]{2,1,0:T(8,128)(2,1)S(1)}, u32[]{:S(2)}, u32[]{:S(2)}) %collective-permute-start.4) | collective-permute-done | bytes 344096 | tf_op jit(solution)/shard_map/ppermute | solution.py:27
  63.4 7.3 %collective-permute-done.3 = bf16[3,64,896]{2,1,0:T(8,128)(2,1)S(1)} collective-permute-done((bf16[3,64,896]{2,1,0:T(8,128)(2,1)S(1)}, bf16[3,64,896]{2,1,0:T(8,128)(2,1)S(1)}, u32[]{:S(2)}, u32[]{:S(2)}) %collective-permute-start.3) | collective-permute-done | bytes 344096 | tf_op jit(solution)/shard_map/ppermute | solution.py:27
  70.9 2.4 fusion
  73.3 14.9 %all-to-all-start.1 = ((bf16[64,8,1792]{2,1,0:T(8,128)(2,1)}), bf16[64,8,1792]{2,1,0:T(8,128)(2,1)}, u32[]{:S(2)}, u32[]{:S(2)}) async-start(bf16[64,8,1792]{2,1,0:T(8,128)(2,1)} %fusion), calls=%async_computation.1 | async-start | bytes 3670016 | tf_op jit(solution)/shard_map/all_to_all | solution.py:253
  88.2 4.8 %collective-permute-start.7 = (bf16[4,3,64,896]{3,2,1,0:T(8,128)(2,1)S(1)}, bf16[4,3,64,896]{3,2,1,0:T(8,128)(2,1)S(1)}, u32[]{:S(2)}, u32[]{:S(2)}) collective-permute-start(bf16[4,3,64,896]{3,2,1,0:T(8,128)(2,1)S(1)} %pad_maximum_fusion.2.refs_0_), channel_id=1, source_target_pairs={{0,48},{16,0},{32,16},{48,32},{1,49},{17,1},{33,17},{49,33},{2,50}... | collective-permute-start | bytes 4128776 | tf_op jit(solution)/shard_map/ppermute | solution.py:27
  93.0 1.9 collective-permute-start.6
  94.9 1.9 collective-permute-start.10
  96.9 33.6 %collective-permute-done.7.refs_2_ = bf16[4,3,64,896]{3,2,1,0:T(8,128)(2,1)S(1)} collective-permute-done((bf16[4,3,64,896]{3,2,1,0:T(8,128)(2,1)S(1)}, bf16[4,3,64,896]{3,2,1,0:T(8,128)(2,1)S(1)}, u32[]{:S(2)}, u32[]{:S(2)}) %collective-permute-start.7) | collective-permute-done | bytes 1376288 | tf_op jit(solution)/shard_map/ppermute | solution.py:27
  130.5 5.6 %collective-permute-start.9 = (bf16[2,3,64,896]{3,2,1,0:T(8,128)(2,1)S(1)}, bf16[2,3,64,896]{3,2,1,0:T(8,128)(2,1)S(1)}, u32[]{:S(2)}, u32[]{:S(2)}) collective-permute-start(bf16[2,3,64,896]{3,2,1,0:T(8,128)(2,1)S(1)} %slice.57), channel_id=1, source_target_pairs={{0,48},{16,0},{32,16},{48,32},{1,49},{17,1},{33,17},{49,33},{2,50}... | collective-permute-start | bytes 2064392 | tf_op jit(solution)/shard_map/ppermute | solution.py:27
  137.3 1.9 collective-permute-start.8
  139.2 1.9 collective-permute-start.12
  141.1 2.4 collective-permute-start.11
  143.5 10.1 %collective-permute-done.9.refs_4_ = bf16[2,3,64,896]{3,2,1,0:T(8,128)(2,1)S(1)} collective-permute-done((bf16[2,3,64,896]{3,2,1,0:T(8,128)(2,1)S(1)}, bf16[2,3,64,896]{3,2,1,0:T(8,128)(2,1)S(1)}, u32[]{:S(2)}, u32[]{:S(2)}) %collective-permute-start.9) | collective-permute-done | bytes 688160 | tf_op jit(solution)/shard_map/ppermute | solution.py:27
  153.7 1.9 collective-permute-start.14
  155.6 6.2 %collective-permute-done.8.refs_3_ = bf16[2,3,64,896]{3,2,1,0:T(8,128)(2,1)} collective-permute-done((bf16[2,3,64,896]{3,2,1,0:T(8,128)(2,1)S(1)}, bf16[2,3,64,896]{3,2,1,0:T(8,128)(2,1)}, u32[]{:S(2)}, u32[]{:S(2)}) %collective-permute-start.8) | collective-permute-done | bytes 688160 | tf_op jit(solution)/shard_map/ppermute | solution.py:27
  161.8 1.9 collective-permute-start.13
  166.2 8.7 %all-to-all-done.1 = bf16[64,8,1792]{2,1,0:T(8,128)(2,1)} async-done(((bf16[64,8,1792]{2,1,0:T(8,128)(2,1)}), bf16[64,8,1792]{2,1,0:T(8,128)(2,1)}, u32[]{:S(2)}, u32[]{:S(2)}) %all-to-all-start.1) | async-done | bytes 1835040 | tf_op jit(solution)/shard_map/all_to_all | solution.py:253
  175.9 7.7 %shard_map.82 = bf16[4,64,3072]{2,1,0:T(8,128)(2,1)S(1)} custom-call(s32[2]{0:T(128)S(1)} %pad_add_fusion.place, bf16[512,512]{1,0:T(8,128)(2,1)S(1)} %copy-done.1, bf16[512,1792]{1,0:T(8,128)(2,1)} %bitcast.41.there_ref, bf16[4,3,64,896]{3,2,1,0:T(8,128)(2,1)S(1)} %pad_maximum_fusion.2.refs_0_, bf16[4,3,64,896]{3,2,1,0:T(8,128)(2,1)} %collective-permute-done.6.refs_1_, ...), custom_call_target="tpu_custom_call" | custom-call | flops 3758096384 | bytes 11010048 | tf_op jit(solution)/shard_map/pallas_call | solution.py:110
  183.7 23.8 %all_to_all.25 = bf16[4,64,3072]{2,1,0:T(8,128)(2,1)S(1)} all-to-all(bf16[4,64,3072]{2,1,0:T(8,128)(2,1)S(1)} %shard_map.82), channel_id=1, replica_groups=mesh['y'=4,'c'=2,'x'=4,'h'=4,'l'=4] {'y'}, dimensions={0} | all-to-all | bytes 3145728 | tf_op jit(solution)/shard_map/all_to_all | solution.py:255
  208.0 15.2 %all_to_all.26.acts_ref = bf16[4,64,2048]{2,1,0:T(8,128)(2,1)S(1)} all-to-all(bf16[4,64,2048]{2,1,0:T(8,128)(2,1)S(1)} %broadcast_in_dim.5), channel_id=1, replica_groups=mesh['y'=4,'c'=2,'x'=4,'h'=4,'l'=4] {'y'}, dimensions={0} | all-to-all | bytes 2097152 | tf_op jit(solution)/shard_map/all_to_all | solution.py:263
  223.2 5.9 %shard_map.83 = bf16[256,2,896]{2,1,0:T(2,128)(2,1)S(1)} custom-call(s32[2]{0:T(128)S(1)} %pad_add_fusion.place, bf16[4,64,2048]{2,1,0:T(8,128)(2,1)S(1)} %all_to_all.26.acts_ref, bf16[4,3,64,896]{3,2,1,0:T(8,128)(2,1)S(1)} %pad_maximum_fusion.2.refs_0_, bf16[4,3,64,896]{3,2,1,0:T(8,128)(2,1)} %collective-permute-done.6.refs_1_, ...), custom_call_target="tpu_custom_call" | custom-call | flops 1879048192 | bytes 7340032 | tf_op jit(solution)/shard_map/pallas_call | solution.py:133
  230.0 13.4 %all-to-all-start.4 = ((bf16[256,2,896]{2,1,0:T(2,128)(2,1)}), bf16[256,2,896]{2,1,0:T(2,128)(2,1)S(1)}, u32[]{:S(2)}, u32[]{:S(2)}) async-start(bf16[256,2,896]{2,1,0:T(2,128)(2,1)} %copy-done), calls=%async_computation.4 | async-start | bytes 1835008 | tf_op jit(solution)/shard_map/all_to_all | solution.py:265
  243.5 49.7 %all-to-all-done.4 = bf16[256,2,896]{2,1,0:T(2,128)(2,1)S(1)} async-done(((bf16[256,2,896]{2,1,0:T(2,128)(2,1)}), bf16[256,2,896]{2,1,0:T(2,128)(2,1)S(1)}, u32[]{:S(2)}, u32[]{:S(2)}) %all-to-all-start.4) | async-done | bytes 917536 | tf_op jit(solution)/shard_map/all_to_all | solution.py:265
  (72 shorter events, 20.4 us)
Async XLA Ops:
  0.0 2.6 copy-start.4
  2.8 11.4 %copy-start.6 = (f32[64,8]{0,1:T(8,128)S(1)}, f32[64,8]{0,1:T(8,128)}, u32[]{:S(2)}) copy-start(f32[64,8]{0,1:T(8,128)} %param.12) | copy-start | bytes 6148
  2.8 11.4 %copy-start.7 = (s32[64,8]{0,1:T(8,128)S(1)}, s32[64,8]{0,1:T(8,128)}, u32[]{:S(2)}) copy-start(s32[64,8]{0,1:T(8,128)} %param.11) | copy-start | bytes 6148
  2.8 12.0 %copy-start.3 = (bf16[64,7168]{1,0:T(8,128)(2,1)S(1)}, bf16[64,7168]{1,0:T(8,128)(2,1)}, u32[]{:S(2)}) copy-start(bf16[64,7168]{1,0:T(8,128)(2,1)} %param.10) | copy-start | bytes 2752516
  3.8 12.0 %copy-start.5 = (f32[64,56]{0,1:T(8,128)S(1)}, f32[64,56]{0,1:T(8,128)}, u32[]{:S(2)}) copy-start(f32[64,56]{0,1:T(8,128)} %param.9) | copy-start | bytes 43012
  3.8 19.8 %collective-permute-start.2 = (bf16[3,64,896]{2,1,0:T(8,128)(2,1)}, bf16[3,64,896]{2,1,0:T(8,128)(2,1)}, u32[]{:S(2)}, u32[]{:S(2)}) collective-permute-start(bf16[3,64,896]{2,1,0:T(8,128)(2,1)} %get-tuple-element.27), channel_id=1, source_target_pairs={{0,48},{16,0},{32,16},{48,32},{1,49},{17,1},{33,17},{49,33},{2,50}... | collective-permute-start | bytes 1032200 | tf_op jit(solution)/shard_map/ppermute | solution.py:27
  8.6 15.0 %collective-permute-start.1 = (bf16[3,64,896]{2,1,0:T(8,128)(2,1)}, bf16[3,64,896]{2,1,0:T(8,128)(2,1)}, u32[]{:S(2)}, u32[]{:S(2)}) collective-permute-start(bf16[3,64,896]{2,1,0:T(8,128)(2,1)} %get-tuple-element.28), channel_id=1, source_target_pairs={{0,32},{16,48},{32,0},{48,16},{1,33},{17,49},{33,1},{49,17},{2,34}... | collective-permute-start | bytes 1032200 | tf_op jit(solution)/shard_map/ppermute | solution.py:27
  11.3 17.9 %collective-permute-start = (bf16[3,64,896]{2,1,0:T(8,128)(2,1)S(1)}, bf16[3,64,896]{2,1,0:T(8,128)(2,1)}, u32[]{:S(2)}, u32[]{:S(2)}) collective-permute-start(bf16[3,64,896]{2,1,0:T(8,128)(2,1)S(1)} %get-tuple-element.29), channel_id=1, source_target_pairs={{0,16},{16,32},{32,48},{48,0},{1,17},{17,33},{33,49},{49,1},{2,18}... | collective-permute-start | bytes 1032200 | tf_op jit(solution)/shard_map/ppermute | solution.py:27
  14.8 1.7 copy-start.2
  29.2 41.6 %all-to-all-start = ((bf16[4,128,1792]{2,1,0:T(8,128)(2,1)}), bf16[4,128,1792]{2,1,0:T(8,128)(2,1)S(1)}, u32[]{:S(2)}, u32[]{:S(2)}) async-start(bf16[4,128,1792]{2,1,0:T(8,128)(2,1)} %maximum_maximum_fusion), calls=%async_computation | async-start | bytes 3670016 | tf_op jit(solution)/shard_map/all_to_all | solution.py:238
  35.2 13.6 %collective-permute-start.5 = (bf16[3,64,896]{2,1,0:T(8,128)(2,1)S(1)}, bf16[3,64,896]{2,1,0:T(8,128)(2,1)S(1)}, u32[]{:S(2)}, u32[]{:S(2)}) collective-permute-start(bf16[3,64,896]{2,1,0:T(8,128)(2,1)S(1)} %get-tuple-element.24), channel_id=1, source_target_pairs={{0,3},{1,0},{2,1},{3,2},{4,7},{5,4},{6,5},{7,6},{8,11},{9,8},{10,9... | collective-permute-start | bytes 1032200 | tf_op jit(solution)/shard_map/ppermute | solution.py:27
  37.2 26.1 %collective-permute-start.4 = (bf16[3,64,896]{2,1,0:T(8,128)(2,1)S(1)}, bf16[3,64,896]{2,1,0:T(8,128)(2,1)S(1)}, u32[]{:S(2)}, u32[]{:S(2)}) collective-permute-start(bf16[3,64,896]{2,1,0:T(8,128)(2,1)S(1)} %get-tuple-element.25), channel_id=1, source_target_pairs={{0,2},{1,3},{2,0},{3,1},{4,6},{5,7},{6,4},{7,5},{8,10},{9,11},{10,... | collective-permute-start | bytes 1032200 | tf_op jit(solution)/shard_map/ppermute | solution.py:27
  42.4 28.2 %collective-permute-start.3 = (bf16[3,64,896]{2,1,0:T(8,128)(2,1)S(1)}, bf16[3,64,896]{2,1,0:T(8,128)(2,1)S(1)}, u32[]{:S(2)}, u32[]{:S(2)}) collective-permute-start(bf16[3,64,896]{2,1,0:T(8,128)(2,1)S(1)} %get-tuple-element.26), channel_id=1, source_target_pairs={{0,1},{1,2},{2,3},{3,0},{4,5},{5,6},{6,7},{7,4},{8,9},{9,10},{10,1... | collective-permute-start | bytes 1032200 | tf_op jit(solution)/shard_map/ppermute | solution.py:27
  73.3 101.6 %all-to-all-start.1 = ((bf16[64,8,1792]{2,1,0:T(8,128)(2,1)}), bf16[64,8,1792]{2,1,0:T(8,128)(2,1)}, u32[]{:S(2)}, u32[]{:S(2)}) async-start(bf16[64,8,1792]{2,1,0:T(8,128)(2,1)} %fusion), calls=%async_computation.1 | async-start | bytes 3670016 | tf_op jit(solution)/shard_map/all_to_all | solution.py:253
  88.2 42.2 %collective-permute-start.7 = (bf16[4,3,64,896]{3,2,1,0:T(8,128)(2,1)S(1)}, bf16[4,3,64,896]{3,2,1,0:T(8,128)(2,1)S(1)}, u32[]{:S(2)}, u32[]{:S(2)}) collective-permute-start(bf16[4,3,64,896]{3,2,1,0:T(8,128)(2,1)S(1)} %pad_maximum_fusion.2.refs_0_), channel_id=1, source_target_pairs={{0,48},{16,0},{32,16},{48,32},{1,49},{17,1},{33,17},{49,33},{2,50}... | collective-permute-start | bytes 4128776 | tf_op jit(solution)/shard_map/ppermute | solution.py:27
  93.0 43.1 %collective-permute-start.6 = (bf16[4,3,64,896]{3,2,1,0:T(8,128)(2,1)S(1)}, bf16[4,3,64,896]{3,2,1,0:T(8,128)(2,1)}, u32[]{:S(2)}, u32[]{:S(2)}) collective-permute-start(bf16[4,3,64,896]{3,2,1,0:T(8,128)(2,1)S(1)} %pad_maximum_fusion.2.refs_0_), channel_id=1, source_target_pairs={{0,16},{16,32},{32,48},{48,0},{1,17},{17,33},{33,49},{49,1},{2,18}... | collective-permute-start | bytes 4128776 | tf_op jit(solution)/shard_map/ppermute | solution.py:27
  94.9 69.9 %collective-permute-start.10 = (bf16[4,3,64,896]{3,2,1,0:T(8,128)(2,1)S(1)}, bf16[4,3,64,896]{3,2,1,0:T(8,128)(2,1)}, u32[]{:S(2)}, u32[]{:S(2)}) collective-permute-start(bf16[4,3,64,896]{3,2,1,0:T(8,128)(2,1)S(1)} %pad_maximum_fusion.2.refs_0_), channel_id=1, source_target_pairs={{0,64},{64,0},{1,65},{65,1},{2,66},{66,2},{3,67},{67,3},{4,68},{68... | collective-permute-start | bytes 4128776 | tf_op jit(solution)/shard_map/ppermute | solution.py:27
  130.5 23.2 %collective-permute-start.9 = (bf16[2,3,64,896]{3,2,1,0:T(8,128)(2,1)S(1)}, bf16[2,3,64,896]{3,2,1,0:T(8,128)(2,1)S(1)}, u32[]{:S(2)}, u32[]{:S(2)}) collective-permute-start(bf16[2,3,64,896]{3,2,1,0:T(8,128)(2,1)S(1)} %slice.57), channel_id=1, source_target_pairs={{0,48},{16,0},{32,16},{48,32},{1,49},{17,1},{33,17},{49,33},{2,50}... | collective-permute-start | bytes 2064392 | tf_op jit(solution)/shard_map/ppermute | solution.py:27
  137.3 24.6 %collective-permute-start.8 = (bf16[2,3,64,896]{3,2,1,0:T(8,128)(2,1)S(1)}, bf16[2,3,64,896]{3,2,1,0:T(8,128)(2,1)}, u32[]{:S(2)}, u32[]{:S(2)}) collective-permute-start(bf16[2,3,64,896]{3,2,1,0:T(8,128)(2,1)S(1)} %slice.56), channel_id=1, source_target_pairs={{0,16},{16,32},{32,48},{48,0},{1,17},{17,33},{33,49},{49,1},{2,18}... | collective-permute-start | bytes 2064392 | tf_op jit(solution)/shard_map/ppermute | solution.py:27
  139.2 27.0 %collective-permute-start.12 = (bf16[4,3,64,896]{3,2,1,0:T(8,128)(2,1)S(1)}, bf16[4,3,64,896]{3,2,1,0:T(8,128)(2,1)}, u32[]{:S(2)}, u32[]{:S(2)}) collective-permute-start(bf16[4,3,64,896]{3,2,1,0:T(8,128)(2,1)S(1)} %collective-permute-done.7.refs_2_), channel_id=1, source_target_pairs={{0,64},{64,0},{1,65},{65,1},{2,66},{66,2},{3,67},{67,3},{4,68},{68... | collective-permute-start | bytes 4128776 | tf_op jit(solution)/shard_map/ppermute | solution.py:27
  141.1 25.1 %collective-permute-start.11 = (bf16[4,3,64,896]{3,2,1,0:T(8,128)(2,1)}, bf16[4,3,64,896]{3,2,1,0:T(8,128)(2,1)}, u32[]{:S(2)}, u32[]{:S(2)}) collective-permute-start(bf16[4,3,64,896]{3,2,1,0:T(8,128)(2,1)} %collective-permute-done.6.refs_1_), channel_id=1, source_target_pairs={{0,64},{64,0},{1,65},{65,1},{2,66},{66,2},{3,67},{67,3},{4,68},{68... | collective-permute-start | bytes 4128776 | tf_op jit(solution)/shard_map/ppermute | solution.py:27
  153.7 11.1 %collective-permute-start.14 = (bf16[2,3,64,896]{3,2,1,0:T(8,128)(2,1)S(1)}, bf16[2,3,64,896]{3,2,1,0:T(8,128)(2,1)}, u32[]{:S(2)}, u32[]{:S(2)}) collective-permute-start(bf16[2,3,64,896]{3,2,1,0:T(8,128)(2,1)S(1)} %collective-permute-done.9.refs_4_), channel_id=1, source_target_pairs={{0,64},{64,0},{1,65},{65,1},{2,66},{66,2},{3,67},{67,3},{4,68},{68... | collective-permute-start | bytes 2064392 | tf_op jit(solution)/shard_map/ppermute | solution.py:27
  161.8 4.4 %collective-permute-start.13 = (bf16[2,3,64,896]{3,2,1,0:T(8,128)(2,1)}, bf16[2,3,64,896]{3,2,1,0:T(8,128)(2,1)}, u32[]{:S(2)}, u32[]{:S(2)}) collective-permute-start(bf16[2,3,64,896]{3,2,1,0:T(8,128)(2,1)} %collective-permute-done.8.refs_3_), channel_id=1, source_target_pairs={{0,64},{64,0},{1,65},{65,1},{2,66},{66,2},{3,67},{67,3},{4,68},{68... | collective-permute-start | bytes 2064392 | tf_op jit(solution)/shard_map/ppermute | solution.py:27
  174.9 1.0 copy-start.1
  229.0 0.9 copy-start
  230.0 63.2 %all-to-all-start.4 = ((bf16[256,2,896]{2,1,0:T(2,128)(2,1)}), bf16[256,2,896]{2,1,0:T(2,128)(2,1)S(1)}, u32[]{:S(2)}, u32[]{:S(2)}) async-start(bf16[256,2,896]{2,1,0:T(2,128)(2,1)} %copy-done), calls=%async_computation.4 | async-start | bytes 1835008 | tf_op jit(solution)/shard_map/all_to_all | solution.py:265

commit v7 on v6

--- a/solution.py
+++ b/solution.py
@@ -238,8 +238,6 @@
     got = lax.all_to_all(sent, "y", split_axis=0, concat_axis=0, tiled=True)
 
     along_l = weights_along_l(jnp.stack(along_x))
-    got, along_l = lax.optimization_barrier((got, along_l))
-    pieces = weights_spread(along_l)
     place = jnp.stack([lax.axis_index("y"), lax.axis_index("c")]).astype(jnp.int32)
 
     total = n_y * n_ex
@@ -250,6 +248,8 @@
     to_split = one_hot_rows(device * (2 * n_y) + kind * n_y + source)
 
     mine = mm(to_send, got.reshape(2 * total, cols)).astype(bf16).reshape(n_ex, 2 * n_y, cols)
+    mine, along_l = lax.optimization_barrier((mine, along_l))
+    pieces = weights_spread(along_l)
     there = lax.all_to_all(mine, EX, split_axis=0, concat_axis=0, tiled=True)
     parts = forward_parts(place, to_split, there.reshape(2 * total, cols), pieces, n_y)
     parts = lax.all_to_all(parts, "y", split_axis=0, concat_axis=0, tiled=True)

time: 296 us -> 296 us (level)
  no operation moved by 1% of the time
where the time goes in v7:
time: 296 us; the launch traced here: 295 us
  waiting for transfers between devices  143 us (48%)
  starting transfers between devices  79.3 us (27%)
  blocking collectives  38.9 us (13%)
  Pallas kernels  15.1 us (5%)
  local copies, waits for them, and re-layouts  8.77 us (3%)
  other arithmetic  5.06 us (2%)
  matrix products  4.36 us (1%)
    ppermute x15, waiting for transfers between devices, shift(): return lax.ppermute(array, axis, [(i, (i + k) % n) for i in range(n)])  84.8 us
    all_to_all x1, waiting for transfers between devices, per_device(): lax.all_to_all(part, ('y',) + EX, split_axis=0, concat_axis=0, tiled=True)  49.7 us
    ppermute x15, starting transfers between devices, shift(): return lax.ppermute(array, axis, [(i, (i + k) % n) for i in range(n)])  46.5 us
    all_to_all x1, blocking collectives, per_device(): parts = lax.all_to_all(parts, 'y', split_axis=0, concat_axis=0, tiled=True)  23.8 us
    all_to_all x1, blocking collectives, per_device(): acts = lax.all_to_all(acts, 'y', split_axis=0, concat_axis=0, tiled=True)  15.2 us
    all_to_all x1, starting transfers between devices, per_device(): there = lax.all_to_all(mine, EX, split_axis=0, concat_axis=0, tiled=True)  14.9 us
    all_to_all x1, starting transfers between devices, per_device(): lax.all_to_all(part, ('y',) + EX, split_axis=0, concat_axis=0, tiled=True)  13.4 us
    all_to_all x1, waiting for transfers between devices, per_device(): there = lax.all_to_all(mine, EX, split_axis=0, concat_axis=0, tiled=True)  8.68 us
  transfers between devices with their start and end apart: 18, of which 11 were waited for; matrix products, arithmetic and copies ran while one was open for 3% of the time, Pallas kernels for 0%

profile of v7, /device:TPU:32, one launch (start us, length us, event | category | flops | bytes accessed | tf_op | source)
XLA Modules:
  0.0 295.3 jit_solution(15116584825409988103)
XLA Ops:
  3.8 4.8 %collective-permute-start.2 = (bf16[3,64,896]{2,1,0:T(8,128)(2,1)}, bf16[3,64,896]{2,1,0:T(8,128)(2,1)}, u32[]{:S(2)}, u32[]{:S(2)}) collective-permute-start(bf16[3,64,896]{2,1,0:T(8,128)(2,1)} %get-tuple-element.27), channel_id=1, source_target_pairs={{0,48},{16,0},{32,16},{48,32},{1,49},{17,1},{33,17},{49,33},{2,50}... | collective-permute-start | bytes 1032200 | tf_op jit(solution)/shard_map/ppermute | solution.py:27
  8.6 2.7 collective-permute-start.1
  11.3 2.8 collective-permute-start
  19.2 4.4 %collective-permute-done.2 = bf16[3,64,896]{2,1,0:T(8,128)(2,1)} collective-permute-done((bf16[3,64,896]{2,1,0:T(8,128)(2,1)}, bf16[3,64,896]{2,1,0:T(8,128)(2,1)}, u32[]{:S(2)}, u32[]{:S(2)}) %collective-permute-start.2) | collective-permute-done | bytes 344096 | tf_op jit(solution)/shard_map/ppermute | solution.py:27
  23.6 5.6 %collective-permute-done = bf16[3,64,896]{2,1,0:T(8,128)(2,1)} collective-permute-done((bf16[3,64,896]{2,1,0:T(8,128)(2,1)S(1)}, bf16[3,64,896]{2,1,0:T(8,128)(2,1)}, u32[]{:S(2)}, u32[]{:S(2)}) %collective-permute-start) | collective-permute-done | bytes 344096 | tf_op jit(solution)/shard_map/ppermute | solution.py:27
  29.2 4.5 %all-to-all-start = ((bf16[4,128,1792]{2,1,0:T(8,128)(2,1)}), bf16[4,128,1792]{2,1,0:T(8,128)(2,1)S(1)}, u32[]{:S(2)}, u32[]{:S(2)}) async-start(bf16[4,128,1792]{2,1,0:T(8,128)(2,1)} %maximum_maximum_fusion), calls=%async_computation | async-start | bytes 3670016 | tf_op jit(solution)/shard_map/all_to_all | solution.py:238
  35.2 2.0 collective-permute-start.5
  37.2 5.2 %collective-permute-start.4 = (bf16[3,64,896]{2,1,0:T(8,128)(2,1)S(1)}, bf16[3,64,896]{2,1,0:T(8,128)(2,1)S(1)}, u32[]{:S(2)}, u32[]{:S(2)}) collective-permute-start(bf16[3,64,896]{2,1,0:T(8,128)(2,1)S(1)} %get-tuple-element.25), channel_id=1, source_target_pairs={{0,2},{1,3},{2,0},{3,1},{4,6},{5,7},{6,4},{7,5},{8,10},{9,11},{10,... | collective-permute-start | bytes 1032200 | tf_op jit(solution)/shard_map/ppermute | solution.py:27
  42.4 4.7 %collective-permute-start.3 = (bf16[3,64,896]{2,1,0:T(8,128)(2,1)S(1)}, bf16[3,64,896]{2,1,0:T(8,128)(2,1)S(1)}, u32[]{:S(2)}, u32[]{:S(2)}) collective-permute-start(bf16[3,64,896]{2,1,0:T(8,128)(2,1)S(1)} %get-tuple-element.26), channel_id=1, source_target_pairs={{0,1},{1,2},{2,3},{3,0},{4,5},{5,6},{6,7},{7,4},{8,9},{9,10},{10,1... | collective-permute-start | bytes 1032200 | tf_op jit(solution)/shard_map/ppermute | solution.py:27
  48.8 14.6 %collective-permute-done.4 = bf16[3,64,896]{2,1,0:T(8,128)(2,1)S(1)} collective-permute-done((bf16[3,64,896]{2,1,0:T(8,128)(2,1)S(1)}, bf16[3,64,896]{2,1,0:T(8,128)(2,1)S(1)}, u32[]{:S(2)}, u32[]{:S(2)}) %collective-permute-start.4) | collective-permute-done | bytes 344096 | tf_op jit(solution)/shard_map/ppermute | solution.py:27
  63.4 7.3 %collective-permute-done.3 = bf16[3,64,896]{2,1,0:T(8,128)(2,1)S(1)} collective-permute-done((bf16[3,64,896]{2,1,0:T(8,128)(2,1)S(1)}, bf16[3,64,896]{2,1,0:T(8,128)(2,1)S(1)}, u32[]{:S(2)}, u32[]{:S(2)}) %collective-permute-start.3) | collective-permute-done | bytes 344096 | tf_op jit(solution)/shard_map/ppermute | solution.py:27
  70.9 2.4 fusion
  73.3 14.9 %all-to-all-start.1 = ((bf16[64,8,1792]{2,1,0:T(8,128)(2,1)}), bf16[64,8,1792]{2,1,0:T(8,128)(2,1)}, u32[]{:S(2)}, u32[]{:S(2)}) async-start(bf16[64,8,1792]{2,1,0:T(8,128)(2,1)} %fusion), calls=%async_computation.1 | async-start | bytes 3670016 | tf_op jit(solution)/shard_map/all_to_all | solution.py:253
  88.2 4.8 %collective-permute-start.7 = (bf16[4,3,64,896]{3,2,1,0:T(8,128)(2,1)S(1)}, bf16[4,3,64,896]{3,2,1,0:T(8,128)(2,1)S(1)}, u32[]{:S(2)}, u32[]{:S(2)}) collective-permute-start(bf16[4,3,64,896]{3,2,1,0:T(8,128)(2,1)S(1)} %pad_maximum_fusion.2.refs_0_), channel_id=1, source_target_pairs={{0,48},{16,0},{32,16},{48,32},{1,49},{17,1},{33,17},{49,33},{2,50}... | collective-permute-start | bytes 4128776 | tf_op jit(solution)/shard_map/ppermute | solution.py:27
  93.0 1.9 collective-permute-start.6
  94.9 1.9 collective-permute-start.10
  96.9 33.6 %collective-permute-done.7.refs_2_ = bf16[4,3,64,896]{3,2,1,0:T(8,128)(2,1)S(1)} collective-permute-done((bf16[4,3,64,896]{3,2,1,0:T(8,128)(2,1)S(1)}, bf16[4,3,64,896]{3,2,1,0:T(8,128)(2,1)S(1)}, u32[]{:S(2)}, u32[]{:S(2)}) %collective-permute-start.7) | collective-permute-done | bytes 1376288 | tf_op jit(solution)/shard_map/ppermute | solution.py:27
  130.5 5.6 %collective-permute-start.9 = (bf16[2,3,64,896]{3,2,1,0:T(8,128)(2,1)S(1)}, bf16[2,3,64,896]{3,2,1,0:T(8,128)(2,1)S(1)}, u32[]{:S(2)}, u32[]{:S(2)}) collective-permute-start(bf16[2,3,64,896]{3,2,1,0:T(8,128)(2,1)S(1)} %slice.57), channel_id=1, source_target_pairs={{0,48},{16,0},{32,16},{48,32},{1,49},{17,1},{33,17},{49,33},{2,50}... | collective-permute-start | bytes 2064392 | tf_op jit(solution)/shard_map/ppermute | solution.py:27
  137.3 1.9 collective-permute-start.8
  139.2 1.9 collective-permute-start.12
  141.1 2.4 collective-permute-start.11
  143.5 10.1 %collective-permute-done.9.refs_4_ = bf16[2,3,64,896]{3,2,1,0:T(8,128)(2,1)S(1)} collective-permute-done((bf16[2,3,64,896]{3,2,1,0:T(8,128)(2,1)S(1)}, bf16[2,3,64,896]{3,2,1,0:T(8,128)(2,1)S(1)}, u32[]{:S(2)}, u32[]{:S(2)}) %collective-permute-start.9) | collective-permute-done | bytes 688160 | tf_op jit(solution)/shard_map/ppermute | solution.py:27
  153.7 1.9 collective-permute-start.14
  155.6 6.2 %collective-permute-done.8.refs_3_ = bf16[2,3,64,896]{3,2,1,0:T(8,128)(2,1)} collective-permute-done((bf16[2,3,64,896]{3,2,1,0:T(8,128)(2,1)S(1)}, bf16[2,3,64,896]{3,2,1,0:T(8,128)(2,1)}, u32[]{:S(2)}, u32[]{:S(2)}) %collective-permute-start.8) | collective-permute-done | bytes 688160 | tf_op jit(solution)/shard_map/ppermute | solution.py:27
  161.8 1.9 collective-permute-start.13
  166.2 8.7 %all-to-all-done.1 = bf16[64,8,1792]{2,1,0:T(8,128)(2,1)} async-done(((bf16[64,8,1792]{2,1,0:T(8,128)(2,1)}), bf16[64,8,1792]{2,1,0:T(8,128)(2,1)}, u32[]{:S(2)}, u32[]{:S(2)}) %all-to-all-start.1) | async-done | bytes 1835040 | tf_op jit(solution)/shard_map/all_to_all | solution.py:253
  175.9 7.7 %shard_map.82 = bf16[4,64,3072]{2,1,0:T(8,128)(2,1)S(1)} custom-call(s32[2]{0:T(128)S(1)} %pad_add_fusion.place, bf16[512,512]{1,0:T(8,128)(2,1)S(1)} %copy-done.1, bf16[512,1792]{1,0:T(8,128)(2,1)} %bitcast.41.there_ref, bf16[4,3,64,896]{3,2,1,0:T(8,128)(2,1)S(1)} %pad_maximum_fusion.2.refs_0_, bf16[4,3,64,896]{3,2,1,0:T(8,128)(2,1)} %collective-permute-done.6.refs_1_, ...), custom_call_target="tpu_custom_call" | custom-call | flops 3758096384 | bytes 11010048 | tf_op jit(solution)/shard_map/pallas_call | solution.py:110
  183.7 23.8 %all_to_all.25 = bf16[4,64,3072]{2,1,0:T(8,128)(2,1)S(1)} all-to-all(bf16[4,64,3072]{2,1,0:T(8,128)(2,1)S(1)} %shard_map.82), channel_id=1, replica_groups=mesh['y'=4,'c'=2,'x'=4,'h'=4,'l'=4] {'y'}, dimensions={0} | all-to-all | bytes 3145728 | tf_op jit(solution)/shard_map/all_to_all | solution.py:255
  208.0 15.2 %all_to_all.26.acts_ref = bf16[4,64,2048]{2,1,0:T(8,128)(2,1)S(1)} all-to-all(bf16[4,64,2048]{2,1,0:T(8,128)(2,1)S(1)} %broadcast_in_dim.5), channel_id=1, replica_groups=mesh['y'=4,'c'=2,'x'=4,'h'=4,'l'=4] {'y'}, dimensions={0} | all-to-all | bytes 2097152 | tf_op jit(solution)/shard_map/all_to_all | solution.py:263
  223.2 5.9 %shard_map.83 = bf16[256,2,896]{2,1,0:T(2,128)(2,1)S(1)} custom-call(s32[2]{0:T(128)S(1)} %pad_add_fusion.place, bf16[4,64,2048]{2,1,0:T(8,128)(2,1)S(1)} %all_to_all.26.acts_ref, bf16[4,3,64,896]{3,2,1,0:T(8,128)(2,1)S(1)} %pad_maximum_fusion.2.refs_0_, bf16[4,3,64,896]{3,2,1,0:T(8,128)(2,1)} %collective-permute-done.6.refs_1_, ...), custom_call_target="tpu_custom_call" | custom-call | flops 1879048192 | bytes 7340032 | tf_op jit(solution)/shard_map/pallas_call | solution.py:133
  230.0 13.4 %all-to-all-start.4 = ((bf16[256,2,896]{2,1,0:T(2,128)(2,1)}), bf16[256,2,896]{2,1,0:T(2,128)(2,1)S(1)}, u32[]{:S(2)}, u32[]{:S(2)}) async-start(bf16[256,2,896]{2,1,0:T(2,128)(2,1)} %copy-done), calls=%async_computation.4 | async-start | bytes 1835008 | tf_op jit(solution)/shard_map/all_to_all | solution.py:265
  243.5 49.7 %all-to-all-done.4 = bf16[256,2,896]{2,1,0:T(2,128)(2,1)S(1)} async-done(((bf16[256,2,896]{2,1,0:T(2,128)(2,1)}), bf16[256,2,896]{2,1,0:T(2,128)(2,1)S(1)}, u32[]{:S(2)}, u32[]{:S(2)}) %all-to-all-start.4) | async-done | bytes 917536 | tf_op jit(solution)/shard_map/all_to_all | solution.py:265
  (72 shorter events, 20.4 us)
Async XLA Ops:
  0.0 2.6 copy-start.4
  2.8 11.4 %copy-start.6 = (f32[64,8]{0,1:T(8,128)S(1)}, f32[64,8]{0,1:T(8,128)}, u32[]{:S(2)}) copy-start(f32[64,8]{0,1:T(8,128)} %param.12) | copy-start | bytes 6148
  2.8 11.4 %copy-start.7 = (s32[64,8]{0,1:T(8,128)S(1)}, s32[64,8]{0,1:T(8,128)}, u32[]{:S(2)}) copy-start(s32[64,8]{0,1:T(8,128)} %param.11) | copy-start | bytes 6148
  2.8 12.0 %copy-start.3 = (bf16[64,7168]{1,0:T(8,128)(2,1)S(1)}, bf16[64,7168]{1,0:T(8,128)(2,1)}, u32[]{:S(2)}) copy-start(bf16[64,7168]{1,0:T(8,128)(2,1)} %param.10) | copy-start | bytes 2752516
  3.8 12.0 %copy-start.5 = (f32[64,56]{0,1:T(8,128)S(1)}, f32[64,56]{0,1:T(8,128)}, u32[]{:S(2)}) copy-start(f32[64,56]{0,1:T(8,128)} %param.9) | copy-start | bytes 43012
  3.8 19.8 %collective-permute-start.2 = (bf16[3,64,896]{2,1,0:T(8,128)(2,1)}, bf16[3,64,896]{2,1,0:T(8,128)(2,1)}, u32[]{:S(2)}, u32[]{:S(2)}) collective-permute-start(bf16[3,64,896]{2,1,0:T(8,128)(2,1)} %get-tuple-element.27), channel_id=1, source_target_pairs={{0,48},{16,0},{32,16},{48,32},{1,49},{17,1},{33,17},{49,33},{2,50}... | collective-permute-start | bytes 1032200 | tf_op jit(solution)/shard_map/ppermute | solution.py:27
  8.6 15.0 %collective-permute-start.1 = (bf16[3,64,896]{2,1,0:T(8,128)(2,1)}, bf16[3,64,896]{2,1,0:T(8,128)(2,1)}, u32[]{:S(2)}, u32[]{:S(2)}) collective-permute-start(bf16[3,64,896]{2,1,0:T(8,128)(2,1)} %get-tuple-element.28), channel_id=1, source_target_pairs={{0,32},{16,48},{32,0},{48,16},{1,33},{17,49},{33,1},{49,17},{2,34}... | collective-permute-start | bytes 1032200 | tf_op jit(solution)/shard_map/ppermute | solution.py:27
  11.3 17.9 %collective-permute-start = (bf16[3,64,896]{2,1,0:T(8,128)(2,1)S(1)}, bf16[3,64,896]{2,1,0:T(8,128)(2,1)}, u32[]{:S(2)}, u32[]{:S(2)}) collective-permute-start(bf16[3,64,896]{2,1,0:T(8,128)(2,1)S(1)} %get-tuple-element.29), channel_id=1, source_target_pairs={{0,16},{16,32},{32,48},{48,0},{1,17},{17,33},{33,49},{49,1},{2,18}... | collective-permute-start | bytes 1032200 | tf_op jit(solution)/shard_map/ppermute | solution.py:27
  14.8 1.7 copy-start.2
  29.2 41.6 %all-to-all-start = ((bf16[4,128,1792]{2,1,0:T(8,128)(2,1)}), bf16[4,128,1792]{2,1,0:T(8,128)(2,1)S(1)}, u32[]{:S(2)}, u32[]{:S(2)}) async-start(bf16[4,128,1792]{2,1,0:T(8,128)(2,1)} %maximum_maximum_fusion), calls=%async_computation | async-start | bytes 3670016 | tf_op jit(solution)/shard_map/all_to_all | solution.py:238
  35.2 13.6 %collective-permute-start.5 = (bf16[3,64,896]{2,1,0:T(8,128)(2,1)S(1)}, bf16[3,64,896]{2,1,0:T(8,128)(2,1)S(1)}, u32[]{:S(2)}, u32[]{:S(2)}) collective-permute-start(bf16[3,64,896]{2,1,0:T(8,128)(2,1)S(1)} %get-tuple-element.24), channel_id=1, source_target_pairs={{0,3},{1,0},{2,1},{3,2},{4,7},{5,4},{6,5},{7,6},{8,11},{9,8},{10,9... | collective-permute-start | bytes 1032200 | tf_op jit(solution)/shard_map/ppermute | solution.py:27
  37.2 26.1 %collective-permute-start.4 = (bf16[3,64,896]{2,1,0:T(8,128)(2,1)S(1)}, bf16[3,64,896]{2,1,0:T(8,128)(2,1)S(1)}, u32[]{:S(2)}, u32[]{:S(2)}) collective-permute-start(bf16[3,64,896]{2,1,0:T(8,128)(2,1)S(1)} %get-tuple-element.25), channel_id=1, source_target_pairs={{0,2},{1,3},{2,0},{3,1},{4,6},{5,7},{6,4},{7,5},{8,10},{9,11},{10,... | collective-permute-start | bytes 1032200 | tf_op jit(solution)/shard_map/ppermute | solution.py:27
  42.4 28.2 %collective-permute-start.3 = (bf16[3,64,896]{2,1,0:T(8,128)(2,1)S(1)}, bf16[3,64,896]{2,1,0:T(8,128)(2,1)S(1)}, u32[]{:S(2)}, u32[]{:S(2)}) collective-permute-start(bf16[3,64,896]{2,1,0:T(8,128)(2,1)S(1)} %get-tuple-element.26), channel_id=1, source_target_pairs={{0,1},{1,2},{2,3},{3,0},{4,5},{5,6},{6,7},{7,4},{8,9},{9,10},{10,1... | collective-permute-start | bytes 1032200 | tf_op jit(solution)/shard_map/ppermute | solution.py:27
  73.3 101.6 %all-to-all-start.1 = ((bf16[64,8,1792]{2,1,0:T(8,128)(2,1)}), bf16[64,8,1792]{2,1,0:T(8,128)(2,1)}, u32[]{:S(2)}, u32[]{:S(2)}) async-start(bf16[64,8,1792]{2,1,0:T(8,128)(2,1)} %fusion), calls=%async_computation.1 | async-start | bytes 3670016 | tf_op jit(solution)/shard_map/all_to_all | solution.py:253
  88.2 42.2 %collective-permute-start.7 = (bf16[4,3,64,896]{3,2,1,0:T(8,128)(2,1)S(1)}, bf16[4,3,64,896]{3,2,1,0:T(8,128)(2,1)S(1)}, u32[]{:S(2)}, u32[]{:S(2)}) collective-permute-start(bf16[4,3,64,896]{3,2,1,0:T(8,128)(2,1)S(1)} %pad_maximum_fusion.2.refs_0_), channel_id=1, source_target_pairs={{0,48},{16,0},{32,16},{48,32},{1,49},{17,1},{33,17},{49,33},{2,50}... | collective-permute-start | bytes 4128776 | tf_op jit(solution)/shard_map/ppermute | solution.py:27
  93.0 43.1 %collective-permute-start.6 = (bf16[4,3,64,896]{3,2,1,0:T(8,128)(2,1)S(1)}, bf16[4,3,64,896]{3,2,1,0:T(8,128)(2,1)}, u32[]{:S(2)}, u32[]{:S(2)}) collective-permute-start(bf16[4,3,64,896]{3,2,1,0:T(8,128)(2,1)S(1)} %pad_maximum_fusion.2.refs_0_), channel_id=1, source_target_pairs={{0,16},{16,32},{32,48},{48,0},{1,17},{17,33},{33,49},{49,1},{2,18}... | collective-permute-start | bytes 4128776 | tf_op jit(solution)/shard_map/ppermute | solution.py:27
  94.9 69.9 %collective-permute-start.10 = (bf16[4,3,64,896]{3,2,1,0:T(8,128)(2,1)S(1)}, bf16[4,3,64,896]{3,2,1,0:T(8,128)(2,1)}, u32[]{:S(2)}, u32[]{:S(2)}) collective-permute-start(bf16[4,3,64,896]{3,2,1,0:T(8,128)(2,1)S(1)} %pad_maximum_fusion.2.refs_0_), channel_id=1, source_target_pairs={{0,64},{64,0},{1,65},{65,1},{2,66},{66,2},{3,67},{67,3},{4,68},{68... | collective-permute-start | bytes 4128776 | tf_op jit(solution)/shard_map/ppermute | solution.py:27
  130.5 23.2 %collective-permute-start.9 = (bf16[2,3,64,896]{3,2,1,0:T(8,128)(2,1)S(1)}, bf16[2,3,64,896]{3,2,1,0:T(8,128)(2,1)S(1)}, u32[]{:S(2)}, u32[]{:S(2)}) collective-permute-start(bf16[2,3,64,896]{3,2,1,0:T(8,128)(2,1)S(1)} %slice.57), channel_id=1, source_target_pairs={{0,48},{16,0},{32,16},{48,32},{1,49},{17,1},{33,17},{49,33},{2,50}... | collective-permute-start | bytes 2064392 | tf_op jit(solution)/shard_map/ppermute | solution.py:27
  137.3 24.6 %collective-permute-start.8 = (bf16[2,3,64,896]{3,2,1,0:T(8,128)(2,1)S(1)}, bf16[2,3,64,896]{3,2,1,0:T(8,128)(2,1)}, u32[]{:S(2)}, u32[]{:S(2)}) collective-permute-start(bf16[2,3,64,896]{3,2,1,0:T(8,128)(2,1)S(1)} %slice.56), channel_id=1, source_target_pairs={{0,16},{16,32},{32,48},{48,0},{1,17},{17,33},{33,49},{49,1},{2,18}... | collective-permute-start | bytes 2064392 | tf_op jit(solution)/shard_map/ppermute | solution.py:27
  139.2 27.0 %collective-permute-start.12 = (bf16[4,3,64,896]{3,2,1,0:T(8,128)(2,1)S(1)}, bf16[4,3,64,896]{3,2,1,0:T(8,128)(2,1)}, u32[]{:S(2)}, u32[]{:S(2)}) collective-permute-start(bf16[4,3,64,896]{3,2,1,0:T(8,128)(2,1)S(1)} %collective-permute-done.7.refs_2_), channel_id=1, source_target_pairs={{0,64},{64,0},{1,65},{65,1},{2,66},{66,2},{3,67},{67,3},{4,68},{68... | collective-permute-start | bytes 4128776 | tf_op jit(solution)/shard_map/ppermute | solution.py:27
  141.1 25.1 %collective-permute-start.11 = (bf16[4,3,64,896]{3,2,1,0:T(8,128)(2,1)}, bf16[4,3,64,896]{3,2,1,0:T(8,128)(2,1)}, u32[]{:S(2)}, u32[]{:S(2)}) collective-permute-start(bf16[4,3,64,896]{3,2,1,0:T(8,128)(2,1)} %collective-permute-done.6.refs_1_), channel_id=1, source_target_pairs={{0,64},{64,0},{1,65},{65,1},{2,66},{66,2},{3,67},{67,3},{4,68},{68... | collective-permute-start | bytes 4128776 | tf_op jit(solution)/shard_map/ppermute | solution.py:27
  153.7 11.1 %collective-permute-start.14 = (bf16[2,3,64,896]{3,2,1,0:T(8,128)(2,1)S(1)}, bf16[2,3,64,896]{3,2,1,0:T(8,128)(2,1)}, u32[]{:S(2)}, u32[]{:S(2)}) collective-permute-start(bf16[2,3,64,896]{3,2,1,0:T(8,128)(2,1)S(1)} %collective-permute-done.9.refs_4_), channel_id=1, source_target_pairs={{0,64},{64,0},{1,65},{65,1},{2,66},{66,2},{3,67},{67,3},{4,68},{68... | collective-permute-start | bytes 2064392 | tf_op jit(solution)/shard_map/ppermute | solution.py:27
  161.8 4.4 %collective-permute-start.13 = (bf16[2,3,64,896]{3,2,1,0:T(8,128)(2,1)}, bf16[2,3,64,896]{3,2,1,0:T(8,128)(2,1)}, u32[]{:S(2)}, u32[]{:S(2)}) collective-permute-start(bf16[2,3,64,896]{3,2,1,0:T(8,128)(2,1)} %collective-permute-done.8.refs_3_), channel_id=1, source_target_pairs={{0,64},{64,0},{1,65},{65,1},{2,66},{66,2},{3,67},{67,3},{4,68},{68... | collective-permute-start | bytes 2064392 | tf_op jit(solution)/shard_map/ppermute | solution.py:27
  174.9 1.0 copy-start.1
  229.0 0.9 copy-start
  230.0 63.2 %all-to-all-start.4 = ((bf16[256,2,896]{2,1,0:T(2,128)(2,1)}), bf16[256,2,896]{2,1,0:T(2,128)(2,1)S(1)}, u32[]{:S(2)}, u32[]{:S(2)}) async-start(bf16[256,2,896]{2,1,0:T(2,128)(2,1)} %copy-done), calls=%async_computation.4 | async-start | bytes 1835008 | tf_op jit(solution)/shard_map/all_to_all | solution.py:265
